TPU v7x, 256 devices: a whole 4x4x8 slice. The times are simulated.
256 devices in a mesh: blk: 2 (over x_lo), pb: 128 (over z, y, x_hi, core).
Axes of the slice: x: 4 (x_hi: 2, x_lo: 2; x = x_hi * 2 + x_lo), y: 4, z: 8, core: 2. Of those that a mesh axis runs over, the one named last changes fastest.
Arguments:
- hidden: bfloat16 [128, 128, 4096], P('pb', 'blk'), may hold values from -24 to 24
- query: bfloat16 [128, 128, 2048], P('pb', 'blk'), may hold values from -37 to 37
- out_grad: bfloat16 [128, 128, 2048], P('pb', 'blk'), may hold values from -6 to 6
- attn_out: bfloat16 [128, 128, 2048], P('pb', 'blk'), may hold values from -6 to 6
- keys: bfloat16 [128, 4, 256, 2048], P('pb', 'blk'), may hold values from -4 to 4
- values: bfloat16 [128, 4, 256, 2048], P('pb', 'blk'), may hold values from -6 to 6
- lengths: int32 [128, 4], P('pb', 'blk'), may hold values from 1 to 256, as said below
- w_query: bfloat16 [4096, 2048], P('pb', 'blk'), may hold values from -0.09375 to 0.09375
Outputs:
- hidden_grad: bfloat16 [128, 128, 4096], P('pb', 'blk')
- key_grad: bfloat16 [128, 4, 256, 2048], P('pb', 'blk')
- value_grad: bfloat16 [128, 4, 256, 2048], P('pb', 'blk')
- w_query_grad: float32 [4096, 2048], P('pb', 'blk')
Inputs may be any that keep to these rules, and one draw needn't show every extreme that they name: `lengths`: every passage has at least one valid token, and every question has a passage with all 256 tokens valid.
All inputs are finite; a program needn't handle non-finite values.
Results may differ from a plain program's by a relative error of at most 0.0056.
Values may be sent and summed in bfloat16 or wider, within the bound.
No kernel may reach another device: no remote copies, remote signals or barrier semaphores. Data moves between devices by JAX's collectives and lax.ppermute only.
A program may use at most 128 MiB of HBM per device.

v0:
```python
import jax
import jax.numpy as jnp
from jax import lax
from jax.sharding import PartitionSpec as P

HDIM = 64


SCORE_SCALE = 0.125
NEGATIVE = -1e30


def key_valid_of(passage_lengths, passage_len):
    tokens = jnp.arange(passage_len, dtype=jnp.int32)
    return (tokens[None, :] < passage_lengths[:, None]).reshape(-1)


def heads_split(matrix):
    return matrix.reshape(matrix.shape[0], -1, HDIM)


def score_block(query_rows, key_rows, key_valid):
    scores = (
        jnp.einsum("qhd,khd->hqk", query_rows, key_rows, preferred_element_type=jnp.float32)
        * SCORE_SCALE
    )
    return jnp.where(key_valid[None, None, :], scores, NEGATIVE)


def row_totals(scores):
    row_max = jnp.max(scores, axis=-1)
    row_total = jnp.sum(jnp.exp(scores - row_max[:, :, None]), axis=-1)
    return (row_max, row_total)


def grad_block(
    scores, log_total, query_rows, grad_rows, output_rows, key_rows, value_rows, key_valid
):
    probs = jnp.where(key_valid[None, None, :], jnp.exp(scores - log_total[:, :, None]), 0.0)
    probs_low = probs.astype(jnp.bfloat16)
    value_grad = jnp.einsum(
        "hqk,qhd->khd", probs_low, grad_rows, preferred_element_type=jnp.float32
    )
    prob_grad = jnp.einsum(
        "qhd,khd->hqk", grad_rows, value_rows, preferred_element_type=jnp.float32
    )
    row_delta = jnp.transpose(
        jnp.sum(grad_rows.astype(jnp.float32) * output_rows.astype(jnp.float32), axis=2)
    )
    score_grad = (probs * (prob_grad - row_delta[:, :, None]) * SCORE_SCALE).astype(jnp.bfloat16)
    key_grad = jnp.einsum(
        "hqk,qhd->khd", score_grad, query_rows, preferred_element_type=jnp.float32
    )
    query_grad = jnp.einsum(
        "hqk,khd->qhd", score_grad, key_rows, preferred_element_type=jnp.float32
    )
    return (query_grad, key_grad.astype(jnp.bfloat16), value_grad.astype(jnp.bfloat16))


def on_device(hidden, query, out_grad, attn_out, keys, values, lengths, w_query):
    passage_len = keys.shape[2]
    query_here, grad_here, output_here = (
        lax.all_to_all(query, "blk", split_axis=2, concat_axis=1, tiled=True),
        lax.all_to_all(out_grad, "blk", split_axis=2, concat_axis=1, tiled=True),
        lax.all_to_all(attn_out, "blk", split_axis=2, concat_axis=1, tiled=True),
    )
    keys_here, values_here = (
        lax.all_to_all(keys, "blk", split_axis=3, concat_axis=1, tiled=True),
        lax.all_to_all(values, "blk", split_axis=3, concat_axis=1, tiled=True),
    )
    every_length = lax.all_gather(lengths, "blk", axis=1, tiled=True)
    key_valid = key_valid_of(every_length[0], passage_len)
    query_rows = heads_split(query_here[0])
    grad_rows = heads_split(grad_here[0])
    output_rows = heads_split(output_here[0])
    key_rows = heads_split(keys_here[0].reshape(-1, keys_here.shape[3]))
    value_rows = heads_split(values_here[0].reshape(-1, values_here.shape[3]))
    scores = score_block(query_rows, key_rows, key_valid)
    row_max, row_total = row_totals(scores)
    log_total = row_max + jnp.log(row_total)
    query_grad, key_part, value_part = grad_block(
        scores, log_total, query_rows, grad_rows, output_rows, key_rows, value_rows, key_valid
    )
    query_slice = query_grad.reshape(query_grad.shape[0], -1).astype(jnp.bfloat16)
    key_grad, value_grad = (
        lax.all_to_all(
            key_part.reshape(keys_here.shape), "blk", split_axis=1, concat_axis=3, tiled=True
        ),
        lax.all_to_all(
            value_part.reshape(values_here.shape), "blk", split_axis=1, concat_axis=3, tiled=True
        ),
    )
    every_token = lax.all_gather(hidden, "blk", axis=1, tiled=True)[0]
    w_query_grad = lax.psum_scatter(
        lax.dot_general(
            every_token, query_slice, (((0,), (0,)), ((), ())), preferred_element_type=jnp.float32
        ),
        "pb",
        scatter_dimension=0,
        tiled=True,
    )
    full_weight = lax.all_gather(w_query, "pb", axis=0, tiled=True)
    state_grad = lax.psum_scatter(
        lax.dot_general(
            query_slice, full_weight, (((1,), (1,)), ((), ())), preferred_element_type=jnp.float32
        ),
        "blk",
        scatter_dimension=0,
        tiled=True,
    )
    hidden_grad = state_grad.astype(jnp.bfloat16).reshape(hidden.shape)
    return (hidden_grad, key_grad, value_grad, w_query_grad)


def solution(mesh):
    return jax.shard_map(
        on_device,
        mesh=mesh,
        in_specs=(
            P("pb", "blk", None),
            P("pb", "blk", None),
            P("pb", "blk", None),
            P("pb", "blk", None),
            P("pb", "blk", None, None),
            P("pb", "blk", None, None),
            P("pb", "blk"),
            P("pb", "blk"),
        ),
        out_specs=(
            P("pb", "blk", None),
            P("pb", "blk", None, None),
            P("pb", "blk", None, None),
            P("pb", "blk"),
        ),
        check_vma=False,
    )
```

profile of v0, /device:TPU:2, one launch (start us, length us, event | category | flops | bytes accessed | tf_op | source)
XLA Modules:
  0.0 931.3 jit_solution(10041088103595932287)
XLA Ops:
  7.9 2.2 copy.52
  10.6 11.5 %reduce = bf16[2048,64]{1,0:T(8,128)(2,1)S(1)} reduce(bf16[2048,1,64]{2,1,0:T(2,128)(2,1)S(1)} %bitcast.76, bf16[]{:T(256)} %broadcast.21), dimensions={1}, to_apply=%bitcast.49.reduce_sub_computation | reduce | bytes 524290
  23.3 5.7 all-to-all-start
  29.0 2.4 copy.58
  31.4 12.3 %reduce.2 = bf16[2048,64]{1,0:T(8,128)(2,1)} reduce(bf16[2048,1,64]{2,1,0:T(2,128)(2,1)S(1)} %bitcast.78, bf16[]{:T(256)} %broadcast.21), dimensions={1}, to_apply=%bitcast.53.reduce_sub_computation | reduce | bytes 524290
  43.7 2.2 reshape.70
  45.9 4.3 all-to-all-start.2
  50.1 2.2 copy.64
  52.4 12.3 %reduce.1 = bf16[2048,64]{1,0:T(8,128)(2,1)} reduce(bf16[2048,1,64]{2,1,0:T(2,128)(2,1)S(1)} %bitcast.77, bf16[]{:T(256)} %broadcast.21), dimensions={1}, to_apply=%bitcast.51.reduce_sub_computation | reduce | bytes 524290
  64.7 2.1 reshape.68
  66.9 3.5 all-to-all-start.4
  70.3 3.8 copy.55
  74.9 5.1 all-to-all-start.1
  80.0 6.2 copy.61
  86.1 14.4 %all-to-all-done.1 = bf16[1,2,256,2048]{2,1,0,3:T(2,128)(2,1)S(1)} async-done(((bf16[1,2,256,2048]{2,1,0,3:T(2,128)(2,1)}), bf16[1,2,256,2048]{2,1,0,3:T(2,128)(2,1)S(1)}, u32[]{:S(2)}, u32[]{:S(2)}) %all-to-all-start.1) | async-done | bytes 2097184 | tf_op jit(solution)/shard_map/all_to_all | solution.py:68
  100.6 6.6 all-to-all-start.3
  108.6 31.4 %all-reduce = s32[4]{0:T(128)S(1)} all-reduce(s32[4]{0:T(128)S(1)} %bitcast_dynamic-update-slice_fusion), channel_id=1, replica_groups=mesh['blk'=2,'pb'=128] {'blk'}, use_global_device_ids=true, to_apply=%add | all-reduce | flops 4 | bytes 32
  143.4 1.7 copy.59
  147.9 2.1 reshape.69
  150.0 2.9 bitcast_convert_fusion
  155.7 1.6 multiply_reduce_fusion
  157.4 2.8 copy.81
  160.1 3.3 reshape_reshape_squeeze.6
  163.4 4.5 copy.80
  167.9 4.4 reshape_reshape_squeeze.7
  173.8 2.0 exponential_reduce_fusion
  175.8 1.6 copy-done
  177.4 4.0 multiply_convert_fusion
  181.4 1.9 copy-done.1
  184.9 7.7 fusion.15
  192.6 9.3 convolution_bitcast_fusion
  201.9 17.5 %copy.74 = f32[4096,1024]{1,0:T(8,128)} copy(f32[4096,1024]{0,1:T(8,128)} %convolution_bitcast_fusion) | data formatting | bytes 33554432
  219.5 6.9 convert_bitcast_fusion
  226.4 3.3 reshape.54
  229.7 1.6 copy.71
  231.3 6.3 all-to-all-start.6
  237.7 2.9 convert_bitcast_fusion.1
  240.6 2.8 reshape.53
  243.3 3.2 copy.68
  246.5 18.4 %all-to-all-done.6 = bf16[1,4,256,1024]{2,3,0,1:T(8,128)(2,1)} async-done(((bf16[1,4,256,1024]{2,3,0,1:T(8,128)(2,1)}), bf16[1,4,256,1024]{2,3,0,1:T(8,128)(2,1)}, u32[]{:S(2)}, u32[]{:S(2)}) %all-to-all-start.6) | async-done | bytes 2097184 | tf_op jit(solution)/shard_map/all_to_all | solution.py:89
  264.9 5.5 all-to-all-start.5
  270.4 6.2 copy.72
  276.6 4.5 all_to_all.97
  281.1 19.5 %all-to-all-done.5 = bf16[1,4,256,1024]{2,3,0,1:T(8,128)(2,1)S(1)} async-done(((bf16[1,4,256,1024]{2,3,0,1:T(8,128)(2,1)}), bf16[1,4,256,1024]{2,3,0,1:T(8,128)(2,1)S(1)}, u32[]{:S(2)}, u32[]{:S(2)}) %all-to-all-start.5) | async-done | bytes 2097184 | tf_op jit(solution)/shard_map/all_to_all | solution.py:86
  300.6 4.0 copy.69
  304.6 4.5 all_to_all.93
  309.1 2.1 convert_bitcast_fusion.2
  311.2 613.2 %reduce-scatter.7.cloned.1.call-done = f32[32,1024]{1,0:T(8,128)} async-done(((f32[4096,1024]{1,0:T(8,128)}), f32[32,1024]{1,0:T(8,128)}) %reduce-scatter.7.cloned.1.call-update) | async-done | bytes 131088
  (52 shorter events, 15.8 us)
Async XLA Ops:
  7.2 177.7 %all-gather.3.cloned.1.call-start = ((), (), s32[]{:S(2)}) async-start(), calls=%async_computation.9 | async-start | bytes 8454144 | tf_op jit(solution)/shard_map/all_gather | solution.py:102
  23.3 22.6 %all-to-all-start = ((bf16[2,2,32768]{2,1,0:T(2,128)(2,1)}), bf16[2,2,32768]{2,1,0:T(2,128)(2,1)S(1)}, u32[]{:S(2)}, u32[]{:S(2)}) async-start(bf16[2,2,32768]{2,1,0:T(2,128)(2,1)} %reshape.66), calls=%async_computation | async-start | bytes 524288 | tf_op jit(solution)/shard_map/all_to_all | solution.py:63
  29.0 41.3 %copy-start.2 = (bf16[1,2,256,2048]{3,2,1,0:T(8,128)(2,1)S(1)}, bf16[1,2,256,2048]{3,2,1,0:T(8,128)(2,1)}, u32[]{:S(2)}) copy-start(bf16[1,2,256,2048]{3,2,1,0:T(8,128)(2,1)} %param.12) | copy-start | bytes 6291460
  45.9 21.0 %all-to-all-start.2 = ((bf16[2,2,32768]{2,1,0:T(2,128)(2,1)}), bf16[2,2,32768]{2,1,0:T(2,128)(2,1)}, u32[]{:S(2)}, u32[]{:S(2)}) async-start(bf16[2,2,32768]{2,1,0:T(2,128)(2,1)} %reshape.70), calls=%async_computation.2 | async-start | bytes 524288 | tf_op jit(solution)/shard_map/all_to_all | solution.py:64
  66.9 7.3 all-to-all-start.4
  74.2 0.7 copy-start.4
  74.9 25.7 %all-to-all-start.1 = ((bf16[1,2,256,2048]{2,1,0,3:T(2,128)(2,1)}), bf16[1,2,256,2048]{2,1,0,3:T(2,128)(2,1)S(1)}, u32[]{:S(2)}, u32[]{:S(2)}) async-start(bf16[1,2,256,2048]{2,1,0,3:T(2,128)(2,1)} %copy.55), calls=%async_computation.1 | async-start | bytes 4194304 | tf_op jit(solution)/shard_map/all_to_all | solution.py:68
  80.0 27.2 %copy-start.7 = (u32[256]{0:T(256)S(1)}, u32[256]{0:T(256)}, u32[]{:S(2)}) copy-start(u32[256]{0:T(256)} %constant.18) | copy-start | bytes 3076
  80.0 28.5 %copy-start.6 = (s32[1,2]{1,0:T(1,128)S(1)}, s32[1,2]{1,0:T(1,128)}, u32[]{:S(2)}) copy-start(s32[1,2]{1,0:T(1,128)} %param.14) | copy-start | bytes 28
  100.6 62.8 %all-to-all-start.3 = ((bf16[1,2,256,2048]{2,1,0,3:T(2,128)(2,1)}), bf16[1,2,256,2048]{2,1,0,3:T(2,128)(2,1)}, u32[]{:S(2)}, u32[]{:S(2)}) async-start(bf16[1,2,256,2048]{2,1,0,3:T(2,128)(2,1)} %copy.61), calls=%async_computation.3 | async-start | bytes 4194304 | tf_op jit(solution)/shard_map/all_to_all | solution.py:69
  107.2 85.4 %all-gather.5.cloned.1.call-start = ((), (), s32[]{:S(2)}) async-start(), calls=%async_computation.11 | async-start | bytes 1572864 | tf_op jit(solution)/shard_map/all_gather | solution.py:93
  108.6 200.5 %reduce-scatter.5.cloned.1.call-start = ((), (), s32[]{:S(2)}) async-start(), calls=%async_computation.10 | async-start | bytes 3145728 | tf_op jit(solution)/shard_map/reduce_scatter | solution.py:103
  173.8 3.6 copy-start
  173.8 3.6 copy-start.3
  173.8 3.6 copy-start.5
  181.4 1.9 copy-start.1
  192.6 731.8 %reduce-scatter.7.cloned.1.call-start = ((), (), s32[]{:S(2)}) async-start(), calls=%async_computation.12 | async-start | bytes 16908288
  231.3 33.6 %all-to-all-start.6 = ((bf16[1,4,256,1024]{2,3,0,1:T(8,128)(2,1)}), bf16[1,4,256,1024]{2,3,0,1:T(8,128)(2,1)}, u32[]{:S(2)}, u32[]{:S(2)}) async-start(bf16[1,4,256,1024]{2,3,0,1:T(8,128)(2,1)} %copy.71), calls=%async_computation.7 | async-start | bytes 4194304 | tf_op jit(solution)/shard_map/all_to_all | solution.py:89
  264.9 35.7 %all-to-all-start.5 = ((bf16[1,4,256,1024]{2,3,0,1:T(8,128)(2,1)}), bf16[1,4,256,1024]{2,3,0,1:T(8,128)(2,1)S(1)}, u32[]{:S(2)}, u32[]{:S(2)}) async-start(bf16[1,4,256,1024]{2,3,0,1:T(8,128)(2,1)} %copy.68), calls=%async_computation.6 | async-start | bytes 4194304 | tf_op jit(solution)/shard_map/all_to_all | solution.py:86
Sparse Core Ops, SparseCore 0:
  11.6 140.1 all-gather.2
  153.6 22.2 all-gather.4
  192.7 38.3 reduce-scatter.4
  234.1 690.1 reduce-scatter.6
where the time goes:
time: 942 us; the launch traced here: 931 us
  waiting for transfers between devices  666 us (71%)
  local copies, waits for them, and re-layouts  103 us (11%)
  other arithmetic  44.9 us (5%)
  starting transfers between devices  37.1 us (4%)
  matrix products  33.7 us (4%)
  blocking collectives  31.4 us (3%)
  between operations  15.1 us (2%)
    unnamed x5, waiting for transfers between devices  614 us
    unnamed x32, local copies, waits for them, and re-layouts  49.1 us
    unnamed x3, other arithmetic  36.2 us
    unnamed x1, blocking collectives  31.4 us
    all_to_all x1, waiting for transfers between devices, on_device(): lax.all_to_all(key_part.reshape(keys_here.shape), 'blk', split_axis=1, co...  19.5 us
  transfers between devices with their start and end apart: 11, of which 4 were waited for; matrix products, arithmetic and copies ran while one was open for 18% of the time, Pallas kernels for 0%

commit v1 on v0

v1 whole, which is shorter than its diff:
```python
import functools

import jax
import jax.numpy as jnp
import numpy as np
from jax import lax
from jax.experimental import pallas as pl
from jax.experimental.pallas import tpu as pltpu
from jax.sharding import PartitionSpec as P

HDIM = 64
PAIR = 2 * HDIM
SCORE_SCALE = 0.125
LOG2E = float(np.log2(np.e))
SCORE_LOG2 = SCORE_SCALE * LOG2E
NEGATIVE = -1e30
FACTORS = (8, 4, 2, 2)
VMEM_LIMIT = 32 * 1024 * 1024
STAT_ROWS = 8

NT = (((1,), (1,)), ((), ()))
NN = (((1,), (0,)), ((), ()))


def dot(lhs, rhs, dims):
    return lax.dot_general(lhs, rhs, dims, preferred_element_type=jnp.float32)


def head_masks():
    lane = lax.broadcasted_iota(jnp.int32, (1, PAIR), 1)
    first = (lane < HDIM).astype(jnp.float32)
    return first.astype(jnp.bfloat16), (1.0 - first).astype(jnp.bfloat16)


def by_head(rows):
    first, second = head_masks()
    return [rows * first, rows * second]


def valid_keys(lengths, passage_len, shape):
    token = lax.broadcasted_iota(jnp.int32, shape, 0)
    limit = jnp.full(shape, lengths[0], jnp.int32)
    for passage in range(1, len(lengths)):
        limit = jnp.where(
            token >= passage * passage_len, passage * passage_len + lengths[passage], limit
        )
    return token < limit


def local_stats(stacked, key_pair, lengths, passage_len):
    scores = dot(key_pair, stacked, NT) * SCORE_LOG2
    scores = jnp.where(valid_keys(lengths, passage_len, scores.shape), scores, NEGATIVE)
    row_max = jnp.max(scores, axis=0, keepdims=True)
    row_total = jnp.sum(jnp.exp2(scores - row_max), axis=0, keepdims=True)
    return row_max, row_total


def own_stats_kernel(pairs, passage_len, passages, len_ref, q_ref, k_ref, g_ref, o_ref, out_ref):
    lengths = [len_ref[i] for i in range(passages)]
    for j in range(pairs):
        cols = slice(j * PAIR, (j + 1) * PAIR)
        stacked = jnp.concatenate(by_head(q_ref[:, cols]), axis=0)
        row_max, row_total = local_stats(stacked, k_ref[:, cols], lengths, passage_len)
        product = g_ref[:, cols].astype(jnp.float32) * o_ref[:, cols].astype(jnp.float32)
        lane = lax.broadcasted_iota(jnp.int32, product.shape, 1)
        both = jnp.concatenate(
            [jnp.where(lane < HDIM, product, 0.0), jnp.where(lane < HDIM, 0.0, product)], axis=0
        )
        delta = jnp.sum(jnp.transpose(both), axis=0, keepdims=True)
        out_ref[j, 0:1, :] = row_max
        out_ref[j, 1:2, :] = row_total
        out_ref[j, 2:3, :] = delta
        out_ref[j, 3:STAT_ROWS, :] = jnp.zeros((STAT_ROWS - 3, row_max.shape[1]), jnp.float32)


def peer_stats_kernel(pairs, passage_len, passages, len_ref, q_ref, k_ref, own_ref, out_ref):
    lengths = [len_ref[i] for i in range(passages)]
    for j in range(pairs):
        cols = slice(j * PAIR, (j + 1) * PAIR)
        stacked = jnp.concatenate(by_head(q_ref[:, cols]), axis=0)
        row_max, row_total = local_stats(stacked, k_ref[:, cols], lengths, passage_len)
        out_ref[j] = own_ref[j]
        out_ref[j, 3:4, :] = row_max
        out_ref[j, 4:5, :] = row_total


def stats_call(kernel, lengths, key_rows, row_arrays, stat_arrays, passage_len, pairs):
    tokens, hd = key_rows.shape
    rows = row_arrays[0].shape[0]
    total_pairs = hd // PAIR
    wide = pairs * PAIR
    row_spec = pl.BlockSpec((rows, wide), lambda i, s: (0, i))
    key_spec = pl.BlockSpec((tokens, wide), lambda i, s: (0, i))
    stat_spec = pl.BlockSpec((pairs, STAT_ROWS, 2 * rows), lambda i, s: (i, 0, 0))
    return pl.pallas_call(
        functools.partial(kernel, pairs, passage_len, lengths.shape[0]),
        out_shape=jax.ShapeDtypeStruct((total_pairs, STAT_ROWS, 2 * rows), jnp.float32),
        grid_spec=pltpu.PrefetchScalarGridSpec(
            num_scalar_prefetch=1,
            grid=(total_pairs // pairs,),
            in_specs=[row_spec, key_spec]
            + [row_spec] * (len(row_arrays) - 1)
            + [stat_spec] * len(stat_arrays),
            out_specs=stat_spec,
        ),
        compiler_params=pltpu.CompilerParams(vmem_limit_bytes=VMEM_LIMIT),
        cost_estimate=pl.CostEstimate(
            flops=16 * rows * tokens * hd, bytes_accessed=2 * tokens * hd, transcendentals=0
        ),
    )(lengths, row_arrays[0], key_rows, *row_arrays[1:], *stat_arrays)


def grad_kernel(
    pairs, passage_len, passages, carried, s_ref, mine_ref, theirs_ref, qo_ref, qp_ref, go_ref,
    gp_ref, k_ref, v_ref, *rest
):
    dq_ref, dk_ref, dv_ref = rest[2:] if carried else rest
    lengths = [s_ref[1 + i] for i in range(passages)]
    rows = qo_ref.shape[0]
    for j in range(pairs):
        cols = slice(j * PAIR, (j + 1) * PAIR)
        mine, theirs = mine_ref[j], theirs_ref[j]

        def log_total(first_max, first_total, second_max, second_total):
            top = jnp.maximum(first_max, second_max)
            total = first_total * jnp.exp2(first_max - top) + second_total * jnp.exp2(
                second_max - top
            )
            return top + jnp.log2(total)

        lse = jnp.concatenate(
            [
                log_total(mine[0:1], mine[1:2], theirs[3:4], theirs[4:5]),
                log_total(mine[3:4], mine[4:5], theirs[0:1], theirs[1:2]),
            ],
            axis=1,
        )
        delta = jnp.concatenate([mine[2:3], theirs[2:3]], axis=1)
        queries = jnp.concatenate(by_head(qo_ref[:, cols]) + by_head(qp_ref[:, cols]), axis=0)
        grads = jnp.concatenate(by_head(go_ref[:, cols]) + by_head(gp_ref[:, cols]), axis=0)
        key_pair = k_ref[:, cols]
        scores = dot(key_pair, queries, NT)
        probs = jnp.exp2(scores * SCORE_LOG2 - lse)
        probs = jnp.where(valid_keys(lengths, passage_len, scores.shape), probs, 0.0)
        dv_ref[:, cols] = dot(probs.astype(jnp.bfloat16), grads, NN).astype(jnp.bfloat16)
        prob_grad = dot(v_ref[:, cols], grads, NT)
        score_grad = (probs * (prob_grad - delta)).astype(jnp.bfloat16)
        dk_ref[:, cols] = (dot(score_grad, queries, NN) * SCORE_SCALE).astype(jnp.bfloat16)
        query_t = dot(jnp.transpose(key_pair), score_grad, NN) * SCORE_SCALE
        query_grad = jnp.transpose(query_t)
        lane = lax.broadcasted_iota(jnp.int32, (rows, PAIR), 1)
        for which in range(2):
            at = which * 2 * rows
            dq_ref[which, :, cols] = jnp.where(
                lane < HDIM, query_grad[at : at + rows], query_grad[at + rows : at + 2 * rows]
            ).astype(dq_ref.dtype)


def grad_call(scalars, mine, theirs, rows4, key_rows, value_rows, carried, dq_type, passage_len,
              passages, pairs):
    tokens, hd = key_rows.shape
    rows = rows4[0].shape[0]
    half = hd // 2
    wide = pairs * PAIR
    steps = half // wide
    row_spec = pl.BlockSpec((rows, wide), lambda i, s: (0, s[0] * steps + i))
    key_spec = pl.BlockSpec((tokens, wide), lambda i, s: (0, s[0] * steps + i))
    stat_spec = pl.BlockSpec(
        (pairs, STAT_ROWS, 2 * rows), lambda i, s: (s[0] * steps + i, 0, 0)
    )
    any_spec = pl.BlockSpec(memory_space=pl.ANY)
    grad_shape = jax.ShapeDtypeStruct((tokens, hd), jnp.bfloat16)
    return pl.pallas_call(
        functools.partial(grad_kernel, pairs, passage_len, passages, len(carried) > 0),
        out_shape=(jax.ShapeDtypeStruct((2, rows, half), dq_type), grad_shape, grad_shape),
        grid_spec=pltpu.PrefetchScalarGridSpec(
            num_scalar_prefetch=1,
            grid=(steps,),
            in_specs=[stat_spec] * 2 + [row_spec] * 4 + [key_spec] * 2
            + [any_spec] * len(carried),
            out_specs=(
                pl.BlockSpec((2, rows, wide), lambda i, s: (0, 0, i)), key_spec, key_spec
            ),
        ),
        input_output_aliases={9: 1, 10: 2} if carried else {},
        compiler_params=pltpu.CompilerParams(vmem_limit_bytes=VMEM_LIMIT),
        cost_estimate=pl.CostEstimate(
            flops=40 * rows * tokens * hd, bytes_accessed=4 * tokens * hd, transcendentals=0
        ),
    )(scalars, mine, theirs, *rows4, key_rows, value_rows, *carried)


def on_device(hidden, query, out_grad, attn_out, keys, values, lengths, w_query):
    nz, ny, nx, nc = FACTORS
    plane = ny * nx * nc
    blk, pb = lax.axis_index("blk"), lax.axis_index("pb")
    z_at, core = pb // plane, lax.rem(pb, nc)
    plane_groups = [[z * plane + r for r in range(plane)] for z in range(nz)]

    def other_blk(x):
        return lax.ppermute(x, "blk", [(0, 1), (1, 0)])

    def other_core(x):
        return lax.ppermute(x, "pb", [(i, i ^ 1) for i in range(nz * plane)])

    def from_z(x, offset):
        total = nz * plane
        return lax.ppermute(
            x, "pb", [(i, (i - offset * plane) % total) for i in range(total)]
        )

    tokens = keys.shape[1] * keys.shape[2]
    passages, passage_len = keys.shape[1], keys.shape[2]
    hd = keys.shape[3]
    rows, width = hidden.shape[1], hidden.shape[2]
    key_rows, value_rows = keys.reshape(tokens, hd), values.reshape(tokens, hd)
    q_own, g_own, o_own = query[0], out_grad[0], attn_out[0]

    q_peer = other_blk(q_own)
    g_peer = other_blk(g_own)

    w_tile = lax.all_gather(w_query, "pb", axis=0, tiled=True, axis_index_groups=plane_groups)
    tile = width // nz

    q_peer, hidden_rows = lax.optimization_barrier((q_peer, hidden[0]))

    def column_block(offset):
        at = lax.rem(z_at + (nz - offset), nz) * tile
        return lax.dynamic_slice_in_dim(hidden_rows, at, tile, axis=1)

    hidden_own = jnp.stack(
        [column_block(0)] + [from_z(column_block(s), s) for s in range(1, nz)], axis=0
    )
    hidden_peer = other_blk(hidden_own)
    hidden_t = jnp.transpose(
        jnp.concatenate([hidden_own, hidden_peer], axis=1).reshape(nz * 2 * rows, tile)
    )

    lens = lengths[0]
    stat_pairs = min(4, hd // PAIR)
    stats_own = stats_call(
        own_stats_kernel, lens, key_rows, [q_own, g_own, o_own], [], passage_len, stat_pairs
    )
    mine = stats_call(
        peer_stats_kernel, lens, key_rows, [q_peer], [stats_own], passage_len, stat_pairs
    )
    theirs = other_blk(mine)

    rows4 = [q_own, q_peer, g_own, g_peer]
    grad_pairs = min(2, hd // PAIR // 2)

    def half_grad(which, carried, dq_type):
        scalars = jnp.concatenate([jnp.reshape(which, (1,)), lens]).astype(jnp.int32)
        return grad_call(scalars, mine, theirs, rows4, key_rows, value_rows, carried, dq_type,
                         passage_len, passages, grad_pairs)

    dq_send, key_part, value_part = half_grad(1 - blk, (), jnp.bfloat16)
    dq_here, key_grad, value_grad = half_grad(blk, (key_part, value_part), jnp.float32)
    dq_there = other_blk(dq_send)
    qg_own = (dq_here[0] + dq_there[1].astype(jnp.float32)).astype(jnp.bfloat16)
    qg_peer = (dq_here[1] + dq_there[0].astype(jnp.float32)).astype(jnp.bfloat16)

    qg_own, qg_peer, hidden_t = lax.optimization_barrier((qg_own, qg_peer, hidden_t))

    blocks = [[None] * nz, [None] * nz]
    for part, start in enumerate((qg_own, qg_peer)):
        blocks[part][0] = start
    ups, downs = (nz // 2, nz - 1 - nz // 2), (nz - 1 - nz // 2, nz // 2)
    for step in range(1, nz // 2 + 1):
        for part in range(2):
            if step <= ups[part]:
                blocks[part][step] = from_z(blocks[part][step - 1], 1)
            if step <= downs[part]:
                blocks[part][nz - step] = from_z(blocks[part][(nz - step + 1) % nz], -1)
    qg_all = jnp.concatenate([blocks[part][s] for s in range(nz) for part in range(2)], axis=0)

    w_term = lax.dot_general(hidden_t, qg_all, NN, preferred_element_type=jnp.float32)
    state_term = lax.dot_general(qg_all, w_tile, NT, preferred_element_type=jnp.float32)

    w_term = w_term.reshape(ny * nx, nc, -1, w_term.shape[1])
    kept = lax.dynamic_index_in_dim(w_term, core, axis=1, keepdims=False)
    given = lax.dynamic_index_in_dim(w_term, 1 - core, axis=1, keepdims=False)
    w_sum = (kept + other_core(given)).astype(jnp.bfloat16)
    plane_at = lax.rem(pb, plane) // nc

    def across_plane(flip):
        block = lax.dynamic_index_in_dim(w_sum, plane_at ^ flip, axis=0, keepdims=False)
        if flip == 0:
            return block
        return lax.ppermute(block, "pb", [(i, i ^ (flip * nc)) for i in range(nz * plane)])

    w_query_grad = sum(across_plane(flip).astype(jnp.float32) for flip in range(ny * nx))

    state_term = state_term.reshape(nz, 2, rows, tile)
    state_sum = state_term[:, 0] + other_blk(state_term[:, 1].astype(jnp.bfloat16)).astype(
        jnp.float32
    )
    state_sum = state_sum.astype(jnp.bfloat16)
    arrived = [state_sum[0]] + [from_z(state_sum[nz - s], s) for s in range(1, nz)]
    state_all = lax.dynamic_slice_in_dim(
        jnp.stack(arrived + arrived, axis=0), lax.rem(nz - z_at, nz), nz, axis=0
    )
    hidden_grad = jnp.transpose(state_all, (1, 0, 2)).reshape(hidden.shape)
    return (hidden_grad, key_grad.reshape(keys.shape), value_grad.reshape(values.shape),
            w_query_grad)


def solution(mesh):
    return jax.shard_map(
        on_device,
        mesh=mesh,
        in_specs=(
            P("pb", "blk", None),
            P("pb", "blk", None),
            P("pb", "blk", None),
            P("pb", "blk", None),
            P("pb", "blk", None, None),
            P("pb", "blk", None, None),
            P("pb", "blk"),
            P("pb", "blk"),
        ),
        out_specs=(
            P("pb", "blk", None),
            P("pb", "blk", None, None),
            P("pb", "blk", None, None),
            P("pb", "blk"),
        ),
        check_vma=False,
    )
```

time: 942 us -> 165 us (0.18)
  waiting for transfers between devices: 666 us -> 32.3 us
  local copies, waits for them, and re-layouts: 103 us -> 15.9 us
  other arithmetic: 44.9 us -> 5.83 us
  starting transfers between devices: 37.1 us -> 72.3 us
  blocking collectives: 31.4 us -> 0 us
  matrix products: 33.7 us -> 4.4 us
  Pallas kernels: 0 us -> 18.4 us
    unnamed x5 -> x1, waiting for transfers between devices: 614 us -> 0.02 us
    ppermute x0 -> x42, starting transfers between devices: none -> 72.3 us  [the longest x28 50.2 us: from_z(): lax.ppermute(x, 'pb', [(i, (i - offset * plane) % total) for i in range(t...]
    all_to_all x7 -> x0, waiting for transfers between devices: 52.4 us -> none  [the longest x1 19.5 us: on_device(): lax.all_to_all(key_part.reshape(keys_here.shape), 'blk', split_axis=1, co...]
    all_to_all x7 -> x0, starting transfers between devices: 37 us -> none  [the longest x1 6.61 us: on_device(): lax.all_to_all(values, 'blk', split_axis=3, concat_axis=1, tiled=True)]
    unnamed x32 -> x64, local copies, waits for them, and re-layouts: 49.1 us -> 12.8 us
    unnamed x3 -> x0, other arithmetic: 36.2 us -> none
    unnamed x1 -> x0, blocking collectives: 31.4 us -> none
    all_to_all x11 -> x0, local copies, waits for them, and re-layouts: 30.1 us -> none  [the longest x2 10.7 us: on_device(): lax.all_to_all(value_part.reshape(values_here.shape), 'blk', split_axis=1...]
  transfers between devices with their start and end apart: 11 -> 43, of which waited for: 4 -> 19; matrix products, arithmetic and copies ran while one was open for 18% -> 10% of each run, Pallas kernels for 0% -> 11%
where the time goes in v1:
time: 165 us; the launch traced here: 164 us
  starting transfers between devices  72.3 us (44%)
  waiting for transfers between devices  32.3 us (20%)
  Pallas kernels  18.4 us (11%)
  local copies, waits for them, and re-layouts  15.9 us (10%)
  between operations  14.5 us (9%)
  other arithmetic  5.83 us (4%)
  matrix products  4.4 us (3%)
    ppermute x28, starting transfers between devices, from_z(): lax.ppermute(x, 'pb', [(i, (i - offset * plane) % total) for i in range(t...  50.2 us
    ppermute x28, waiting for transfers between devices, from_z(): lax.ppermute(x, 'pb', [(i, (i - offset * plane) % total) for i in range(t...  22.7 us
    ppermute x7, starting transfers between devices, across_plane(): lax.ppermute(block, 'pb', [(i, i ^ flip * nc) for i in range(nz * plane)])  13.8 us
    unnamed x64, local copies, waits for them, and re-layouts  12.8 us
    pallas_call x2, Pallas kernels, grad_call(): pl.pallas_call(functools.partial(grad_kernel, pairs, passage_len, passage...  12.7 us
    ppermute x6, starting transfers between devices, other_blk(): return lax.ppermute(x, 'blk', [(0, 1), (1, 0)])  7.95 us
    pallas_call x2, Pallas kernels, stats_call(): pl.pallas_call(functools.partial(kernel, pairs, passage_len, lengths.shap...  5.75 us
    ppermute x6, waiting for transfers between devices, other_blk(): return lax.ppermute(x, 'blk', [(0, 1), (1, 0)])  5.43 us
  transfers between devices with their start and end apart: 43, of which 19 were waited for; matrix products, arithmetic and copies ran while one was open for 10% of the time, Pallas kernels for 11%

profile of v1, /device:TPU:2, one launch (start us, length us, event | category | flops | bytes accessed | tf_op | source)
XLA Modules:
  0.0 163.5 jit_solution(748272776006197518)
XLA Ops:
  7.2 2.4 %collective-permute-start = (bf16[64,2048]{1,0:T(8,128)(2,1)}, bf16[64,2048]{1,0:T(8,128)(2,1)S(1)}, u32[]{:S(2)}, u32[]{:S(2)}) collective-permute-start(bf16[64,2048]{1,0:T(8,128)(2,1)} %bitcast.120), channel_id=1, source_target_pairs={{0,128},{128,0},{1,129},{129,1},{2,130},{130,2},{3,131},{131,3},{4... | collective-permute-start | bytes 786440 | tf_op jit(solution)/shard_map/ppermute | solution.py:201
  10.3 1.6 copy-done.1
  14.8 2.9 %shard_map.111.own_ref = f32[16,8,128]{2,1,0:T(8,128)S(1)} custom-call(s32[2]{0:T(128)S(1)} %bitcast.110, bf16[64,2048]{1,0:T(8,128)(2,1)S(1)} %bitcast.121, bf16[512,2048]{1,0:T(8,128)(2,1)S(1)} %bitcast.113, bf16[64,2048]{1,0:T(8,128)(2,1)S(1)} %bitcast.125, bf16[64,2048]{1,0:T(8,128)(2,1)S(1)} %bitcast.119), custom_call_target="tpu_custom_call" | custom-call | flops 1073741824 | bytes 2097152 | tf_op jit(solution)/shard_map/pallas_call | solution.py:95
  17.8 2.8 %shard_map.112.mine_ref = f32[16,8,128]{2,1,0:T(8,128)S(1)} custom-call(s32[2]{0:T(128)S(1)} %bitcast.112, bf16[64,2048]{1,0:T(8,128)(2,1)S(1)} %collective-permute-done.q_ref.qp_ref, bf16[512,2048]{1,0:T(8,128)(2,1)S(1)} %bitcast.114, f32[16,8,128]{2,1,0:T(8,128)S(1)} %shard_map.111.own_ref), custom_call_target="tpu_custom_call" | custom-call | flops 1073741824 | bytes 2097152 | tf_op jit(solution)/shard_map/pallas_call | solution.py:95
  20.6 2.0 %collective-permute-start.1 = (f32[16,8,128]{2,1,0:T(8,128)S(1)}, f32[16,8,128]{2,1,0:T(8,128)S(1)}, u32[]{:S(2)}, u32[]{:S(2)}) collective-permute-start(f32[16,8,128]{2,1,0:T(8,128)S(1)} %shard_map.112.mine_ref), channel_id=1, source_target_pairs={{0,128},{128,0},{1,129},{129,1},{2,130},{130,2},{3,131},{131,3},{4... | collective-permute-start | bytes 196616 | tf_op jit(solution)/shard_map/ppermute | solution.py:201
  22.7 4.2 %collective-permute-start.4 = (bf16[64,512]{1,0:T(8,128)(2,1)S(1)}, bf16[64,512]{1,0:T(8,128)(2,1)S(1)}, u32[]{:S(2)}, u32[]{:S(2)}) collective-permute-start(bf16[64,512]{1,0:T(8,128)(2,1)S(1)} %get-tuple-element.49), channel_id=1, source_target_pairs={{0,112},{1,113},{2,114},{3,115},{4,116},{5,117},{6,118},{7,119},{8... | collective-permute-start | bytes 196616 | tf_op jit(solution)/shard_map/ppermute | solution.py:208
  26.9 1.5 collective-permute-start.5
  29.4 1.5 collective-permute-done.4
  30.9 3.5 %collective-permute-start.7 = (bf16[64,512]{1,0:T(8,128)(2,1)S(1)}, bf16[64,512]{1,0:T(8,128)(2,1)S(1)}, u32[]{:S(2)}, u32[]{:S(2)}) collective-permute-start(bf16[64,512]{1,0:T(8,128)(2,1)S(1)} %get-tuple-element.46), channel_id=1, source_target_pairs={{0,64},{1,65},{2,66},{3,67},{4,68},{5,69},{6,70},{7,71},{8,72},{9,... | collective-permute-start | bytes 196616 | tf_op jit(solution)/shard_map/ppermute | solution.py:208
  35.1 3.7 %collective-permute-start.8 = (bf16[64,512]{1,0:T(8,128)(2,1)S(1)}, bf16[64,512]{1,0:T(8,128)(2,1)S(1)}, u32[]{:S(2)}, u32[]{:S(2)}) collective-permute-start(bf16[64,512]{1,0:T(8,128)(2,1)S(1)} %get-tuple-element.45), channel_id=1, source_target_pairs={{0,48},{1,49},{2,50},{3,51},{4,52},{5,53},{6,54},{7,55},{8,56},{9,... | collective-permute-start | bytes 196616 | tf_op jit(solution)/shard_map/ppermute | solution.py:208
  40.2 2.4 %collective-permute-start.10 = (bf16[64,512]{1,0:T(8,128)(2,1)S(1)}, bf16[64,512]{1,0:T(8,128)(2,1)S(1)}, u32[]{:S(2)}, u32[]{:S(2)}) collective-permute-start(bf16[64,512]{1,0:T(8,128)(2,1)S(1)} %get-tuple-element.43), channel_id=1, source_target_pairs={{0,16},{1,17},{2,18},{3,19},{4,20},{5,21},{6,22},{7,23},{8,24},{9,... | collective-permute-start | bytes 196616 | tf_op jit(solution)/shard_map/ppermute | solution.py:208
  43.2 1.8 %collective-permute-done.8 = bf16[64,512]{1,0:T(8,128)(2,1)S(1)} collective-permute-done((bf16[64,512]{1,0:T(8,128)(2,1)S(1)}, bf16[64,512]{1,0:T(8,128)(2,1)S(1)}, u32[]{:S(2)}, u32[]{:S(2)}) %collective-permute-start.8) | collective-permute-done | bytes 65568 | tf_op jit(solution)/shard_map/ppermute | solution.py:208
  47.7 1.7 %collective-permute-start.11 = (bf16[8,64,512]{2,1,0:T(8,128)(2,1)}, bf16[8,64,512]{2,1,0:T(8,128)(2,1)}, u32[]{:S(2)}, u32[]{:S(2)}) collective-permute-start(bf16[8,64,512]{2,1,0:T(8,128)(2,1)} %constant_dynamic-update-slice_fusion), channel_id=1, source_target_pairs={{0,128},{128,0},{1,129},{129,1},{2,130},{130,2},{3,131},{131,3},{4... | collective-permute-start | bytes 1572872 | tf_op jit(solution)/shard_map/ppermute | solution.py:201
  49.4 6.3 %shard_map.113 = (bf16[2,64,1024]{2,1,0:T(8,128)(2,1)S(1)}, bf16[512,2048]{1,0:T(8,128)(2,1)}, bf16[512,2048]{1,0:T(8,128)(2,1)}) custom-call(s32[3]{0:T(128)S(1)} %get-tuple-element.50.s_ref, f32[16,8,128]{2,1,0:T(8,128)S(1)} %shard_map.112.mine_ref, f32[16,8,128]{2,1,0:T(8,128)S(1)} %collective-permute-done.1.theirs_ref, bf16[64,2048]{1,0:T(8,128)(2,1)S(1)} %bitcast.122, ...), custom_call_target="tpu_custom_call" | custom-call | flops 2684354560 | bytes 4194304 | tf_op jit(solution)/shard_map/pallas_call | solution.py:173
  56.2 1.6 copy-done.4
  57.8 6.3 %shard_map.114 = (f32[2,64,1024]{2,1,0:T(8,128)S(1)}, bf16[512,2048]{1,0:T(8,128)(2,1)}, bf16[512,2048]{1,0:T(8,128)(2,1)}) custom-call(s32[3]{0:T(128)S(1)} %get-tuple-element.51.s_ref, f32[16,8,128]{2,1,0:T(8,128)S(1)} %shard_map.112.mine_ref, f32[16,8,128]{2,1,0:T(8,128)S(1)} %collective-permute-done.1.theirs_ref, ...), custom_call_target="tpu_custom_call", output_to_operand_aliasing={{1}: (9, {}), {2}: (10, {})} | custom-call | flops 2684354560 | bytes 4194304 | tf_op jit(solution)/shard_map/pallas_call | solution.py:173
  64.1 2.6 %collective-permute-done.3 = bf16[2,64,1024]{2,1,0:T(8,128)(2,1)} collective-permute-done((bf16[2,64,1024]{2,1,0:T(8,128)(2,1)S(1)}, bf16[2,64,1024]{2,1,0:T(8,128)(2,1)}, u32[]{:S(2)}, u32[]{:S(2)}) %collective-permute-start.3) | collective-permute-done | bytes 262176 | tf_op jit(solution)/shard_map/ppermute | solution.py:201
  67.7 1.3 pad_maximum_fusion
  69.8 1.6 %collective-permute-start.19 = (bf16[64,1024]{1,0:T(8,128)(2,1)S(1)}, bf16[64,1024]{1,0:T(8,128)(2,1)S(1)}, u32[]{:S(2)}, u32[]{:S(2)}) collective-permute-start(bf16[64,1024]{1,0:T(8,128)(2,1)S(1)} %get-tuple-element.22), channel_id=1, source_target_pairs={{0,16},{1,17},{2,18},{3,19},{4,20},{5,21},{6,22},{7,23},{8,24},{9,... | collective-permute-start | bytes 393224 | tf_op jit(solution)/shard_map/ppermute | solution.py:208
  71.5 1.9 %collective-permute-start.23 = (bf16[64,1024]{1,0:T(8,128)(2,1)S(1)}, bf16[64,1024]{1,0:T(8,128)(2,1)S(1)}, u32[]{:S(2)}, u32[]{:S(2)}) collective-permute-start(bf16[64,1024]{1,0:T(8,128)(2,1)S(1)} %get-tuple-element.21), channel_id=1, source_target_pairs={{0,16},{1,17},{2,18},{3,19},{4,20},{5,21},{6,22},{7,23},{8,24},{9,... | collective-permute-start | bytes 393224 | tf_op jit(solution)/shard_map/ppermute | solution.py:208
  74.4 1.5 collective-permute-start.14
  75.9 1.2 collective-permute-done.13
  77.8 1.3 collective-permute-start.20
  80.1 2.4 %collective-permute-start.16 = (bf16[64,1024]{1,0:T(8,128)(2,1)S(1)}, bf16[64,1024]{1,0:T(8,128)(2,1)S(1)}, u32[]{:S(2)}, u32[]{:S(2)}) collective-permute-start(bf16[64,1024]{1,0:T(8,128)(2,1)S(1)} %collective-permute-done.14), channel_id=1, source_target_pairs={{0,112},{1,113},{2,114},{3,115},{4,116},{5,117},{6,118},{7,119},{8... | collective-permute-start | bytes 393224 | tf_op jit(solution)/shard_map/ppermute | solution.py:208
  83.4 1.9 %collective-permute-start.17 = (bf16[64,1024]{1,0:T(8,128)(2,1)S(1)}, bf16[64,1024]{1,0:T(8,128)(2,1)S(1)}, u32[]{:S(2)}, u32[]{:S(2)}) collective-permute-start(bf16[64,1024]{1,0:T(8,128)(2,1)S(1)} %collective-permute-done.15), channel_id=1, source_target_pairs={{0,112},{1,113},{2,114},{3,115},{4,116},{5,117},{6,118},{7,119},{8... | collective-permute-start | bytes 393224 | tf_op jit(solution)/shard_map/ppermute | solution.py:208
  85.5 1.7 %collective-permute-done.24 = bf16[64,1024]{1,0:T(8,128)(2,1)S(1)} collective-permute-done((bf16[64,1024]{1,0:T(8,128)(2,1)S(1)}, bf16[64,1024]{1,0:T(8,128)(2,1)S(1)}, u32[]{:S(2)}, u32[]{:S(2)}) %collective-permute-start.24) | collective-permute-done | bytes 131104 | tf_op jit(solution)/shard_map/ppermute | solution.py:208
  87.3 3.1 %collective-permute-start.18 = (bf16[64,1024]{1,0:T(8,128)(2,1)S(1)}, bf16[64,1024]{1,0:T(8,128)(2,1)S(1)}, u32[]{:S(2)}, u32[]{:S(2)}) collective-permute-start(bf16[64,1024]{1,0:T(8,128)(2,1)S(1)} %collective-permute-done.16), channel_id=1, source_target_pairs={{0,112},{1,113},{2,114},{3,115},{4,116},{5,117},{6,118},{7,119},{8... | collective-permute-start | bytes 393224 | tf_op jit(solution)/shard_map/ppermute | solution.py:208
  90.4 2.4 %collective-permute-done.21 = bf16[64,1024]{1,0:T(8,128)(2,1)S(1)} collective-permute-done((bf16[64,1024]{1,0:T(8,128)(2,1)S(1)}, bf16[64,1024]{1,0:T(8,128)(2,1)S(1)}, u32[]{:S(2)}, u32[]{:S(2)}) %collective-permute-start.21) | collective-permute-done | bytes 131104 | tf_op jit(solution)/shard_map/ppermute | solution.py:208
  92.9 6.0 %collective-permute-done.22 = bf16[64,1024]{1,0:T(8,128)(2,1)S(1)} collective-permute-done((bf16[64,1024]{1,0:T(8,128)(2,1)S(1)}, bf16[64,1024]{1,0:T(8,128)(2,1)S(1)}, u32[]{:S(2)}, u32[]{:S(2)}) %collective-permute-start.22) | collective-permute-done | bytes 131104 | tf_op jit(solution)/shard_map/ppermute | solution.py:208
  99.1 1.3 fusion.13
  100.9 3.4 %all-gather.2.cloned.1.call-done = bf16[512,1024]{1,0:T(8,128)(2,1)} async-done(((bf16[32,1024]{1,0:T(8,128)(2,1)}), bf16[512,1024]{1,0:T(8,128)(2,1)}) %all-gather.2.cloned.1.call-update) | async-done | bytes 1048592 | tf_op jit(solution)/shard_map/all_gather | solution.py:222
  104.3 3.1 %fusion.12 = f32[1024,512]{1,0:T(8,128)S(1)} fusion(bf16[1024,1024]{1,0:T(8,128)(2,1)} %copy-done.10, bf16[512,1024]{1,0:T(8,128)(2,1)} %all-gather.2.cloned.1.call-done), kind=kOutput, calls=%fused_computation.84 | convolution fusion | flops 1073741824 | bytes 5242880 | tf_op jit(solution)/shard_map/dot_general | solution.py:278
  107.5 1.3 copy-done.11
  109.7 1.5 collective-permute-start.26
  111.1 1.5 fusion.2
  112.7 2.7 %collective-permute-start.41 = (bf16[32,1024]{1,0:T(8,128)(2,1)S(1)}, bf16[32,1024]{1,0:T(8,128)(2,1)S(1)}, u32[]{:S(2)}, u32[]{:S(2)}) collective-permute-start(bf16[32,1024]{1,0:T(8,128)(2,1)S(1)} %get-tuple-element.29), channel_id=1, source_target_pairs={{0,14},{1,15},{2,12},{3,13},{4,10},{5,11},{6,8},{7,9},{8,6},{9,7},... | collective-permute-start | bytes 196616 | tf_op jit(solution)/shard_map/ppermute | solution.py:290
  116.3 3.1 %collective-permute-start.39 = (bf16[32,1024]{1,0:T(8,128)(2,1)S(1)}, bf16[32,1024]{1,0:T(8,128)(2,1)S(1)}, u32[]{:S(2)}, u32[]{:S(2)}) collective-permute-start(bf16[32,1024]{1,0:T(8,128)(2,1)S(1)} %get-tuple-element.31), channel_id=1, source_target_pairs={{0,10},{1,11},{2,8},{3,9},{4,14},{5,15},{6,12},{7,13},{8,2},{9,3},... | collective-permute-start | bytes 196616 | tf_op jit(solution)/shard_map/ppermute | solution.py:290
  119.4 2.5 %collective-permute-start.38 = (bf16[32,1024]{1,0:T(8,128)(2,1)S(1)}, bf16[32,1024]{1,0:T(8,128)(2,1)S(1)}, u32[]{:S(2)}, u32[]{:S(2)}) collective-permute-start(bf16[32,1024]{1,0:T(8,128)(2,1)S(1)} %get-tuple-element.32), channel_id=1, source_target_pairs={{0,8},{1,9},{2,10},{3,11},{4,12},{5,13},{6,14},{7,15},{8,0},{9,1},... | collective-permute-start | bytes 196616 | tf_op jit(solution)/shard_map/ppermute | solution.py:290
  121.9 2.8 %collective-permute-done.26 = bf16[8,64,512]{2,1,0:T(8,128)(2,1)} collective-permute-done((bf16[8,64,512]{2,1,0:T(8,128)(2,1)}, bf16[8,64,512]{2,1,0:T(8,128)(2,1)}, u32[]{:S(2)}, u32[]{:S(2)}) %collective-permute-start.26) | collective-permute-done | bytes 524320 | tf_op jit(solution)/shard_map/ppermute | solution.py:201
  124.7 2.3 %collective-permute-start.37 = (bf16[32,1024]{1,0:T(8,128)(2,1)S(1)}, bf16[32,1024]{1,0:T(8,128)(2,1)S(1)}, u32[]{:S(2)}, u32[]{:S(2)}) collective-permute-start(bf16[32,1024]{1,0:T(8,128)(2,1)S(1)} %get-tuple-element.33), channel_id=1, source_target_pairs={{0,6},{1,7},{2,4},{3,5},{4,2},{5,3},{6,0},{7,1},{8,14},{9,15},{10,... | collective-permute-start | bytes 196616 | tf_op jit(solution)/shard_map/ppermute | solution.py:290
  128.9 2.2 %collective-permute-start.35 = (bf16[32,1024]{1,0:T(8,128)(2,1)S(1)}, bf16[32,1024]{1,0:T(8,128)(2,1)S(1)}, u32[]{:S(2)}, u32[]{:S(2)}) collective-permute-start(bf16[32,1024]{1,0:T(8,128)(2,1)S(1)} %get-tuple-element.28), channel_id=1, source_target_pairs={{0,2},{1,3},{2,0},{3,1},{4,6},{5,7},{6,4},{7,5},{8,10},{9,11},{10,... | collective-permute-start | bytes 196616 | tf_op jit(solution)/shard_map/ppermute | solution.py:290
  131.1 3.5 %collective-permute-start.27 = (bf16[64,512]{1,0:T(8,128)(2,1)S(1)}, bf16[64,512]{1,0:T(8,128)(2,1)S(1)}, u32[]{:S(2)}, u32[]{:S(2)}) collective-permute-start(bf16[64,512]{1,0:T(8,128)(2,1)S(1)} %get-tuple-element.42), channel_id=1, source_target_pairs={{0,112},{1,113},{2,114},{3,115},{4,116},{5,117},{6,118},{7,119},{8... | collective-permute-start | bytes 196616 | tf_op jit(solution)/shard_map/ppermute | solution.py:208
  135.4 4.1 %collective-permute-start.28 = (bf16[64,512]{1,0:T(8,128)(2,1)S(1)}, bf16[64,512]{1,0:T(8,128)(2,1)S(1)}, u32[]{:S(2)}, u32[]{:S(2)}) collective-permute-start(bf16[64,512]{1,0:T(8,128)(2,1)S(1)} %get-tuple-element.41), channel_id=1, source_target_pairs={{0,96},{1,97},{2,98},{3,99},{4,100},{5,101},{6,102},{7,103},{8,104... | collective-permute-start | bytes 196616 | tf_op jit(solution)/shard_map/ppermute | solution.py:208
  139.5 2.1 %collective-permute-start.29 = (bf16[64,512]{1,0:T(8,128)(2,1)S(1)}, bf16[64,512]{1,0:T(8,128)(2,1)S(1)}, u32[]{:S(2)}, u32[]{:S(2)}) collective-permute-start(bf16[64,512]{1,0:T(8,128)(2,1)S(1)} %get-tuple-element.40), channel_id=1, source_target_pairs={{0,80},{1,81},{2,82},{3,83},{4,84},{5,85},{6,86},{7,87},{8,88},{9,... | collective-permute-start | bytes 196616 | tf_op jit(solution)/shard_map/ppermute | solution.py:208
  141.6 3.0 %collective-permute-start.30 = (bf16[64,512]{1,0:T(8,128)(2,1)S(1)}, bf16[64,512]{1,0:T(8,128)(2,1)S(1)}, u32[]{:S(2)}, u32[]{:S(2)}) collective-permute-start(bf16[64,512]{1,0:T(8,128)(2,1)S(1)} %get-tuple-element.39), channel_id=1, source_target_pairs={{0,64},{1,65},{2,66},{3,67},{4,68},{5,69},{6,70},{7,71},{8,72},{9,... | collective-permute-start | bytes 196616 | tf_op jit(solution)/shard_map/ppermute | solution.py:208
  145.3 3.8 %collective-permute-start.32 = (bf16[64,512]{1,0:T(8,128)(2,1)S(1)}, bf16[64,512]{1,0:T(8,128)(2,1)S(1)}, u32[]{:S(2)}, u32[]{:S(2)}) collective-permute-start(bf16[64,512]{1,0:T(8,128)(2,1)S(1)} %get-tuple-element.37), channel_id=1, source_target_pairs={{0,32},{1,33},{2,34},{3,35},{4,36},{5,37},{6,38},{7,39},{8,40},{9,... | collective-permute-start | bytes 196616 | tf_op jit(solution)/shard_map/ppermute | solution.py:208
  149.8 2.1 %collective-permute-done.30 = bf16[64,512]{1,0:T(8,128)(2,1)S(1)} collective-permute-done((bf16[64,512]{1,0:T(8,128)(2,1)S(1)}, bf16[64,512]{1,0:T(8,128)(2,1)S(1)}, u32[]{:S(2)}, u32[]{:S(2)}) %collective-permute-start.30) | collective-permute-done | bytes 65568 | tf_op jit(solution)/shard_map/ppermute | solution.py:208
  152.0 2.2 %collective-permute-done.31 = bf16[64,512]{1,0:T(8,128)(2,1)S(1)} collective-permute-done((bf16[64,512]{1,0:T(8,128)(2,1)S(1)}, bf16[64,512]{1,0:T(8,128)(2,1)S(1)}, u32[]{:S(2)}, u32[]{:S(2)}) %collective-permute-start.31) | collective-permute-done | bytes 65568 | tf_op jit(solution)/shard_map/ppermute | solution.py:208
  (126 shorter events, 25.4 us)
Async XLA Ops:
  7.2 97.1 %all-gather.2.cloned.1.call-start = ((), (), s32[]{:S(2)}) async-start(), calls=%async_computation | async-start | bytes 1114112 | tf_op jit(solution)/shard_map/all_gather | solution.py:222
  7.2 10.6 %collective-permute-start = (bf16[64,2048]{1,0:T(8,128)(2,1)}, bf16[64,2048]{1,0:T(8,128)(2,1)S(1)}, u32[]{:S(2)}, u32[]{:S(2)}) collective-permute-start(bf16[64,2048]{1,0:T(8,128)(2,1)} %bitcast.120), channel_id=1, source_target_pairs={{0,128},{128,0},{1,129},{129,1},{2,130},{130,2},{3,131},{131,3},{4... | collective-permute-start | bytes 786440 | tf_op jit(solution)/shard_map/ppermute | solution.py:201
  9.6 39.8 %collective-permute-start.2 = (bf16[64,2048]{1,0:T(8,128)(2,1)}, bf16[64,2048]{1,0:T(8,128)(2,1)S(1)}, u32[]{:S(2)}, u32[]{:S(2)}) collective-permute-start(bf16[64,2048]{1,0:T(8,128)(2,1)} %bitcast.124), channel_id=1, source_target_pairs={{0,128},{128,0},{1,129},{129,1},{2,130},{130,2},{3,131},{131,3},{4... | collective-permute-start | bytes 786440 | tf_op jit(solution)/shard_map/ppermute | solution.py:201
  17.7 4.9 %copy-start.13 = (bf16[1,64,4096]{2,1,0:T(8,128)(2,1)S(1)}, bf16[1,64,4096]{2,1,0:T(8,128)(2,1)}, u32[]{:S(2)}) copy-start(bf16[1,64,4096]{2,1,0:T(8,128)(2,1)} %param.8) | copy-start | bytes 1572868
  17.8 31.6 %copy-start.3 = (bf16[1,2,256,2048]{3,2,1,0:T(8,128)(2,1)S(1)}, bf16[1,2,256,2048]{3,2,1,0:T(8,128)(2,1)}, u32[]{:S(2)}) copy-start(bf16[1,2,256,2048]{3,2,1,0:T(8,128)(2,1)} %param.13) | copy-start | bytes 6291460
  17.8 31.6 %copy-start.9 = (bf16[1,64,2048]{2,1,0:T(8,128)(2,1)S(1)}, bf16[1,64,2048]{2,1,0:T(8,128)(2,1)}, u32[]{:S(2)}) copy-start(bf16[1,64,2048]{2,1,0:T(8,128)(2,1)} %param.10) | copy-start | bytes 786436
  20.6 28.8 %collective-permute-start.1 = (f32[16,8,128]{2,1,0:T(8,128)S(1)}, f32[16,8,128]{2,1,0:T(8,128)S(1)}, u32[]{:S(2)}, u32[]{:S(2)}) collective-permute-start(f32[16,8,128]{2,1,0:T(8,128)S(1)} %shard_map.112.mine_ref), channel_id=1, source_target_pairs={{0,128},{128,0},{1,129},{129,1},{2,130},{130,2},{3,131},{131,3},{4... | collective-permute-start | bytes 196616 | tf_op jit(solution)/shard_map/ppermute | solution.py:201
  22.7 8.2 %collective-permute-start.4 = (bf16[64,512]{1,0:T(8,128)(2,1)S(1)}, bf16[64,512]{1,0:T(8,128)(2,1)S(1)}, u32[]{:S(2)}, u32[]{:S(2)}) collective-permute-start(bf16[64,512]{1,0:T(8,128)(2,1)S(1)} %get-tuple-element.49), channel_id=1, source_target_pairs={{0,112},{1,113},{2,114},{3,115},{4,116},{5,117},{6,118},{7,119},{8... | collective-permute-start | bytes 196616 | tf_op jit(solution)/shard_map/ppermute | solution.py:208
  26.9 8.2 %collective-permute-start.5 = (bf16[64,512]{1,0:T(8,128)(2,1)S(1)}, bf16[64,512]{1,0:T(8,128)(2,1)S(1)}, u32[]{:S(2)}, u32[]{:S(2)}) collective-permute-start(bf16[64,512]{1,0:T(8,128)(2,1)S(1)} %get-tuple-element.48), channel_id=1, source_target_pairs={{0,96},{1,97},{2,98},{3,99},{4,100},{5,101},{6,102},{7,103},{8,104... | collective-permute-start | bytes 196616 | tf_op jit(solution)/shard_map/ppermute | solution.py:208
  28.3 11.1 %collective-permute-start.6 = (bf16[64,512]{1,0:T(8,128)(2,1)S(1)}, bf16[64,512]{1,0:T(8,128)(2,1)S(1)}, u32[]{:S(2)}, u32[]{:S(2)}) collective-permute-start(bf16[64,512]{1,0:T(8,128)(2,1)S(1)} %get-tuple-element.47), channel_id=1, source_target_pairs={{0,80},{1,81},{2,82},{3,83},{4,84},{5,85},{6,86},{7,87},{8,88},{9,... | collective-permute-start | bytes 196616 | tf_op jit(solution)/shard_map/ppermute | solution.py:208
  30.9 9.3 %collective-permute-start.7 = (bf16[64,512]{1,0:T(8,128)(2,1)S(1)}, bf16[64,512]{1,0:T(8,128)(2,1)S(1)}, u32[]{:S(2)}, u32[]{:S(2)}) collective-permute-start(bf16[64,512]{1,0:T(8,128)(2,1)S(1)} %get-tuple-element.46), channel_id=1, source_target_pairs={{0,64},{1,65},{2,66},{3,67},{4,68},{5,69},{6,70},{7,71},{8,72},{9,... | collective-permute-start | bytes 196616 | tf_op jit(solution)/shard_map/ppermute | solution.py:208
  35.1 9.9 %collective-permute-start.8 = (bf16[64,512]{1,0:T(8,128)(2,1)S(1)}, bf16[64,512]{1,0:T(8,128)(2,1)S(1)}, u32[]{:S(2)}, u32[]{:S(2)}) collective-permute-start(bf16[64,512]{1,0:T(8,128)(2,1)S(1)} %get-tuple-element.45), channel_id=1, source_target_pairs={{0,48},{1,49},{2,50},{3,51},{4,52},{5,53},{6,54},{7,55},{8,56},{9,... | collective-permute-start | bytes 196616 | tf_op jit(solution)/shard_map/ppermute | solution.py:208
  39.4 7.0 %collective-permute-start.9 = (bf16[64,512]{1,0:T(8,128)(2,1)S(1)}, bf16[64,512]{1,0:T(8,128)(2,1)S(1)}, u32[]{:S(2)}, u32[]{:S(2)}) collective-permute-start(bf16[64,512]{1,0:T(8,128)(2,1)S(1)} %get-tuple-element.44), channel_id=1, source_target_pairs={{0,32},{1,33},{2,34},{3,35},{4,36},{5,37},{6,38},{7,39},{8,40},{9,... | collective-permute-start | bytes 196616 | tf_op jit(solution)/shard_map/ppermute | solution.py:208
  40.2 6.8 %collective-permute-start.10 = (bf16[64,512]{1,0:T(8,128)(2,1)S(1)}, bf16[64,512]{1,0:T(8,128)(2,1)S(1)}, u32[]{:S(2)}, u32[]{:S(2)}) collective-permute-start(bf16[64,512]{1,0:T(8,128)(2,1)S(1)} %get-tuple-element.43), channel_id=1, source_target_pairs={{0,16},{1,17},{2,18},{3,19},{4,20},{5,21},{6,22},{7,23},{8,24},{9,... | collective-permute-start | bytes 196616 | tf_op jit(solution)/shard_map/ppermute | solution.py:208
  47.7 20.0 %collective-permute-start.11 = (bf16[8,64,512]{2,1,0:T(8,128)(2,1)}, bf16[8,64,512]{2,1,0:T(8,128)(2,1)}, u32[]{:S(2)}, u32[]{:S(2)}) collective-permute-start(bf16[8,64,512]{2,1,0:T(8,128)(2,1)} %constant_dynamic-update-slice_fusion), channel_id=1, source_target_pairs={{0,128},{128,0},{1,129},{129,1},{2,130},{130,2},{3,131},{131,3},{4... | collective-permute-start | bytes 1572872 | tf_op jit(solution)/shard_map/ppermute | solution.py:201
  49.4 6.7 %copy-start.7 = (bf16[1,64,2048]{2,1,0:T(8,128)(2,1)S(1)}, bf16[1,64,2048]{2,1,0:T(8,128)(2,1)}, u32[]{:S(2)}) copy-start(bf16[1,64,2048]{2,1,0:T(8,128)(2,1)} %param.9) | copy-start | bytes 786436
  55.8 10.9 %collective-permute-start.3 = (bf16[2,64,1024]{2,1,0:T(8,128)(2,1)S(1)}, bf16[2,64,1024]{2,1,0:T(8,128)(2,1)}, u32[]{:S(2)}, u32[]{:S(2)}) collective-permute-start(bf16[2,64,1024]{2,1,0:T(8,128)(2,1)S(1)} %get-tuple-element.19), channel_id=1, source_target_pairs={{0,128},{128,0},{1,129},{129,1},{2,130},{130,2},{3,131},{131,3},{4... | collective-permute-start | bytes 786440 | tf_op jit(solution)/shard_map/ppermute | solution.py:201
  69.0 5.3 %collective-permute-start.12 = (bf16[64,1024]{1,0:T(8,128)(2,1)S(1)}, bf16[64,1024]{1,0:T(8,128)(2,1)S(1)}, u32[]{:S(2)}, u32[]{:S(2)}) collective-permute-start(bf16[64,1024]{1,0:T(8,128)(2,1)S(1)} %get-tuple-element.21), channel_id=1, source_target_pairs={{0,112},{1,113},{2,114},{3,115},{4,116},{5,117},{6,118},{7,119},{8... | collective-permute-start | bytes 393224 | tf_op jit(solution)/shard_map/ppermute | solution.py:208
  69.3 7.8 %collective-permute-start.13 = (bf16[64,1024]{1,0:T(8,128)(2,1)S(1)}, bf16[64,1024]{1,0:T(8,128)(2,1)S(1)}, u32[]{:S(2)}, u32[]{:S(2)}) collective-permute-start(bf16[64,1024]{1,0:T(8,128)(2,1)S(1)} %get-tuple-element.22), channel_id=1, source_target_pairs={{0,112},{1,113},{2,114},{3,115},{4,116},{5,117},{6,118},{7,119},{8... | collective-permute-start | bytes 393224 | tf_op jit(solution)/shard_map/ppermute | solution.py:208
  69.8 8.0 %collective-permute-start.19 = (bf16[64,1024]{1,0:T(8,128)(2,1)S(1)}, bf16[64,1024]{1,0:T(8,128)(2,1)S(1)}, u32[]{:S(2)}, u32[]{:S(2)}) collective-permute-start(bf16[64,1024]{1,0:T(8,128)(2,1)S(1)} %get-tuple-element.22), channel_id=1, source_target_pairs={{0,16},{1,17},{2,18},{3,19},{4,20},{5,21},{6,22},{7,23},{8,24},{9,... | collective-permute-start | bytes 393224 | tf_op jit(solution)/shard_map/ppermute | solution.py:208
  71.5 7.7 %collective-permute-start.23 = (bf16[64,1024]{1,0:T(8,128)(2,1)S(1)}, bf16[64,1024]{1,0:T(8,128)(2,1)S(1)}, u32[]{:S(2)}, u32[]{:S(2)}) collective-permute-start(bf16[64,1024]{1,0:T(8,128)(2,1)S(1)} %get-tuple-element.21), channel_id=1, source_target_pairs={{0,16},{1,17},{2,18},{3,19},{4,20},{5,21},{6,22},{7,23},{8,24},{9,... | collective-permute-start | bytes 393224 | tf_op jit(solution)/shard_map/ppermute | solution.py:208
  74.4 5.7 %collective-permute-start.14 = (bf16[64,1024]{1,0:T(8,128)(2,1)S(1)}, bf16[64,1024]{1,0:T(8,128)(2,1)S(1)}, u32[]{:S(2)}, u32[]{:S(2)}) collective-permute-start(bf16[64,1024]{1,0:T(8,128)(2,1)S(1)} %collective-permute-done.12), channel_id=1, source_target_pairs={{0,112},{1,113},{2,114},{3,115},{4,116},{5,117},{6,118},{7,119},{8... | collective-permute-start | bytes 393224 | tf_op jit(solution)/shard_map/ppermute | solution.py:208
  77.1 6.3 %collective-permute-start.15 = (bf16[64,1024]{1,0:T(8,128)(2,1)S(1)}, bf16[64,1024]{1,0:T(8,128)(2,1)S(1)}, u32[]{:S(2)}, u32[]{:S(2)}) collective-permute-start(bf16[64,1024]{1,0:T(8,128)(2,1)S(1)} %collective-permute-done.13), channel_id=1, source_target_pairs={{0,112},{1,113},{2,114},{3,115},{4,116},{5,117},{6,118},{7,119},{8... | collective-permute-start | bytes 393224 | tf_op jit(solution)/shard_map/ppermute | solution.py:208
  77.8 7.6 %collective-permute-start.20 = (bf16[64,1024]{1,0:T(8,128)(2,1)S(1)}, bf16[64,1024]{1,0:T(8,128)(2,1)S(1)}, u32[]{:S(2)}, u32[]{:S(2)}) collective-permute-start(bf16[64,1024]{1,0:T(8,128)(2,1)S(1)} %collective-permute-done.19), channel_id=1, source_target_pairs={{0,16},{1,17},{2,18},{3,19},{4,20},{5,21},{6,22},{7,23},{8,24},{9,... | collective-permute-start | bytes 393224 | tf_op jit(solution)/shard_map/ppermute | solution.py:208
  79.2 8.0 %collective-permute-start.24 = (bf16[64,1024]{1,0:T(8,128)(2,1)S(1)}, bf16[64,1024]{1,0:T(8,128)(2,1)S(1)}, u32[]{:S(2)}, u32[]{:S(2)}) collective-permute-start(bf16[64,1024]{1,0:T(8,128)(2,1)S(1)} %collective-permute-done.23), channel_id=1, source_target_pairs={{0,16},{1,17},{2,18},{3,19},{4,20},{5,21},{6,22},{7,23},{8,24},{9,... | collective-permute-start | bytes 393224 | tf_op jit(solution)/shard_map/ppermute | solution.py:208
  80.1 7.2 %collective-permute-start.16 = (bf16[64,1024]{1,0:T(8,128)(2,1)S(1)}, bf16[64,1024]{1,0:T(8,128)(2,1)S(1)}, u32[]{:S(2)}, u32[]{:S(2)}) collective-permute-start(bf16[64,1024]{1,0:T(8,128)(2,1)S(1)} %collective-permute-done.14), channel_id=1, source_target_pairs={{0,112},{1,113},{2,114},{3,115},{4,116},{5,117},{6,118},{7,119},{8... | collective-permute-start | bytes 393224 | tf_op jit(solution)/shard_map/ppermute | solution.py:208
  83.4 9.3 %collective-permute-start.17 = (bf16[64,1024]{1,0:T(8,128)(2,1)S(1)}, bf16[64,1024]{1,0:T(8,128)(2,1)S(1)}, u32[]{:S(2)}, u32[]{:S(2)}) collective-permute-start(bf16[64,1024]{1,0:T(8,128)(2,1)S(1)} %collective-permute-done.15), channel_id=1, source_target_pairs={{0,112},{1,113},{2,114},{3,115},{4,116},{5,117},{6,118},{7,119},{8... | collective-permute-start | bytes 393224 | tf_op jit(solution)/shard_map/ppermute | solution.py:208
  85.4 7.4 %collective-permute-start.21 = (bf16[64,1024]{1,0:T(8,128)(2,1)S(1)}, bf16[64,1024]{1,0:T(8,128)(2,1)S(1)}, u32[]{:S(2)}, u32[]{:S(2)}) collective-permute-start(bf16[64,1024]{1,0:T(8,128)(2,1)S(1)} %collective-permute-done.20), channel_id=1, source_target_pairs={{0,16},{1,17},{2,18},{3,19},{4,20},{5,21},{6,22},{7,23},{8,24},{9,... | collective-permute-start | bytes 393224 | tf_op jit(solution)/shard_map/ppermute | solution.py:208
  87.1 11.8 %collective-permute-start.25 = (bf16[64,1024]{1,0:T(8,128)(2,1)S(1)}, bf16[64,1024]{1,0:T(8,128)(2,1)S(1)}, u32[]{:S(2)}, u32[]{:S(2)}) collective-permute-start(bf16[64,1024]{1,0:T(8,128)(2,1)S(1)} %collective-permute-done.24), channel_id=1, source_target_pairs={{0,16},{1,17},{2,18},{3,19},{4,20},{5,21},{6,22},{7,23},{8,24},{9,... | collective-permute-start | bytes 393224 | tf_op jit(solution)/shard_map/ppermute | solution.py:208
  87.3 5.6 %collective-permute-start.18 = (bf16[64,1024]{1,0:T(8,128)(2,1)S(1)}, bf16[64,1024]{1,0:T(8,128)(2,1)S(1)}, u32[]{:S(2)}, u32[]{:S(2)}) collective-permute-start(bf16[64,1024]{1,0:T(8,128)(2,1)S(1)} %collective-permute-done.16), channel_id=1, source_target_pairs={{0,112},{1,113},{2,114},{3,115},{4,116},{5,117},{6,118},{7,119},{8... | collective-permute-start | bytes 393224 | tf_op jit(solution)/shard_map/ppermute | solution.py:208
  92.8 6.2 %collective-permute-start.22 = (bf16[64,1024]{1,0:T(8,128)(2,1)S(1)}, bf16[64,1024]{1,0:T(8,128)(2,1)S(1)}, u32[]{:S(2)}, u32[]{:S(2)}) collective-permute-start(bf16[64,1024]{1,0:T(8,128)(2,1)S(1)} %collective-permute-done.21), channel_id=1, source_target_pairs={{0,16},{1,17},{2,18},{3,19},{4,20},{5,21},{6,22},{7,23},{8,24},{9,... | collective-permute-start | bytes 393224 | tf_op jit(solution)/shard_map/ppermute | solution.py:208
  100.5 10.6 %collective-permute-start.34 = (f32[8,32,1024]{2,1,0:T(8,128)S(1)}, f32[8,32,1024]{2,1,0:T(8,128)}, u32[]{:S(2)}, u32[]{:S(2)}) collective-permute-start(f32[8,32,1024]{2,1,0:T(8,128)S(1)} %dynamic-slice_bitcast_fusion), channel_id=1, source_target_pairs={{0,1},{1,0},{2,3},{3,2},{4,5},{5,4},{6,7},{7,6},{8,9},{9,8},{10,11... | collective-permute-start | bytes 3145736 | tf_op jit(solution)/shard_map/ppermute | solution.py:204
  109.7 15.1 %collective-permute-start.26 = (bf16[8,64,512]{2,1,0:T(8,128)(2,1)}, bf16[8,64,512]{2,1,0:T(8,128)(2,1)}, u32[]{:S(2)}, u32[]{:S(2)}) collective-permute-start(bf16[8,64,512]{2,1,0:T(8,128)(2,1)} %fusion.3), channel_id=1, source_target_pairs={{0,128},{128,0},{1,129},{129,1},{2,130},{130,2},{3,131},{131,3},{4... | collective-permute-start | bytes 1572872 | tf_op jit(solution)/shard_map/ppermute | solution.py:201
  111.1 15.9 %copy-start.12 = (f32[1024,512]{1,0:T(8,128)S(1)}, f32[1024,512]{1,0:T(8,128)}, u32[]{:S(2)}) copy-start(f32[1024,512]{1,0:T(8,128)} %copy-done.11) | copy-start | bytes 6291460
  112.7 16.1 %collective-permute-start.41 = (bf16[32,1024]{1,0:T(8,128)(2,1)S(1)}, bf16[32,1024]{1,0:T(8,128)(2,1)S(1)}, u32[]{:S(2)}, u32[]{:S(2)}) collective-permute-start(bf16[32,1024]{1,0:T(8,128)(2,1)S(1)} %get-tuple-element.29), channel_id=1, source_target_pairs={{0,14},{1,15},{2,12},{3,13},{4,10},{5,11},{6,8},{7,9},{8,6},{9,7},... | collective-permute-start | bytes 196616 | tf_op jit(solution)/shard_map/ppermute | solution.py:290
  115.3 13.5 %collective-permute-start.40 = (bf16[32,1024]{1,0:T(8,128)(2,1)S(1)}, bf16[32,1024]{1,0:T(8,128)(2,1)S(1)}, u32[]{:S(2)}, u32[]{:S(2)}) collective-permute-start(bf16[32,1024]{1,0:T(8,128)(2,1)S(1)} %get-tuple-element.30), channel_id=1, source_target_pairs={{0,12},{1,13},{2,14},{3,15},{4,8},{5,9},{6,10},{7,11},{8,4},{9,5},... | collective-permute-start | bytes 196616 | tf_op jit(solution)/shard_map/ppermute | solution.py:290
  116.3 14.8 %collective-permute-start.39 = (bf16[32,1024]{1,0:T(8,128)(2,1)S(1)}, bf16[32,1024]{1,0:T(8,128)(2,1)S(1)}, u32[]{:S(2)}, u32[]{:S(2)}) collective-permute-start(bf16[32,1024]{1,0:T(8,128)(2,1)S(1)} %get-tuple-element.31), channel_id=1, source_target_pairs={{0,10},{1,11},{2,8},{3,9},{4,14},{5,15},{6,12},{7,13},{8,2},{9,3},... | collective-permute-start | bytes 196616 | tf_op jit(solution)/shard_map/ppermute | solution.py:290
  119.4 15.1 %collective-permute-start.38 = (bf16[32,1024]{1,0:T(8,128)(2,1)S(1)}, bf16[32,1024]{1,0:T(8,128)(2,1)S(1)}, u32[]{:S(2)}, u32[]{:S(2)}) collective-permute-start(bf16[32,1024]{1,0:T(8,128)(2,1)S(1)} %get-tuple-element.32), channel_id=1, source_target_pairs={{0,8},{1,9},{2,10},{3,11},{4,12},{5,13},{6,14},{7,15},{8,0},{9,1},... | collective-permute-start | bytes 196616 | tf_op jit(solution)/shard_map/ppermute | solution.py:290
  124.7 9.8 %collective-permute-start.37 = (bf16[32,1024]{1,0:T(8,128)(2,1)S(1)}, bf16[32,1024]{1,0:T(8,128)(2,1)S(1)}, u32[]{:S(2)}, u32[]{:S(2)}) collective-permute-start(bf16[32,1024]{1,0:T(8,128)(2,1)S(1)} %get-tuple-element.33), channel_id=1, source_target_pairs={{0,6},{1,7},{2,4},{3,5},{4,2},{5,3},{6,0},{7,1},{8,14},{9,15},{10,... | collective-permute-start | bytes 196616 | tf_op jit(solution)/shard_map/ppermute | solution.py:290
  128.8 5.8 %collective-permute-start.36 = (bf16[32,1024]{1,0:T(8,128)(2,1)S(1)}, bf16[32,1024]{1,0:T(8,128)(2,1)S(1)}, u32[]{:S(2)}, u32[]{:S(2)}) collective-permute-start(bf16[32,1024]{1,0:T(8,128)(2,1)S(1)} %get-tuple-element.34), channel_id=1, source_target_pairs={{0,4},{1,5},{2,6},{3,7},{4,0},{5,1},{6,2},{7,3},{8,12},{9,13},{10,... | collective-permute-start | bytes 196616 | tf_op jit(solution)/shard_map/ppermute | solution.py:290
  128.9 5.8 %collective-permute-start.35 = (bf16[32,1024]{1,0:T(8,128)(2,1)S(1)}, bf16[32,1024]{1,0:T(8,128)(2,1)S(1)}, u32[]{:S(2)}, u32[]{:S(2)}) collective-permute-start(bf16[32,1024]{1,0:T(8,128)(2,1)S(1)} %get-tuple-element.28), channel_id=1, source_target_pairs={{0,2},{1,3},{2,0},{3,1},{4,6},{5,7},{6,4},{7,5},{8,10},{9,11},{10,... | collective-permute-start | bytes 196616 | tf_op jit(solution)/shard_map/ppermute | solution.py:290
  131.1 14.2 %collective-permute-start.27 = (bf16[64,512]{1,0:T(8,128)(2,1)S(1)}, bf16[64,512]{1,0:T(8,128)(2,1)S(1)}, u32[]{:S(2)}, u32[]{:S(2)}) collective-permute-start(bf16[64,512]{1,0:T(8,128)(2,1)S(1)} %get-tuple-element.42), channel_id=1, source_target_pairs={{0,112},{1,113},{2,114},{3,115},{4,116},{5,117},{6,118},{7,119},{8... | collective-permute-start | bytes 196616 | tf_op jit(solution)/shard_map/ppermute | solution.py:208
  135.4 13.7 %collective-permute-start.28 = (bf16[64,512]{1,0:T(8,128)(2,1)S(1)}, bf16[64,512]{1,0:T(8,128)(2,1)S(1)}, u32[]{:S(2)}, u32[]{:S(2)}) collective-permute-start(bf16[64,512]{1,0:T(8,128)(2,1)S(1)} %get-tuple-element.41), channel_id=1, source_target_pairs={{0,96},{1,97},{2,98},{3,99},{4,100},{5,101},{6,102},{7,103},{8,104... | collective-permute-start | bytes 196616 | tf_op jit(solution)/shard_map/ppermute | solution.py:208
  139.5 10.3 %collective-permute-start.29 = (bf16[64,512]{1,0:T(8,128)(2,1)S(1)}, bf16[64,512]{1,0:T(8,128)(2,1)S(1)}, u32[]{:S(2)}, u32[]{:S(2)}) collective-permute-start(bf16[64,512]{1,0:T(8,128)(2,1)S(1)} %get-tuple-element.40), channel_id=1, source_target_pairs={{0,80},{1,81},{2,82},{3,83},{4,84},{5,85},{6,86},{7,87},{8,88},{9,... | collective-permute-start | bytes 196616 | tf_op jit(solution)/shard_map/ppermute | solution.py:208
  141.6 10.4 %collective-permute-start.30 = (bf16[64,512]{1,0:T(8,128)(2,1)S(1)}, bf16[64,512]{1,0:T(8,128)(2,1)S(1)}, u32[]{:S(2)}, u32[]{:S(2)}) collective-permute-start(bf16[64,512]{1,0:T(8,128)(2,1)S(1)} %get-tuple-element.39), channel_id=1, source_target_pairs={{0,64},{1,65},{2,66},{3,67},{4,68},{5,69},{6,70},{7,71},{8,72},{9,... | collective-permute-start | bytes 196616 | tf_op jit(solution)/shard_map/ppermute | solution.py:208
  144.6 9.6 %collective-permute-start.31 = (bf16[64,512]{1,0:T(8,128)(2,1)S(1)}, bf16[64,512]{1,0:T(8,128)(2,1)S(1)}, u32[]{:S(2)}, u32[]{:S(2)}) collective-permute-start(bf16[64,512]{1,0:T(8,128)(2,1)S(1)} %get-tuple-element.38), channel_id=1, source_target_pairs={{0,48},{1,49},{2,50},{3,51},{4,52},{5,53},{6,54},{7,55},{8,56},{9,... | collective-permute-start | bytes 196616 | tf_op jit(solution)/shard_map/ppermute | solution.py:208
  145.3 8.9 %collective-permute-start.32 = (bf16[64,512]{1,0:T(8,128)(2,1)S(1)}, bf16[64,512]{1,0:T(8,128)(2,1)S(1)}, u32[]{:S(2)}, u32[]{:S(2)}) collective-permute-start(bf16[64,512]{1,0:T(8,128)(2,1)S(1)} %get-tuple-element.37), channel_id=1, source_target_pairs={{0,32},{1,33},{2,34},{3,35},{4,36},{5,37},{6,38},{7,39},{8,40},{9,... | collective-permute-start | bytes 196616 | tf_op jit(solution)/shard_map/ppermute | solution.py:208
  149.1 6.1 %collective-permute-start.33 = (bf16[64,512]{1,0:T(8,128)(2,1)S(1)}, bf16[64,512]{1,0:T(8,128)(2,1)S(1)}, u32[]{:S(2)}, u32[]{:S(2)}) collective-permute-start(bf16[64,512]{1,0:T(8,128)(2,1)S(1)} %get-tuple-element.35), channel_id=1, source_target_pairs={{0,16},{1,17},{2,18},{3,19},{4,20},{5,21},{6,22},{7,23},{8,24},{9,... | collective-permute-start | bytes 196616 | tf_op jit(solution)/shard_map/ppermute | solution.py:208
  (9 other events, 12.4 us)
Sparse Core Ops, SparseCore 0:
  56.3 48.0 all-gather.1

commit v2 on v1

--- a/solution.py
+++ b/solution.py
@@ -15,8 +15,15 @@
 SCORE_LOG2 = SCORE_SCALE * LOG2E
 NEGATIVE = -1e30
 FACTORS = (8, 4, 2, 2)
-VMEM_LIMIT = 32 * 1024 * 1024
+VMEM_LIMIT = 24 * 1024 * 1024
+VMEM_WIDE = 60 * 1024 * 1024
 STAT_ROWS = 8
+
+
+def cost(microseconds):
+    return pl.CostEstimate(
+        flops=int(1.1e9 * microseconds), bytes_accessed=1000, transcendentals=0
+    )
 
 NT = (((1,), (1,)), ((), ()))
 NN = (((1,), (0,)), ((), ()))
@@ -103,10 +110,8 @@
             + [stat_spec] * len(stat_arrays),
             out_specs=stat_spec,
         ),
-        compiler_params=pltpu.CompilerParams(vmem_limit_bytes=VMEM_LIMIT),
-        cost_estimate=pl.CostEstimate(
-            flops=16 * rows * tokens * hd, bytes_accessed=2 * tokens * hd, transcendentals=0
-        ),
+        compiler_params=pltpu.CompilerParams(vmem_limit_bytes=VMEM_WIDE),
+        cost_estimate=cost(3),
     )(lengths, row_arrays[0], key_rows, *row_arrays[1:], *stat_arrays)
 
 
@@ -151,7 +156,7 @@
         lane = lax.broadcasted_iota(jnp.int32, (rows, PAIR), 1)
         for which in range(2):
             at = which * 2 * rows
-            dq_ref[which, :, cols] = jnp.where(
+            dq_ref[which if carried else 1 - which, :, cols] = jnp.where(
                 lane < HDIM, query_grad[at : at + rows], query_grad[at + rows : at + 2 * rows]
             ).astype(dq_ref.dtype)
 
@@ -183,58 +188,191 @@
             ),
         ),
         input_output_aliases={9: 1, 10: 2} if carried else {},
+        compiler_params=pltpu.CompilerParams(vmem_limit_bytes=VMEM_WIDE),
+        cost_estimate=cost(6),
+    )(scalars, mine, theirs, *rows4, key_rows, value_rows, *carried)
+
+
+def whole(shape):
+    return pl.BlockSpec(shape, lambda i, s: (0,) * len(shape))
+
+
+def weight_kernel(chunk, part, s_ref, own_ref, peer_ref, *rest):
+    blocks, (kept_ref, given_ref), term_ref = rest[:-3], rest[-3:-1], rest[-1]
+    core, x_at = s_ref[0], s_ref[1]
+    tokens = jnp.concatenate(
+        [ref[y] for y in range(len(blocks)) for ref in (own_ref, peer_ref)], axis=0
+    )
+    term_ref[...] = dot(
+        jnp.transpose(tokens), jnp.concatenate([ref[...] for ref in blocks], axis=0), NN
+    )
+    cores = 2
+    per_z = 2 * cores * part
+    for z in range(chunk // per_z):
+        for x in range(2):
+            base = z * per_z + (x_at ^ x) * (cores * part)
+            kept_ref[x, z] = term_ref[pl.ds(pl.multiple_of(base + core * part, part), part), :]
+            given_ref[x, z] = term_ref[
+                pl.ds(pl.multiple_of(base + (1 - core) * part, part), part), :
+            ].astype(jnp.bfloat16)
+
+
+def weight_call(scalars, hidden_own, hidden_peer, blocks, nz, part, z_step):
+    ny, rows, tile = hidden_own.shape
+    features = blocks[0].shape[1]
+    chunk = z_step * 4 * part
+    hidden_spec = pl.BlockSpec((ny, rows, chunk), lambda i, s: (0, 0, i))
+    out_spec = pl.BlockSpec((2, z_step, part, features), lambda i, s: (0, i, 0, 0))
+    shape = (2, nz, part, features)
+    return pl.pallas_call(
+        functools.partial(weight_kernel, chunk, part),
+        out_shape=(
+            jax.ShapeDtypeStruct(shape, jnp.float32), jax.ShapeDtypeStruct(shape, jnp.bfloat16)
+        ),
+        grid_spec=pltpu.PrefetchScalarGridSpec(
+            num_scalar_prefetch=1,
+            grid=(nz // z_step,),
+            in_specs=[hidden_spec] * 2 + [whole(blocks[0].shape)] * ny,
+            out_specs=(out_spec, out_spec),
+            scratch_shapes=[pltpu.VMEM((chunk, features), jnp.float32)],
+        ),
         compiler_params=pltpu.CompilerParams(vmem_limit_bytes=VMEM_LIMIT),
-        cost_estimate=pl.CostEstimate(
-            flops=40 * rows * tokens * hd, bytes_accessed=4 * tokens * hd, transcendentals=0
-        ),
-    )(scalars, mine, theirs, *rows4, key_rows, value_rows, *carried)
+        cost_estimate=cost(2),
+    )(scalars, hidden_own, hidden_peer, *blocks)
+
+
+def state_kernel(rows, s_ref, w_ref, *rest):
+    blocks, (kept_ref, given_ref) = rest[:-2], rest[-2:]
+    term = dot(jnp.concatenate([ref[...] for ref in blocks], axis=0), w_ref[...], NT)
+    for y in range(len(blocks)):
+        at = y * 2 * rows
+        kept_ref[y] = term[at : at + rows]
+        given_ref[y] = term[at + rows : at + 2 * rows].astype(jnp.bfloat16)
+
+
+def state_call(scalars, w_tile, blocks, chunk):
+    ny, tile, features = len(blocks), w_tile.shape[0], w_tile.shape[1]
+    rows = blocks[0].shape[0] // 2
+    out_spec = pl.BlockSpec((ny, rows, chunk), lambda i, s: (0, 0, i))
+    shape = (ny, rows, tile)
+    return pl.pallas_call(
+        functools.partial(state_kernel, rows),
+        out_shape=(
+            jax.ShapeDtypeStruct(shape, jnp.float32), jax.ShapeDtypeStruct(shape, jnp.bfloat16)
+        ),
+        grid_spec=pltpu.PrefetchScalarGridSpec(
+            num_scalar_prefetch=1,
+            grid=(tile // chunk,),
+            in_specs=[pl.BlockSpec((chunk, features), lambda i, s: (i, 0))]
+            + [whole(blocks[0].shape)] * ny,
+            out_specs=(out_spec, out_spec),
+        ),
+        compiler_params=pltpu.CompilerParams(vmem_limit_bytes=VMEM_LIMIT),
+        cost_estimate=cost(2),
+    )(scalars, w_tile, *blocks)
+
+
+def split_kernel(nz, s_ref, in_ref, *out_refs):
+    ny = len(out_refs)
+    width = in_ref.shape[1] // (nz * ny)
+    for offset, out_ref in enumerate(out_refs):
+        owner = lax.rem(s_ref[2] + (ny - offset), ny)
+        for z in range(nz):
+            at = pl.multiple_of((z * ny + owner) * width, width)
+            out_ref[:, z * width : (z + 1) * width] = in_ref[:, pl.ds(at, width)]
+
+
+def split_call(scalars, array, nz, ny):
+    rows, width = array.shape
+    shape = (rows, width // ny)
+    return pl.pallas_call(
+        functools.partial(split_kernel, nz),
+        out_shape=[jax.ShapeDtypeStruct(shape, array.dtype)] * ny,
+        grid_spec=pltpu.PrefetchScalarGridSpec(
+            num_scalar_prefetch=1,
+            grid=(1,),
+            in_specs=[whole(array.shape)],
+            out_specs=[whole(shape)] * ny,
+        ),
+        compiler_params=pltpu.CompilerParams(vmem_limit_bytes=VMEM_LIMIT),
+        cost_estimate=cost(1),
+    )(scalars, array)
+
+
+def place_kernel(nz, s_ref, *rest):
+    blocks, out_ref = rest[:-1], rest[-1]
+    ny = len(blocks)
+    width = blocks[0].shape[1] // nz
+    for offset, block in enumerate(blocks):
+        owner = lax.rem(s_ref[2] + (ny - offset), ny)
+        for z in range(nz):
+            at = pl.multiple_of((z * ny + owner) * width, width)
+            out_ref[:, pl.ds(at, width)] = block[:, z * width : (z + 1) * width]
+
+
+def place_call(scalars, blocks, nz):
+    rows, tile = blocks[0].shape
+    shape = (rows, tile * len(blocks))
+    return pl.pallas_call(
+        functools.partial(place_kernel, nz),
+        out_shape=jax.ShapeDtypeStruct(shape, blocks[0].dtype),
+        grid_spec=pltpu.PrefetchScalarGridSpec(
+            num_scalar_prefetch=1,
+            grid=(1,),
+            in_specs=[whole((rows, tile))] * len(blocks),
+            out_specs=whole(shape),
+        ),
+        compiler_params=pltpu.CompilerParams(vmem_limit_bytes=VMEM_LIMIT),
+        cost_estimate=cost(1),
+    )(scalars, *blocks)
 
 
 def on_device(hidden, query, out_grad, attn_out, keys, values, lengths, w_query):
     nz, ny, nx, nc = FACTORS
     plane = ny * nx * nc
+    devices = nz * plane
     blk, pb = lax.axis_index("blk"), lax.axis_index("pb")
-    z_at, core = pb // plane, lax.rem(pb, nc)
-    plane_groups = [[z * plane + r for r in range(plane)] for z in range(nz)]
+    core, x_at = lax.rem(pb, nc), lax.rem(pb // nc, nx)
+    y_at = lax.rem(pb // (nx * nc), ny)
+    offsets = list(dict.fromkeys((1, ny - 1, *range(2, ny - 1))))
+    place = jnp.stack([core, x_at, y_at]).astype(jnp.int32)
+    z_groups = [[z * plane + r for z in range(nz)] for r in range(plane)]
 
     def other_blk(x):
         return lax.ppermute(x, "blk", [(0, 1), (1, 0)])
 
     def other_core(x):
-        return lax.ppermute(x, "pb", [(i, i ^ 1) for i in range(nz * plane)])
-
-    def from_z(x, offset):
-        total = nz * plane
-        return lax.ppermute(
-            x, "pb", [(i, (i - offset * plane) % total) for i in range(total)]
-        )
+        return lax.ppermute(x, "pb", [(i, i ^ 1) for i in range(devices)])
+
+    def other_x(x):
+        return lax.ppermute(x, "pb", [(i, i ^ nc) for i in range(devices)])
+
+    def from_y(x, offset):
+        step = nx * nc
+        def target(i):
+            y = i // step % ny
+            return i + ((y - offset) % ny - y) * step
+        return lax.ppermute(x, "pb", [(i, target(i)) for i in range(devices)])
 
     tokens = keys.shape[1] * keys.shape[2]
     passages, passage_len = keys.shape[1], keys.shape[2]
     hd = keys.shape[3]
     rows, width = hidden.shape[1], hidden.shape[2]
+    part = w_query.shape[0]
     key_rows, value_rows = keys.reshape(tokens, hd), values.reshape(tokens, hd)
     q_own, g_own, o_own = query[0], out_grad[0], attn_out[0]
 
     q_peer = other_blk(q_own)
     g_peer = other_blk(g_own)
 
-    w_tile = lax.all_gather(w_query, "pb", axis=0, tiled=True, axis_index_groups=plane_groups)
-    tile = width // nz
-
-    q_peer, hidden_rows = lax.optimization_barrier((q_peer, hidden[0]))
-
-    def column_block(offset):
-        at = lax.rem(z_at + (nz - offset), nz) * tile
-        return lax.dynamic_slice_in_dim(hidden_rows, at, tile, axis=1)
-
-    hidden_own = jnp.stack(
-        [column_block(0)] + [from_z(column_block(s), s) for s in range(1, nz)], axis=0
-    )
-    hidden_peer = other_blk(hidden_own)
-    hidden_t = jnp.transpose(
-        jnp.concatenate([hidden_own, hidden_peer], axis=1).reshape(nz * 2 * rows, tile)
-    )
+    def in_order(first, mine, other):
+        return jnp.where(
+            first, jnp.concatenate([mine, other], axis=0), jnp.concatenate([other, mine], axis=0)
+        )
+
+    w_pair = in_order(core == 0, w_query, other_core(w_query))
+    w_near = in_order(x_at == 0, w_pair, other_x(w_pair))
+    w_tile = lax.all_gather(w_near, "pb", axis=0, tiled=True, axis_index_groups=z_groups)
 
     lens = lengths[0]
     stat_pairs = min(4, hd // PAIR)
@@ -246,6 +384,11 @@
     )
     theirs = other_blk(mine)
 
+    place, _ = lax.optimization_barrier((place, stats_own))
+    shares = split_call(place, hidden[0], nz, ny)
+    hidden_own = jnp.stack([shares[0]] + [from_y(shares[s], s) for s in offsets], axis=0)
+    theirs, hidden_own = lax.optimization_barrier((theirs, hidden_own))
+
     rows4 = [q_own, q_peer, g_own, g_peer]
     grad_pairs = min(2, hd // PAIR // 2)
 
@@ -257,50 +400,29 @@
     dq_send, key_part, value_part = half_grad(1 - blk, (), jnp.bfloat16)
     dq_here, key_grad, value_grad = half_grad(blk, (key_part, value_part), jnp.float32)
     dq_there = other_blk(dq_send)
-    qg_own = (dq_here[0] + dq_there[1].astype(jnp.float32)).astype(jnp.bfloat16)
-    qg_peer = (dq_here[1] + dq_there[0].astype(jnp.float32)).astype(jnp.bfloat16)
-
-    qg_own, qg_peer, hidden_t = lax.optimization_barrier((qg_own, qg_peer, hidden_t))
-
-    blocks = [[None] * nz, [None] * nz]
-    for part, start in enumerate((qg_own, qg_peer)):
-        blocks[part][0] = start
-    ups, downs = (nz // 2, nz - 1 - nz // 2), (nz - 1 - nz // 2, nz // 2)
-    for step in range(1, nz // 2 + 1):
-        for part in range(2):
-            if step <= ups[part]:
-                blocks[part][step] = from_z(blocks[part][step - 1], 1)
-            if step <= downs[part]:
-                blocks[part][nz - step] = from_z(blocks[part][(nz - step + 1) % nz], -1)
-    qg_all = jnp.concatenate([blocks[part][s] for s in range(nz) for part in range(2)], axis=0)
-
-    w_term = lax.dot_general(hidden_t, qg_all, NN, preferred_element_type=jnp.float32)
-    state_term = lax.dot_general(qg_all, w_tile, NT, preferred_element_type=jnp.float32)
-
-    w_term = w_term.reshape(ny * nx, nc, -1, w_term.shape[1])
-    kept = lax.dynamic_index_in_dim(w_term, core, axis=1, keepdims=False)
-    given = lax.dynamic_index_in_dim(w_term, 1 - core, axis=1, keepdims=False)
-    w_sum = (kept + other_core(given)).astype(jnp.bfloat16)
-    plane_at = lax.rem(pb, plane) // nc
-
-    def across_plane(flip):
-        block = lax.dynamic_index_in_dim(w_sum, plane_at ^ flip, axis=0, keepdims=False)
-        if flip == 0:
-            return block
-        return lax.ppermute(block, "pb", [(i, i ^ (flip * nc)) for i in range(nz * plane)])
-
-    w_query_grad = sum(across_plane(flip).astype(jnp.float32) for flip in range(ny * nx))
-
-    state_term = state_term.reshape(nz, 2, rows, tile)
-    state_sum = state_term[:, 0] + other_blk(state_term[:, 1].astype(jnp.bfloat16)).astype(
-        jnp.float32
-    )
-    state_sum = state_sum.astype(jnp.bfloat16)
-    arrived = [state_sum[0]] + [from_z(state_sum[nz - s], s) for s in range(1, nz)]
-    state_all = lax.dynamic_slice_in_dim(
-        jnp.stack(arrived + arrived, axis=0), lax.rem(nz - z_at, nz), nz, axis=0
-    )
-    hidden_grad = jnp.transpose(state_all, (1, 0, 2)).reshape(hidden.shape)
+    dq_there, dq_here, hidden_own = lax.optimization_barrier((dq_there, dq_here, hidden_own))
+    hidden_peer = other_blk(hidden_own)
+    qg = (dq_here + dq_there.astype(jnp.float32)).astype(jnp.bfloat16)
+    qg = qg.reshape(2 * rows, hd // 2)
+
+    blocks = [qg] + [from_y(qg, s) for s in offsets]
+
+    w_kept, w_given = weight_call(place, hidden_own, hidden_peer, blocks, nz, part, max(nz // 4, 1))
+    w_other = other_core(w_given)
+    w_send = (w_kept[1] + w_other[1].astype(jnp.float32)).astype(jnp.bfloat16)
+    w_sum = (w_kept[0] + w_other[0].astype(jnp.float32)) + other_x(w_send).astype(jnp.float32)
+    w_parts = lax.all_to_all(
+        w_sum.astype(jnp.bfloat16), "pb", split_axis=0, concat_axis=0, tiled=True,
+        axis_index_groups=z_groups,
+    )
+    w_query_grad = jnp.sum(w_parts.astype(jnp.float32), axis=0)
+
+    state_kept, state_given = state_call(place, w_tile, blocks, w_tile.shape[0] // 4)
+    state_sum = (state_kept + other_blk(state_given).astype(jnp.float32)).astype(jnp.bfloat16)
+    back = [state_sum[0]] + [None] * (ny - 1)
+    for at, offset in enumerate(offsets):
+        back[offset] = from_y(state_sum[at + 1], -offset)
+    hidden_grad = place_call(place, back, nz).reshape(hidden.shape)
     return (hidden_grad, key_grad.reshape(keys.shape), value_grad.reshape(values.shape),
             w_query_grad)
 

time: 165 us -> 132 us (0.80)
  starting transfers between devices: 72.3 us -> 33.3 us
  Pallas kernels: 18.4 us -> 33.3 us
  local copies, waits for them, and re-layouts: 15.9 us -> 6.94 us
  matrix products: 4.4 us -> 0 us
  waiting for transfers between devices: 32.3 us -> 35.4 us
  other arithmetic: 5.83 us -> 7.72 us
    ppermute x36 -> x13, starting transfers between devices: 64.3 us -> 16.8 us  [the longest x9 13.8 us: from_y(): return lax.ppermute(x, 'pb', [(i, target(i)) for i in range(devices)])]
    all_to_all x0 -> x1, waiting for transfers between devices: none -> 10.9 us  [on_device(): lax.all_to_all(w_sum.astype(jnp.bfloat16), 'pb', split_axis=0, concat_axi...]
    pallas_call x0 -> x4, Pallas kernels: none -> 8.52 us  [the longest x1 3.32 us: state_call(): pl.pallas_call(functools.partial(state_kernel, rows), out_shape=(jax.Shap...]
    all_to_all x0 -> x1, starting transfers between devices: none -> 8.48 us  [on_device(): lax.all_to_all(w_sum.astype(jnp.bfloat16), 'pb', split_axis=0, concat_axi...]
    unnamed x64 -> x30, local copies, waits for them, and re-layouts: 12.8 us -> 6.9 us
    pallas_call x2, Pallas kernels: 5.75 us -> 10.2 us  [stats_call(): pl.pallas_call(functools.partial(kernel, pairs, passage_len, lengths.shap...]
    dot_general x2 -> x0, matrix products: 4.4 us -> none  [the longest x1 3.14 us: on_device(): lax.dot_general(qg_all, w_tile, NT, preferred_element_type=jnp.float32)]
    all_gather x1, waiting for transfers between devices: 3.45 us -> 0.01 us  [on_device(): lax.all_gather(w_near, 'pb', axis=0, tiled=True, axis_index_groups=z_groups)]
  transfers between devices with their start and end apart: 43 -> 21, of which waited for: 19 -> 7; matrix products, arithmetic and copies ran while one was open for 10% -> 6% of each run, Pallas kernels for 11% -> 24%
where the time goes in v2:
time: 132 us; the launch traced here: 131 us
  waiting for transfers between devices  35.4 us (27%)
  starting transfers between devices  33.3 us (25%)
  Pallas kernels  33.3 us (25%)
  between operations  14.2 us (11%)
  other arithmetic  7.72 us (6%)
  local copies, waits for them, and re-layouts  6.94 us (5%)
    pallas_call x2, Pallas kernels, grad_call(): pl.pallas_call(functools.partial(grad_kernel, pairs, passage_len, passage...  14.5 us
    ppermute x9, starting transfers between devices, from_y(): return lax.ppermute(x, 'pb', [(i, target(i)) for i in range(devices)])  13.8 us
    all_to_all x1, waiting for transfers between devices, on_device(): lax.all_to_all(w_sum.astype(jnp.bfloat16), 'pb', split_axis=0, concat_axi...  10.9 us
    pallas_call x2, Pallas kernels, stats_call(): pl.pallas_call(functools.partial(kernel, pairs, passage_len, lengths.shap...  10.2 us
    ppermute x2, waiting for transfers between devices, other_x(): return lax.ppermute(x, 'pb', [(i, i ^ nc) for i in range(devices)])  9.86 us
    ppermute x9, waiting for transfers between devices, from_y(): return lax.ppermute(x, 'pb', [(i, target(i)) for i in range(devices)])  9.36 us
    all_to_all x1, starting transfers between devices, on_device(): lax.all_to_all(w_sum.astype(jnp.bfloat16), 'pb', split_axis=0, concat_axi...  8.48 us
    ppermute x6, starting transfers between devices, other_blk(): return lax.ppermute(x, 'blk', [(0, 1), (1, 0)])  7.96 us
  transfers between devices with their start and end apart: 21, of which 7 were waited for; matrix products, arithmetic and copies ran while one was open for 6% of the time, Pallas kernels for 24%

profile of v2, /device:TPU:2, one launch (start us, length us, event | category | flops | bytes accessed | tf_op | source)
XLA Modules:
  0.0 130.7 jit_solution(7537172904512533987)
XLA Ops:
  7.2 2.4 %collective-permute-start.2 = (bf16[64,2048]{1,0:T(8,128)(2,1)}, bf16[64,2048]{1,0:T(8,128)(2,1)S(1)}, u32[]{:S(2)}, u32[]{:S(2)}) collective-permute-start(bf16[64,2048]{1,0:T(8,128)(2,1)} %bitcast.54), channel_id=1, source_target_pairs={{0,128},{128,0},{1,129},{129,1},{2,130},{130,2},{3,131},{131,3},{4... | collective-permute-start | bytes 786440 | tf_op jit(solution)/shard_map/ppermute | solution.py:342
  9.6 0.1 collective-permute-start.7
  9.7 5.2 %shard_map.111.own_ref = f32[16,8,128]{2,1,0:T(8,128)} custom-call(s32[2]{0:T(128)} %bitcast.44, bf16[64,2048]{1,0:T(8,128)(2,1)} %bitcast.55, bf16[512,2048]{1,0:T(8,128)(2,1)} %bitcast.47, bf16[64,2048]{1,0:T(8,128)(2,1)} %bitcast.59, bf16[64,2048]{1,0:T(8,128)(2,1)} %bitcast.53), custom_call_target="tpu_custom_call" | custom-call | flops 3300000000 | bytes 1000 | tf_op jit(solution)/shard_map/pallas_call | solution.py:102
  14.9 0.1 pad_add_fusion.s_ref
  15.0 1.9 %collective-permute-start.1 = (bf16[64,1024]{1,0:T(8,128)(2,1)S(1)}, bf16[64,1024]{1,0:T(8,128)(2,1)S(1)}, u32[]{:S(2)}, u32[]{:S(2)}) collective-permute-start(bf16[64,1024]{1,0:T(8,128)(2,1)S(1)} %maximum_select_fusion.1), channel_id=1, source_target_pairs={{0,2},{1,3},{2,0},{3,1},{4,6},{5,7},{6,4},{7,5},{8,10},{9,11},{10,... | collective-permute-start | bytes 393224 | tf_op jit(solution)/shard_map/ppermute | solution.py:348
  16.9 0.7 shard_map.113
  17.6 3.1 %collective-permute-start.4 = (bf16[64,1024]{1,0:T(8,128)(2,1)S(1)}, bf16[64,1024]{1,0:T(8,128)(2,1)S(1)}, u32[]{:S(2)}, u32[]{:S(2)}) collective-permute-start(bf16[64,1024]{1,0:T(8,128)(2,1)S(1)} %get-tuple-element.26), channel_id=1, source_target_pairs={{0,12},{1,13},{2,14},{3,15},{4,0},{5,1},{6,2},{7,3},{8,4},{9,5},{1... | collective-permute-start | bytes 393224 | tf_op jit(solution)/shard_map/ppermute | solution.py:355
  20.7 0.7 pad_add_fusion.2
  21.4 3.5 %collective-permute-done.1 = bf16[64,1024]{1,0:T(8,128)(2,1)S(1)} collective-permute-done((bf16[64,1024]{1,0:T(8,128)(2,1)S(1)}, bf16[64,1024]{1,0:T(8,128)(2,1)S(1)}, u32[]{:S(2)}, u32[]{:S(2)}) %collective-permute-start.1) | collective-permute-done | bytes 131104 | tf_op jit(solution)/shard_map/ppermute | solution.py:348
  24.9 3.2 %collective-permute-start.6 = (bf16[64,1024]{1,0:T(8,128)(2,1)S(1)}, bf16[64,1024]{1,0:T(8,128)(2,1)S(1)}, u32[]{:S(2)}, u32[]{:S(2)}) collective-permute-start(bf16[64,1024]{1,0:T(8,128)(2,1)S(1)} %get-tuple-element.28), channel_id=1, source_target_pairs={{0,8},{1,9},{2,10},{3,11},{4,12},{5,13},{6,14},{7,15},{8,0},{9,1},... | collective-permute-start | bytes 393224 | tf_op jit(solution)/shard_map/ppermute | solution.py:355
  28.1 0.8 maximum_select_fusion
  28.9 0.7 copy-done.12
  29.6 5.0 %shard_map.112.mine_ref = f32[16,8,128]{2,1,0:T(8,128)} custom-call(s32[2]{0:T(128)} %bitcast.45, bf16[64,2048]{1,0:T(8,128)(2,1)} %copy-done.12, bf16[512,2048]{1,0:T(8,128)(2,1)} %bitcast.48, f32[16,8,128]{2,1,0:T(8,128)} %shard_map.111.own_ref), custom_call_target="tpu_custom_call" | custom-call | flops 3300000000 | bytes 1000 | tf_op jit(solution)/shard_map/pallas_call | solution.py:102
  34.6 1.8 %collective-permute-start.3 = (f32[16,8,128]{2,1,0:T(8,128)}, f32[16,8,128]{2,1,0:T(8,128)S(1)}, u32[]{:S(2)}, u32[]{:S(2)}) collective-permute-start(f32[16,8,128]{2,1,0:T(8,128)} %shard_map.112.mine_ref), channel_id=1, source_target_pairs={{0,128},{128,0},{1,129},{129,1},{2,130},{130,2},{3,131},{131,3},{4... | collective-permute-start | bytes 196616 | tf_op jit(solution)/shard_map/ppermute | solution.py:342
  36.5 2.6 %collective-permute-done.3.theirs_ref = f32[16,8,128]{2,1,0:T(8,128)S(1)} collective-permute-done((f32[16,8,128]{2,1,0:T(8,128)}, f32[16,8,128]{2,1,0:T(8,128)S(1)}, u32[]{:S(2)}, u32[]{:S(2)}) %collective-permute-start.3) | collective-permute-done | bytes 65568 | tf_op jit(solution)/shard_map/ppermute | solution.py:342
  39.1 0.6 copy-done.14
  39.7 0.1 copy-done.13
  39.8 7.2 %shard_map.114 = (bf16[2,64,1024]{2,1,0:T(8,128)(2,1)}, bf16[512,2048]{1,0:T(8,128)(2,1)}, bf16[512,2048]{1,0:T(8,128)(2,1)}) custom-call(s32[3]{0:T(128)} %get-tuple-element.49.s_ref, f32[16,8,128]{2,1,0:T(8,128)} %shard_map.112.mine_ref, f32[16,8,128]{2,1,0:T(8,128)} %copy-done.14, bf16[64,2048]{1,0:T(8,128)(2,1)} %bitcast.56, ...), custom_call_target="tpu_custom_call" | custom-call | flops 6600000000 | bytes 1000 | tf_op jit(solution)/shard_map/pallas_call | solution.py:178
  47.1 1.9 %collective-permute-start.8 = (bf16[2,64,1024]{2,1,0:T(8,128)(2,1)}, bf16[2,64,1024]{2,1,0:T(8,128)(2,1)S(1)}, u32[]{:S(2)}, u32[]{:S(2)}) collective-permute-start(bf16[2,64,1024]{2,1,0:T(8,128)(2,1)} %get-tuple-element.30), channel_id=1, source_target_pairs={{0,128},{128,0},{1,129},{129,1},{2,130},{130,2},{3,131},{131,3},{4... | collective-permute-start | bytes 786440 | tf_op jit(solution)/shard_map/ppermute | solution.py:342
  49.0 7.3 %shard_map.115 = (f32[2,64,1024]{2,1,0:T(8,128)}, bf16[512,2048]{1,0:T(8,128)(2,1)}, bf16[512,2048]{1,0:T(8,128)(2,1)}) custom-call(s32[3]{0:T(128)} %get-tuple-element.48.s_ref, f32[16,8,128]{2,1,0:T(8,128)} %shard_map.112.mine_ref, f32[16,8,128]{2,1,0:T(8,128)} %copy-done.14, ...), custom_call_target="tpu_custom_call", output_to_operand_aliasing={{1}: (9, {}), {2}: (10, {})} | custom-call | flops 6600000000 | bytes 1000 | tf_op jit(solution)/shard_map/pallas_call | solution.py:178
  56.2 0.3 collective-permute-start.16
  56.5 1.1 add_convert_fusion.2
  57.7 0.8 collective-permute-start.10
  58.4 1.8 %collective-permute-start.11 = (bf16[128,1024]{1,0:T(8,128)(2,1)S(1)}, bf16[128,1024]{1,0:T(8,128)(2,1)S(1)}, u32[]{:S(2)}, u32[]{:S(2)}) collective-permute-start(bf16[128,1024]{1,0:T(8,128)(2,1)S(1)} %bitcast.35), channel_id=1, source_target_pairs={{0,8},{1,9},{2,10},{3,11},{4,12},{5,13},{6,14},{7,15},{8,0},{9,1},... | collective-permute-start | bytes 786440 | tf_op jit(solution)/shard_map/ppermute | solution.py:355
  60.2 0.9 collective-permute-start.9
  61.2 8.7 %collective-permute-done.10.rest_2_ = bf16[128,1024]{1,0:T(8,128)(2,1)S(1)} collective-permute-done((bf16[128,1024]{1,0:T(8,128)(2,1)S(1)}, bf16[128,1024]{1,0:T(8,128)(2,1)S(1)}, u32[]{:S(2)}, u32[]{:S(2)}) %collective-permute-start.10) | collective-permute-done | bytes 262176 | tf_op jit(solution)/shard_map/ppermute | solution.py:355
  69.9 0.7 collective-permute-done.9.rest_1_
  70.5 3.1 %shard_map.118 = (f32[2,8,32,1024]{3,2,1,0:T(8,128)S(1)}, bf16[2,8,32,1024]{3,2,1,0:T(8,128)(2,1)S(1)}) custom-call(s32[3]{0:T(128)S(1)} %pad_add_fusion.s_ref, bf16[4,64,1024]{2,1,0:T(8,128)(2,1)S(1)} %pad_maximum_fusion.own_ref, bf16[4,64,1024]{2,1,0:T(8,128)(2,1)S(1)} %collective-permute-done.16.peer_ref, bf16[128,1024]{1,0:T(8,128)(2,1)S(1)} %bitcast.37, ...), custom_call_target="tpu_custom_call" | custom-call | flops 2200000000 | bytes 1000 | tf_op jit(solution)/shard_map/pallas_call | solution.py:227
  73.7 0.1 collective-permute-start.17
  73.8 2.6 %collective-permute-done.17 = bf16[2,8,32,1024]{3,2,1,0:T(8,128)(2,1)S(1)} collective-permute-done((bf16[2,8,32,1024]{3,2,1,0:T(8,128)(2,1)S(1)}, bf16[2,8,32,1024]{3,2,1,0:T(8,128)(2,1)S(1)}, u32[]{:S(2)}, u32[]{:S(2)}) %collective-permute-start.17) | collective-permute-done | bytes 1048608 | tf_op jit(solution)/shard_map/ppermute | solution.py:345
  76.4 1.0 copy-done.8
  77.4 1.0 fusion.1
  78.3 1.0 collective-permute-start.18
  79.4 1.6 %copy-done = bf16[1024,1024]{1,0:T(8,128)(2,1)S(1)} copy-done((bf16[1024,1024]{1,0:T(8,128)(2,1)S(1)}, bf16[1024,1024]{1,0:T(8,128)(2,1)}, u32[]{:S(2)}) %copy-start) | copy-done | bytes 2097176
  80.9 0.9 copy-done.3
  81.9 0.9 copy-done.5
  82.8 0.9 copy-done.7
  83.8 3.3 %shard_map.116 = (f32[4,64,1024]{2,1,0:T(8,128)S(1)}, bf16[4,64,1024]{2,1,0:T(8,128)(2,1)}) custom-call(s32[3]{0:T(128)S(1)} %pad_add_fusion.s_ref, bf16[1024,1024]{1,0:T(8,128)(2,1)S(1)} %copy-done, bf16[128,1024]{1,0:T(8,128)(2,1)S(1)} %bitcast.38, bf16[128,1024]{1,0:T(8,128)(2,1)S(1)} %copy-done.7, bf16[128,1024]{1,0:T(8,128)(2,1)S(1)} %copy-done.3, ...), custom_call_target="tpu_custom_call" | custom-call | flops 2200000000 | bytes 1000 | tf_op jit(solution)/shard_map/pallas_call | solution.py:258
  87.1 1.5 %collective-permute-start.12 = (bf16[4,64,1024]{2,1,0:T(8,128)(2,1)}, bf16[4,64,1024]{2,1,0:T(8,128)(2,1)}, u32[]{:S(2)}, u32[]{:S(2)}) collective-permute-start(bf16[4,64,1024]{2,1,0:T(8,128)(2,1)} %get-tuple-element.38), channel_id=1, source_target_pairs={{0,128},{128,0},{1,129},{129,1},{2,130},{130,2},{3,131},{131,3},{4... | collective-permute-start | bytes 1572872 | tf_op jit(solution)/shard_map/ppermute | solution.py:342
  88.6 6.3 %collective-permute-done.18 = bf16[8,32,1024]{2,1,0:T(8,128)(2,1)} collective-permute-done((bf16[8,32,1024]{2,1,0:T(8,128)(2,1)}, bf16[8,32,1024]{2,1,0:T(8,128)(2,1)}, u32[]{:S(2)}, u32[]{:S(2)}) %collective-permute-start.18) | collective-permute-done | bytes 524320 | tf_op jit(solution)/shard_map/ppermute | solution.py:348
  94.9 2.1 %fusion = bf16[8,32,1024]{2,1,0:T(8,128)(2,1)} fusion(bf16[8,32,1024]{2,1,0:T(8,128)(2,1)} %collective-permute-done.18, f32[2,8,32,1024]{3,2,1,0:T(8,128)S(1)} %get-tuple-element.42, bf16[2,8,32,1024]{3,2,1,0:T(8,128)(2,1)S(1)} %copy-done.9), kind=kLoop, calls=%fused_computation.1 | loop fusion | flops 1310720 | bytes 2621440 | tf_op jit(solution)/shard_map/convert_element_type | solution.py:415
  97.1 8.5 %all-to-all-start = ((bf16[8,32,1024]{2,1,0:T(8,128)(2,1)}), bf16[8,32,1024]{2,1,0:T(8,128)(2,1)S(1)}, u32[]{:S(2)}, u32[]{:S(2)}) async-start(bf16[8,32,1024]{2,1,0:T(8,128)(2,1)} %fusion), calls=%async_computation | async-start | bytes 1048576 | tf_op jit(solution)/shard_map/all_to_all | solution.py:414
  105.5 1.2 add_convert_fusion.1
  106.8 0.4 collective-permute-start.13
  107.2 3.6 %collective-permute-start.14 = (bf16[64,1024]{1,0:T(8,128)(2,1)S(1)}, bf16[64,1024]{1,0:T(8,128)(2,1)S(1)}, u32[]{:S(2)}, u32[]{:S(2)}) collective-permute-start(bf16[64,1024]{1,0:T(8,128)(2,1)S(1)} %get-tuple-element.45), channel_id=1, source_target_pairs={{0,8},{1,9},{2,10},{3,11},{4,12},{5,13},{6,14},{7,15},{8,0},{9,1},... | collective-permute-start | bytes 393224 | tf_op jit(solution)/shard_map/ppermute | solution.py:355
  110.8 10.9 %all-to-all-done = bf16[8,32,1024]{2,1,0:T(8,128)(2,1)S(1)} async-done(((bf16[8,32,1024]{2,1,0:T(8,128)(2,1)}), bf16[8,32,1024]{2,1,0:T(8,128)(2,1)S(1)}, u32[]{:S(2)}, u32[]{:S(2)}) %all-to-all-start) | async-done | bytes 524320 | tf_op jit(solution)/shard_map/all_to_all | solution.py:414
  121.7 0.7 convert_reduce_fusion
  122.5 1.4 %shard_map.117 = bf16[64,4096]{1,0:T(8,128)(2,1)} custom-call(s32[3]{0:T(128)S(1)} %pad_add_fusion.s_ref, bf16[64,1024]{1,0:T(8,128)(2,1)S(1)} %get-tuple-element.47.rest_0_, bf16[64,1024]{1,0:T(8,128)(2,1)S(1)} %collective-permute-done.13.rest_1_, bf16[64,1024]{1,0:T(8,128)(2,1)S(1)} %collective-permute-done.14.rest_2_, ...), custom_call_target="tpu_custom_call" | custom-call | flops 1100000000 | bytes 1000 | tf_op jit(solution)/shard_map/pallas_call | solution.py:316
  (44 shorter events, 0.3 us)
Async XLA Ops:
  7.2 72.2 %all-gather.2.cloned.1.call-start = ((), (), s32[]{:S(2)}) async-start(), calls=%async_computation.1 | async-start | bytes 2359296 | tf_op jit(solution)/shard_map/all_gather | solution.py:375
  7.2 21.7 %collective-permute-start.2 = (bf16[64,2048]{1,0:T(8,128)(2,1)}, bf16[64,2048]{1,0:T(8,128)(2,1)S(1)}, u32[]{:S(2)}, u32[]{:S(2)}) collective-permute-start(bf16[64,2048]{1,0:T(8,128)(2,1)} %bitcast.54), channel_id=1, source_target_pairs={{0,128},{128,0},{1,129},{129,1},{2,130},{130,2},{3,131},{131,3},{4... | collective-permute-start | bytes 786440 | tf_op jit(solution)/shard_map/ppermute | solution.py:342
  9.6 29.5 %collective-permute-start.7 = (bf16[64,2048]{1,0:T(8,128)(2,1)}, bf16[64,2048]{1,0:T(8,128)(2,1)S(1)}, u32[]{:S(2)}, u32[]{:S(2)}) collective-permute-start(bf16[64,2048]{1,0:T(8,128)(2,1)} %bitcast.58), channel_id=1, source_target_pairs={{0,128},{128,0},{1,129},{129,1},{2,130},{130,2},{3,131},{131,3},{4... | collective-permute-start | bytes 786440 | tf_op jit(solution)/shard_map/ppermute | solution.py:342
  9.7 5.3 %collective-permute-start = (bf16[32,1024]{1,0:T(8,128)(2,1)}, bf16[32,1024]{1,0:T(8,128)(2,1)S(1)}, u32[]{:S(2)}, u32[]{:S(2)}) collective-permute-start(bf16[32,1024]{1,0:T(8,128)(2,1)} %param.15), channel_id=1, source_target_pairs={{0,1},{1,0},{2,3},{3,2},{4,5},{5,4},{6,7},{7,6},{8,9},{9,8},{10,11... | collective-permute-start | bytes 196616 | tf_op jit(solution)/shard_map/ppermute | solution.py:345
  9.7 5.3 %copy-start.10 = (bf16[32,1024]{1,0:T(8,128)(2,1)S(1)}, bf16[32,1024]{1,0:T(8,128)(2,1)}, u32[]{:S(2)}) copy-start(bf16[32,1024]{1,0:T(8,128)(2,1)} %param.15) | copy-start | bytes 196612
  9.7 7.2 %copy-start.1 = (bf16[1,64,4096]{2,1,0:T(8,128)(2,1)S(1)}, bf16[1,64,4096]{2,1,0:T(8,128)(2,1)}, u32[]{:S(2)}) copy-start(bf16[1,64,4096]{2,1,0:T(8,128)(2,1)} %param.8) | copy-start | bytes 1572868
  15.0 5.7 %copy-start.11 = (s32[1,2]{1,0:T(1,128)S(1)}, s32[1,2]{1,0:T(1,128)}, u32[]{:S(2)}) copy-start(s32[1,2]{1,0:T(1,128)} %param.14) | copy-start | bytes 28
  15.0 9.9 %collective-permute-start.1 = (bf16[64,1024]{1,0:T(8,128)(2,1)S(1)}, bf16[64,1024]{1,0:T(8,128)(2,1)S(1)}, u32[]{:S(2)}, u32[]{:S(2)}) collective-permute-start(bf16[64,1024]{1,0:T(8,128)(2,1)S(1)} %maximum_select_fusion.1), channel_id=1, source_target_pairs={{0,2},{1,3},{2,0},{3,1},{4,6},{5,7},{6,4},{7,5},{8,10},{9,11},{10,... | collective-permute-start | bytes 393224 | tf_op jit(solution)/shard_map/ppermute | solution.py:348
  17.6 18.8 %collective-permute-start.4 = (bf16[64,1024]{1,0:T(8,128)(2,1)S(1)}, bf16[64,1024]{1,0:T(8,128)(2,1)S(1)}, u32[]{:S(2)}, u32[]{:S(2)}) collective-permute-start(bf16[64,1024]{1,0:T(8,128)(2,1)S(1)} %get-tuple-element.26), channel_id=1, source_target_pairs={{0,12},{1,13},{2,14},{3,15},{4,0},{5,1},{6,2},{7,3},{8,4},{9,5},{1... | collective-permute-start | bytes 393224 | tf_op jit(solution)/shard_map/ppermute | solution.py:355
  20.7 15.7 %collective-permute-start.5 = (bf16[64,1024]{1,0:T(8,128)(2,1)S(1)}, bf16[64,1024]{1,0:T(8,128)(2,1)S(1)}, u32[]{:S(2)}, u32[]{:S(2)}) collective-permute-start(bf16[64,1024]{1,0:T(8,128)(2,1)S(1)} %get-tuple-element.27), channel_id=1, source_target_pairs={{0,4},{1,5},{2,6},{3,7},{4,8},{5,9},{6,10},{7,11},{8,12},{9,13},{1... | collective-permute-start | bytes 393224 | tf_op jit(solution)/shard_map/ppermute | solution.py:355
  24.9 11.5 %collective-permute-start.6 = (bf16[64,1024]{1,0:T(8,128)(2,1)S(1)}, bf16[64,1024]{1,0:T(8,128)(2,1)S(1)}, u32[]{:S(2)}, u32[]{:S(2)}) collective-permute-start(bf16[64,1024]{1,0:T(8,128)(2,1)S(1)} %get-tuple-element.28), channel_id=1, source_target_pairs={{0,8},{1,9},{2,10},{3,11},{4,12},{5,13},{6,14},{7,15},{8,0},{9,1},... | collective-permute-start | bytes 393224 | tf_op jit(solution)/shard_map/ppermute | solution.py:355
  28.9 0.7 copy-start.12
  34.6 4.5 %collective-permute-start.3 = (f32[16,8,128]{2,1,0:T(8,128)}, f32[16,8,128]{2,1,0:T(8,128)S(1)}, u32[]{:S(2)}, u32[]{:S(2)}) collective-permute-start(f32[16,8,128]{2,1,0:T(8,128)} %shard_map.112.mine_ref), channel_id=1, source_target_pairs={{0,128},{128,0},{1,129},{129,1},{2,130},{130,2},{3,131},{131,3},{4... | collective-permute-start | bytes 196616 | tf_op jit(solution)/shard_map/ppermute | solution.py:342
  39.1 0.6 copy-start.14
  39.1 0.7 copy-start.13
  47.1 9.2 %collective-permute-start.8 = (bf16[2,64,1024]{2,1,0:T(8,128)(2,1)}, bf16[2,64,1024]{2,1,0:T(8,128)(2,1)S(1)}, u32[]{:S(2)}, u32[]{:S(2)}) collective-permute-start(bf16[2,64,1024]{2,1,0:T(8,128)(2,1)} %get-tuple-element.30), channel_id=1, source_target_pairs={{0,128},{128,0},{1,129},{129,1},{2,130},{130,2},{3,131},{131,3},{4... | collective-permute-start | bytes 786440 | tf_op jit(solution)/shard_map/ppermute | solution.py:342
  56.2 14.3 %collective-permute-start.16 = (bf16[4,64,1024]{2,1,0:T(8,128)(2,1)S(1)}, bf16[4,64,1024]{2,1,0:T(8,128)(2,1)S(1)}, u32[]{:S(2)}, u32[]{:S(2)}) collective-permute-start(bf16[4,64,1024]{2,1,0:T(8,128)(2,1)S(1)} %pad_maximum_fusion.own_ref), channel_id=1, source_target_pairs={{0,128},{128,0},{1,129},{129,1},{2,130},{130,2},{3,131},{131,3},{4... | collective-permute-start | bytes 1572872 | tf_op jit(solution)/shard_map/ppermute | solution.py:342
  57.7 12.2 %collective-permute-start.10 = (bf16[128,1024]{1,0:T(8,128)(2,1)S(1)}, bf16[128,1024]{1,0:T(8,128)(2,1)S(1)}, u32[]{:S(2)}, u32[]{:S(2)}) collective-permute-start(bf16[128,1024]{1,0:T(8,128)(2,1)S(1)} %bitcast.34), channel_id=1, source_target_pairs={{0,4},{1,5},{2,6},{3,7},{4,8},{5,9},{6,10},{7,11},{8,12},{9,13},{1... | collective-permute-start | bytes 786440 | tf_op jit(solution)/shard_map/ppermute | solution.py:355
  58.4 11.5 %collective-permute-start.11 = (bf16[128,1024]{1,0:T(8,128)(2,1)S(1)}, bf16[128,1024]{1,0:T(8,128)(2,1)S(1)}, u32[]{:S(2)}, u32[]{:S(2)}) collective-permute-start(bf16[128,1024]{1,0:T(8,128)(2,1)S(1)} %bitcast.35), channel_id=1, source_target_pairs={{0,8},{1,9},{2,10},{3,11},{4,12},{5,13},{6,14},{7,15},{8,0},{9,1},... | collective-permute-start | bytes 786440 | tf_op jit(solution)/shard_map/ppermute | solution.py:355
  60.2 10.3 %collective-permute-start.9 = (bf16[128,1024]{1,0:T(8,128)(2,1)S(1)}, bf16[128,1024]{1,0:T(8,128)(2,1)S(1)}, u32[]{:S(2)}, u32[]{:S(2)}) collective-permute-start(bf16[128,1024]{1,0:T(8,128)(2,1)S(1)} %bitcast.36), channel_id=1, source_target_pairs={{0,12},{1,13},{2,14},{3,15},{4,0},{5,1},{6,2},{7,3},{8,4},{9,5},{1... | collective-permute-start | bytes 786440 | tf_op jit(solution)/shard_map/ppermute | solution.py:355
  69.9 3.8 %copy-start.2 = (bf16[128,1024]{1,0:T(8,128)(2,1)}, bf16[128,1024]{1,0:T(8,128)(2,1)S(1)}, u32[]{:S(2)}) copy-start(bf16[128,1024]{1,0:T(8,128)(2,1)S(1)} %collective-permute-done.10.rest_2_) | copy-start | bytes 786436
  69.9 3.8 %copy-start.4 = (bf16[128,1024]{1,0:T(8,128)(2,1)}, bf16[128,1024]{1,0:T(8,128)(2,1)S(1)}, u32[]{:S(2)}) copy-start(bf16[128,1024]{1,0:T(8,128)(2,1)S(1)} %collective-permute-done.11.rest_3_) | copy-start | bytes 786436
  70.5 3.1 %copy-start.6 = (bf16[128,1024]{1,0:T(8,128)(2,1)}, bf16[128,1024]{1,0:T(8,128)(2,1)S(1)}, u32[]{:S(2)}) copy-start(bf16[128,1024]{1,0:T(8,128)(2,1)S(1)} %collective-permute-done.9.rest_1_) | copy-start | bytes 786436
  73.7 2.7 %collective-permute-start.17 = (bf16[2,8,32,1024]{3,2,1,0:T(8,128)(2,1)S(1)}, bf16[2,8,32,1024]{3,2,1,0:T(8,128)(2,1)S(1)}, u32[]{:S(2)}, u32[]{:S(2)}) collective-permute-start(bf16[2,8,32,1024]{3,2,1,0:T(8,128)(2,1)S(1)} %get-tuple-element.43), channel_id=1, source_target_pairs={{0,1},{1,0},{2,3},{3,2},{4,5},{5,4},{6,7},{7,6},{8,9},{9,8},{10,11... | collective-permute-start | bytes 3145736 | tf_op jit(solution)/shard_map/ppermute | solution.py:345
  76.4 1.0 copy-start.8
  78.3 16.6 %collective-permute-start.18 = (bf16[8,32,1024]{2,1,0:T(8,128)(2,1)}, bf16[8,32,1024]{2,1,0:T(8,128)(2,1)}, u32[]{:S(2)}, u32[]{:S(2)}) collective-permute-start(bf16[8,32,1024]{2,1,0:T(8,128)(2,1)} %fusion.1), channel_id=1, source_target_pairs={{0,2},{1,3},{2,0},{3,1},{4,6},{5,7},{6,4},{7,5},{8,10},{9,11},{10,... | collective-permute-start | bytes 1572872 | tf_op jit(solution)/shard_map/ppermute | solution.py:348
  79.4 1.6 %copy-start = (bf16[1024,1024]{1,0:T(8,128)(2,1)S(1)}, bf16[1024,1024]{1,0:T(8,128)(2,1)}, u32[]{:S(2)}) copy-start(bf16[1024,1024]{1,0:T(8,128)(2,1)} %all-gather.2.cloned.1.call-done.w_ref) | copy-start | bytes 6291460
  80.9 0.9 copy-start.3
  81.9 0.9 copy-start.5
  82.8 0.9 copy-start.7
  83.8 11.1 %copy-start.9 = (bf16[2,8,32,1024]{3,2,1,0:T(8,128)(2,1)S(1)}, bf16[2,8,32,1024]{3,2,1,0:T(8,128)(2,1)}, u32[]{:S(2)}) copy-start(bf16[2,8,32,1024]{3,2,1,0:T(8,128)(2,1)} %copy-done.8) | copy-start | bytes 3145732
  87.1 18.4 %collective-permute-start.12 = (bf16[4,64,1024]{2,1,0:T(8,128)(2,1)}, bf16[4,64,1024]{2,1,0:T(8,128)(2,1)}, u32[]{:S(2)}, u32[]{:S(2)}) collective-permute-start(bf16[4,64,1024]{2,1,0:T(8,128)(2,1)} %get-tuple-element.38), channel_id=1, source_target_pairs={{0,128},{128,0},{1,129},{129,1},{2,130},{130,2},{3,131},{131,3},{4... | collective-permute-start | bytes 1572872 | tf_op jit(solution)/shard_map/ppermute | solution.py:342
  97.1 24.6 %all-to-all-start = ((bf16[8,32,1024]{2,1,0:T(8,128)(2,1)}), bf16[8,32,1024]{2,1,0:T(8,128)(2,1)S(1)}, u32[]{:S(2)}, u32[]{:S(2)}) async-start(bf16[8,32,1024]{2,1,0:T(8,128)(2,1)} %fusion), calls=%async_computation | async-start | bytes 1048576 | tf_op jit(solution)/shard_map/all_to_all | solution.py:414
  106.8 15.6 %collective-permute-start.13 = (bf16[64,1024]{1,0:T(8,128)(2,1)S(1)}, bf16[64,1024]{1,0:T(8,128)(2,1)S(1)}, u32[]{:S(2)}, u32[]{:S(2)}) collective-permute-start(bf16[64,1024]{1,0:T(8,128)(2,1)S(1)} %get-tuple-element.46), channel_id=1, source_target_pairs={{0,4},{1,5},{2,6},{3,7},{4,8},{5,9},{6,10},{7,11},{8,12},{9,13},{1... | collective-permute-start | bytes 393224 | tf_op jit(solution)/shard_map/ppermute | solution.py:355
  107.2 15.2 %collective-permute-start.14 = (bf16[64,1024]{1,0:T(8,128)(2,1)S(1)}, bf16[64,1024]{1,0:T(8,128)(2,1)S(1)}, u32[]{:S(2)}, u32[]{:S(2)}) collective-permute-start(bf16[64,1024]{1,0:T(8,128)(2,1)S(1)} %get-tuple-element.45), channel_id=1, source_target_pairs={{0,8},{1,9},{2,10},{3,11},{4,12},{5,13},{6,14},{7,15},{8,0},{9,1},... | collective-permute-start | bytes 393224 | tf_op jit(solution)/shard_map/ppermute | solution.py:355
  110.8 11.7 %collective-permute-start.15 = (bf16[64,1024]{1,0:T(8,128)(2,1)S(1)}, bf16[64,1024]{1,0:T(8,128)(2,1)S(1)}, u32[]{:S(2)}, u32[]{:S(2)}) collective-permute-start(bf16[64,1024]{1,0:T(8,128)(2,1)S(1)} %get-tuple-element.44), channel_id=1, source_target_pairs={{0,12},{1,13},{2,14},{3,15},{4,0},{5,1},{6,2},{7,3},{8,4},{9,5},{1... | collective-permute-start | bytes 393224 | tf_op jit(solution)/shard_map/ppermute | solution.py:355
Sparse Core Ops, SparseCore 0:
  29.0 40.9 all-gather.1

commit v3 on v2

--- a/solution.py
+++ b/solution.py
@@ -15,8 +15,8 @@
 SCORE_LOG2 = SCORE_SCALE * LOG2E
 NEGATIVE = -1e30
 FACTORS = (8, 4, 2, 2)
-VMEM_LIMIT = 24 * 1024 * 1024
-VMEM_WIDE = 60 * 1024 * 1024
+VMEM_LIMIT = 16 * 1024 * 1024
+VMEM_WIDE = 56 * 1024 * 1024
 STAT_ROWS = 8
 
 
@@ -91,7 +91,7 @@
         out_ref[j, 4:5, :] = row_total
 
 
-def stats_call(kernel, lengths, key_rows, row_arrays, stat_arrays, passage_len, pairs):
+def stats_call(kernel, vmem, lengths, key_rows, row_arrays, stat_arrays, passage_len, pairs):
     tokens, hd = key_rows.shape
     rows = row_arrays[0].shape[0]
     total_pairs = hd // PAIR
@@ -110,7 +110,7 @@
             + [stat_spec] * len(stat_arrays),
             out_specs=stat_spec,
         ),
-        compiler_params=pltpu.CompilerParams(vmem_limit_bytes=VMEM_WIDE),
+        compiler_params=pltpu.CompilerParams(vmem_limit_bytes=vmem),
         cost_estimate=cost(3),
     )(lengths, row_arrays[0], key_rows, *row_arrays[1:], *stat_arrays)
 
@@ -189,7 +189,7 @@
         ),
         input_output_aliases={9: 1, 10: 2} if carried else {},
         compiler_params=pltpu.CompilerParams(vmem_limit_bytes=VMEM_WIDE),
-        cost_estimate=cost(6),
+        cost_estimate=cost(0.2 if carried else 6),
     )(scalars, mine, theirs, *rows4, key_rows, value_rows, *carried)
 
 
@@ -198,14 +198,22 @@
 
 
 def weight_kernel(chunk, part, s_ref, own_ref, peer_ref, *rest):
-    blocks, (kept_ref, given_ref), term_ref = rest[:-3], rest[-3:-1], rest[-1]
-    core, x_at = s_ref[0], s_ref[1]
+    blocks, (kept_ref, given_ref, all_ref, term_ref) = rest[:-4], rest[-4:]
+    core, x_at, y_at = s_ref[0], s_ref[1], s_ref[2]
     tokens = jnp.concatenate(
-        [ref[y] for y in range(len(blocks)) for ref in (own_ref, peer_ref)], axis=0
-    )
-    term_ref[...] = dot(
-        jnp.transpose(tokens), jnp.concatenate([ref[...] for ref in blocks], axis=0), NN
-    )
+        [
+            ref[lax.rem(y_at + y, len(blocks))]
+            for y in range(len(blocks))
+            for ref in (own_ref, peer_ref)
+        ],
+        axis=0,
+    )
+
+    @pl.when(pl.program_id(0) == 0)
+    def _():
+        all_ref[...] = jnp.concatenate([ref[...] for ref in blocks], axis=0)
+
+    term_ref[...] = dot(jnp.transpose(tokens), all_ref[...], NN)
     cores = 2
     per_z = 2 * cores * part
     for z in range(chunk // per_z):
@@ -227,13 +235,15 @@
     return pl.pallas_call(
         functools.partial(weight_kernel, chunk, part),
         out_shape=(
-            jax.ShapeDtypeStruct(shape, jnp.float32), jax.ShapeDtypeStruct(shape, jnp.bfloat16)
+            jax.ShapeDtypeStruct(shape, jnp.float32),
+            jax.ShapeDtypeStruct(shape, jnp.bfloat16),
+            jax.ShapeDtypeStruct((ny * 2 * rows, features), jnp.bfloat16),
         ),
         grid_spec=pltpu.PrefetchScalarGridSpec(
             num_scalar_prefetch=1,
             grid=(nz // z_step,),
             in_specs=[hidden_spec] * 2 + [whole(blocks[0].shape)] * ny,
-            out_specs=(out_spec, out_spec),
+            out_specs=(out_spec, out_spec, whole((ny * 2 * rows, features))),
             scratch_shapes=[pltpu.VMEM((chunk, features), jnp.float32)],
         ),
         compiler_params=pltpu.CompilerParams(vmem_limit_bytes=VMEM_LIMIT),
@@ -241,20 +251,29 @@
     )(scalars, hidden_own, hidden_peer, *blocks)
 
 
-def state_kernel(rows, s_ref, w_ref, *rest):
-    blocks, (kept_ref, given_ref) = rest[:-2], rest[-2:]
-    term = dot(jnp.concatenate([ref[...] for ref in blocks], axis=0), w_ref[...], NT)
-    for y in range(len(blocks)):
+def state_kernel(rows, s_ref, mine_ref, other_ref, all_ref, kept_ref, given_ref):
+    first = s_ref[0] == 0
+    nz, near, _ = mine_ref.shape
+    part = near // 2
+    weight = []
+    for z in range(nz):
+        for x in range(2):
+            mine = mine_ref[z, x * part : (x + 1) * part]
+            other = other_ref[z, x * part : (x + 1) * part]
+            weight += [jnp.where(first, mine, other), jnp.where(first, other, mine)]
+    term = dot(all_ref[...], jnp.concatenate(weight, axis=0), NT)
+    for y in range(kept_ref.shape[0]):
         at = y * 2 * rows
         kept_ref[y] = term[at : at + rows]
         given_ref[y] = term[at + rows : at + 2 * rows].astype(jnp.bfloat16)
 
 
-def state_call(scalars, w_tile, blocks, chunk):
-    ny, tile, features = len(blocks), w_tile.shape[0], w_tile.shape[1]
-    rows = blocks[0].shape[0] // 2
+def state_call(scalars, w_mine, w_sibling, tokens, rows, z_step):
+    ny, (nz, near, features) = tokens.shape[0] // (2 * rows), w_mine.shape
+    chunk = z_step * near * 2
+    w_spec = pl.BlockSpec((z_step, near, features), lambda i, s: (i, 0, 0))
     out_spec = pl.BlockSpec((ny, rows, chunk), lambda i, s: (0, 0, i))
-    shape = (ny, rows, tile)
+    shape = (ny, rows, nz * near * 2)
     return pl.pallas_call(
         functools.partial(state_kernel, rows),
         out_shape=(
@@ -262,59 +281,49 @@
         ),
         grid_spec=pltpu.PrefetchScalarGridSpec(
             num_scalar_prefetch=1,
-            grid=(tile // chunk,),
-            in_specs=[pl.BlockSpec((chunk, features), lambda i, s: (i, 0))]
-            + [whole(blocks[0].shape)] * ny,
+            grid=(nz // z_step,),
+            in_specs=[w_spec] * 2 + [whole(tokens.shape)],
             out_specs=(out_spec, out_spec),
         ),
         compiler_params=pltpu.CompilerParams(vmem_limit_bytes=VMEM_LIMIT),
         cost_estimate=cost(2),
-    )(scalars, w_tile, *blocks)
-
-
-def split_kernel(nz, s_ref, in_ref, *out_refs):
-    ny = len(out_refs)
-    width = in_ref.shape[1] // (nz * ny)
-    for offset, out_ref in enumerate(out_refs):
-        owner = lax.rem(s_ref[2] + (ny - offset), ny)
-        for z in range(nz):
-            at = pl.multiple_of((z * ny + owner) * width, width)
-            out_ref[:, z * width : (z + 1) * width] = in_ref[:, pl.ds(at, width)]
-
-
-def split_call(scalars, array, nz, ny):
+    )(scalars, w_mine, w_sibling, tokens)
+
+
+def split_kernel(in_ref, out_ref):
+    ny, _, tile = out_ref.shape
+    width = PAIR
+    for y in range(ny):
+        for z in range(tile // width):
+            at = (z * ny + y) * width
+            out_ref[y, :, z * width : (z + 1) * width] = in_ref[:, at : at + width]
+
+
+def split_call(array, ny):
     rows, width = array.shape
-    shape = (rows, width // ny)
-    return pl.pallas_call(
-        functools.partial(split_kernel, nz),
-        out_shape=[jax.ShapeDtypeStruct(shape, array.dtype)] * ny,
-        grid_spec=pltpu.PrefetchScalarGridSpec(
-            num_scalar_prefetch=1,
-            grid=(1,),
-            in_specs=[whole(array.shape)],
-            out_specs=[whole(shape)] * ny,
-        ),
+    return pl.pallas_call(
+        split_kernel,
+        out_shape=jax.ShapeDtypeStruct((ny, rows, width // ny), array.dtype),
         compiler_params=pltpu.CompilerParams(vmem_limit_bytes=VMEM_LIMIT),
         cost_estimate=cost(1),
-    )(scalars, array)
-
-
-def place_kernel(nz, s_ref, *rest):
+    )(array)
+
+
+def place_kernel(z_order, s_ref, *rest):
     blocks, out_ref = rest[:-1], rest[-1]
-    ny = len(blocks)
-    width = blocks[0].shape[1] // nz
+    ny, width = len(blocks), PAIR
     for offset, block in enumerate(blocks):
         owner = lax.rem(s_ref[2] + (ny - offset), ny)
-        for z in range(nz):
-            at = pl.multiple_of((z * ny + owner) * width, width)
+        for z, flip in enumerate(z_order):
+            at = pl.multiple_of(((s_ref[3] ^ flip) * ny + owner) * width, width)
             out_ref[:, pl.ds(at, width)] = block[:, z * width : (z + 1) * width]
 
 
-def place_call(scalars, blocks, nz):
+def place_call(scalars, blocks, z_order):
     rows, tile = blocks[0].shape
     shape = (rows, tile * len(blocks))
     return pl.pallas_call(
-        functools.partial(place_kernel, nz),
+        functools.partial(place_kernel, z_order),
         out_shape=jax.ShapeDtypeStruct(shape, blocks[0].dtype),
         grid_spec=pltpu.PrefetchScalarGridSpec(
             num_scalar_prefetch=1,
@@ -335,7 +344,11 @@
     core, x_at = lax.rem(pb, nc), lax.rem(pb // nc, nx)
     y_at = lax.rem(pb // (nx * nc), ny)
     offsets = list(dict.fromkeys((1, ny - 1, *range(2, ny - 1))))
-    place = jnp.stack([core, x_at, y_at]).astype(jnp.int32)
+    z_at = pb // plane
+    place = jnp.stack([core, x_at, y_at, z_at]).astype(jnp.int32)
+    y_groups = [
+        [z * plane + y * nx * nc + r for y in range(ny)] for z in range(nz) for r in range(nx * nc)
+    ]
     z_groups = [[z * plane + r for z in range(nz)] for r in range(plane)]
 
     def other_blk(x):
@@ -353,6 +366,22 @@
             y = i // step % ny
             return i + ((y - offset) % ny - y) * step
         return lax.ppermute(x, "pb", [(i, target(i)) for i in range(devices)])
+
+    def other_z(x, flip):
+        return lax.ppermute(x, "pb", [(i, i ^ (flip * plane)) for i in range(devices)])
+
+    def swap_y(x):
+        return lax.all_to_all(
+            x, "pb", split_axis=0, concat_axis=0, tiled=True, axis_index_groups=y_groups
+        )
+
+    def swap_z(x):
+        return lax.all_to_all(
+            x, "pb", split_axis=0, concat_axis=0, tiled=True, axis_index_groups=z_groups
+        )
+
+    def after(x, *others):
+        return lax.optimization_barrier((x, *others))[0]
 
     tokens = keys.shape[1] * keys.shape[2]
     passages, passage_len = keys.shape[1], keys.shape[2]
@@ -365,29 +394,35 @@
     q_peer = other_blk(q_own)
     g_peer = other_blk(g_own)
 
-    def in_order(first, mine, other):
-        return jnp.where(
-            first, jnp.concatenate([mine, other], axis=0), jnp.concatenate([other, mine], axis=0)
-        )
-
-    w_pair = in_order(core == 0, w_query, other_core(w_query))
-    w_near = in_order(x_at == 0, w_pair, other_x(w_pair))
-    w_tile = lax.all_gather(w_near, "pb", axis=0, tiled=True, axis_index_groups=z_groups)
-
     lens = lengths[0]
     stat_pairs = min(4, hd // PAIR)
     stats_own = stats_call(
-        own_stats_kernel, lens, key_rows, [q_own, g_own, o_own], [], passage_len, stat_pairs
+        own_stats_kernel, VMEM_WIDE, lens, key_rows, [q_own, g_own, o_own], [], passage_len, stat_pairs
+    )
+    w_there = other_x(w_query)
+    w_near = jnp.where(
+        x_at == 0,
+        jnp.concatenate([w_query, w_there], axis=0),
+        jnp.concatenate([w_there, w_query], axis=0),
     )
     mine = stats_call(
-        peer_stats_kernel, lens, key_rows, [q_peer], [stats_own], passage_len, stat_pairs
+        peer_stats_kernel, VMEM_LIMIT, lens, key_rows, [q_peer], [stats_own], passage_len, stat_pairs
     )
     theirs = other_blk(mine)
 
-    place, _ = lax.optimization_barrier((place, stats_own))
-    shares = split_call(place, hidden[0], nz, ny)
-    hidden_own = jnp.stack([shares[0]] + [from_y(shares[s], s) for s in offsets], axis=0)
-    theirs, hidden_own = lax.optimization_barrier((theirs, hidden_own))
+    shares = split_call(hidden[0], ny)
+    hidden_own = swap_y(after(shares, mine))
+
+    w_mine, flip, z_order = after(w_near, mine)[None], nz // 2, [0]
+
+    def along_z(w_rows, flip, order):
+        if flip == 0:
+            return w_rows, order
+        return jnp.concatenate([w_rows, other_z(w_rows, flip)], axis=0), order + [
+            z ^ flip for z in order
+        ]
+
+    w_mine, z_order = along_z(w_mine, flip, z_order)
 
     rows4 = [q_own, q_peer, g_own, g_peer]
     grad_pairs = min(2, hd // PAIR // 2)
@@ -398,31 +433,38 @@
                          passage_len, passages, grad_pairs)
 
     dq_send, key_part, value_part = half_grad(1 - blk, (), jnp.bfloat16)
+    lens = after(lens, w_mine)
     dq_here, key_grad, value_grad = half_grad(blk, (key_part, value_part), jnp.float32)
     dq_there = other_blk(dq_send)
     dq_there, dq_here, hidden_own = lax.optimization_barrier((dq_there, dq_here, hidden_own))
-    hidden_peer = other_blk(hidden_own)
     qg = (dq_here + dq_there.astype(jnp.float32)).astype(jnp.bfloat16)
     qg = qg.reshape(2 * rows, hd // 2)
-
-    blocks = [qg] + [from_y(qg, s) for s in offsets]
-
-    w_kept, w_given = weight_call(place, hidden_own, hidden_peer, blocks, nz, part, max(nz // 4, 1))
+    hidden_peer = other_blk(hidden_own)
+
+    arrived = {s: from_y(qg, s) for s in offsets}
+    blocks = [qg] + [arrived[s] for s in range(1, ny)]
+
+    w_mine, z_order = along_z(w_mine, flip // 2, z_order)
+
+    w_kept, w_given, qg_all = weight_call(
+        after(place, w_mine), hidden_own, hidden_peer, blocks, nz, part, max(nz // 4, 1)
+    )
     w_other = other_core(w_given)
     w_send = (w_kept[1] + w_other[1].astype(jnp.float32)).astype(jnp.bfloat16)
-    w_sum = (w_kept[0] + w_other[0].astype(jnp.float32)) + other_x(w_send).astype(jnp.float32)
-    w_parts = lax.all_to_all(
-        w_sum.astype(jnp.bfloat16), "pb", split_axis=0, concat_axis=0, tiled=True,
-        axis_index_groups=z_groups,
-    )
+    w_across = other_x(w_send)
+    w_sum = (w_kept[0] + w_other[0].astype(jnp.float32)) + w_across.astype(jnp.float32)
+
+    w_mine, z_order = along_z(after(w_mine, w_send), flip // 4, z_order)
+    w_sibling = other_core(after(w_mine, w_across))
+    state_kept, state_given = state_call(
+        place, w_mine, w_sibling, qg_all, rows, max(nz // 4, 1)
+    )
+    state_there = other_blk(state_given)
+    w_parts = swap_z(w_sum.astype(jnp.bfloat16))
     w_query_grad = jnp.sum(w_parts.astype(jnp.float32), axis=0)
-
-    state_kept, state_given = state_call(place, w_tile, blocks, w_tile.shape[0] // 4)
-    state_sum = (state_kept + other_blk(state_given).astype(jnp.float32)).astype(jnp.bfloat16)
-    back = [state_sum[0]] + [None] * (ny - 1)
-    for at, offset in enumerate(offsets):
-        back[offset] = from_y(state_sum[at + 1], -offset)
-    hidden_grad = place_call(place, back, nz).reshape(hidden.shape)
+    state_sum = (state_kept + state_there.astype(jnp.float32)).astype(jnp.bfloat16)
+    back = [state_sum[0]] + [from_y(state_sum[s], -s) for s in range(1, ny)]
+    hidden_grad = place_call(place, back, z_order).reshape(hidden.shape)
     return (hidden_grad, key_grad.reshape(keys.shape), value_grad.reshape(values.shape),
             w_query_grad)
 

time: 132 us -> 119 us (0.902)
  between operations: 14.2 us -> 0.82 us
  waiting for transfers between devices: 35.4 us -> 42.7 us
  local copies, waits for them, and re-layouts: 6.94 us -> 2.7 us
  starting transfers between devices: 33.3 us -> 37 us
  other arithmetic: 7.72 us -> 4.62 us
  Pallas kernels: 33.3 us -> 30.7 us
    ppermute x0 -> x3, waiting for transfers between devices: none -> 16 us  [other_z(): lax.ppermute(x, 'pb', [(i, i ^ flip * plane) for i in range(devices)])]
    ppermute x0 -> x3, starting transfers between devices: none -> 10 us  [other_z(): lax.ppermute(x, 'pb', [(i, i ^ flip * plane) for i in range(devices)])]
    ppermute x2, waiting for transfers between devices: 9.86 us -> 2.2 us  [other_x(): return lax.ppermute(x, 'pb', [(i, i ^ nc) for i in range(devices)])]
    ppermute x6, waiting for transfers between devices: 2.59 us -> 9.28 us  [other_blk(): return lax.ppermute(x, 'blk', [(0, 1), (1, 0)])]
    all_to_all x1 -> x2, waiting for transfers between devices: 10.9 us -> 4.44 us  [the longest x1 4.44 us: swap_z(): lax.all_to_all(x, 'pb', split_axis=0, concat_axis=0, tiled=True, axis_ind...]
    unnamed x30 -> x21, local copies, waits for them, and re-layouts: 6.9 us -> 2.63 us
    ppermute x9 -> x6, waiting for transfers between devices: 9.36 us -> 5.43 us  [from_y(): return lax.ppermute(x, 'pb', [(i, target(i)) for i in range(devices)])]
    ppermute x9 -> x6, starting transfers between devices: 13.8 us -> 10.4 us  [from_y(): return lax.ppermute(x, 'pb', [(i, target(i)) for i in range(devices)])]
  transfers between devices with their start and end apart: 21 -> 21, of which waited for: 7 -> 12; matrix products, arithmetic and copies ran while one was open for 6% -> 4% of each run, Pallas kernels for 24% -> 20%
where the time goes in v3:
time: 119 us
  waiting for transfers between devices  42.7 us (36%)
  starting transfers between devices  37 us (31%)
  Pallas kernels  30.7 us (26%)
  other arithmetic  4.62 us (4%)
  local copies, waits for them, and re-layouts  2.7 us (2%)
    ppermute x3, waiting for transfers between devices, other_z(): lax.ppermute(x, 'pb', [(i, i ^ flip * plane) for i in range(devices)])  16 us
    pallas_call x2, Pallas kernels, grad_call(): pl.pallas_call(functools.partial(grad_kernel, pairs, passage_len, passage...  14.5 us
    ppermute x6, starting transfers between devices, from_y(): return lax.ppermute(x, 'pb', [(i, target(i)) for i in range(devices)])  10.4 us
    ppermute x3, starting transfers between devices, other_z(): lax.ppermute(x, 'pb', [(i, i ^ flip * plane) for i in range(devices)])  10 us
    ppermute x6, waiting for transfers between devices, other_blk(): return lax.ppermute(x, 'blk', [(0, 1), (1, 0)])  9.28 us
    pallas_call x2, Pallas kernels, stats_call(): pl.pallas_call(functools.partial(kernel, pairs, passage_len, lengths.shap...  8.02 us
    ppermute x6, starting transfers between devices, other_blk(): return lax.ppermute(x, 'blk', [(0, 1), (1, 0)])  6 us
    ppermute x6, waiting for transfers between devices, from_y(): return lax.ppermute(x, 'pb', [(i, target(i)) for i in range(devices)])  5.43 us
  transfers between devices with their start and end apart: 21, of which 12 were waited for; matrix products, arithmetic and copies ran while one was open for 4% of the time, Pallas kernels for 20%

profile of v3, /device:TPU:2, one launch (start us, length us, event | category | flops | bytes accessed | tf_op | source)
XLA Modules:
  0.0 118.6 jit_solution(9792087885776164631)
XLA Ops:
  0.6 2.2 %collective-permute-start = (bf16[32,1024]{1,0:T(8,128)(2,1)}, bf16[32,1024]{1,0:T(8,128)(2,1)S(1)}, u32[]{:S(2)}, u32[]{:S(2)}) collective-permute-start(bf16[32,1024]{1,0:T(8,128)(2,1)} %param.15), channel_id=1, source_target_pairs={{0,2},{1,3},{2,0},{3,1},{4,6},{5,7},{6,4},{7,5},{8,10},{9,11},{10,... | collective-permute-start | bytes 196616 | tf_op jit(solution)/shard_map/ppermute | solution.py:361
  2.9 1.4 %collective-permute-start.1 = (bf16[64,2048]{1,0:T(8,128)(2,1)}, bf16[64,2048]{1,0:T(8,128)(2,1)S(1)}, u32[]{:S(2)}, u32[]{:S(2)}) collective-permute-start(bf16[64,2048]{1,0:T(8,128)(2,1)} %bitcast.52), channel_id=1, source_target_pairs={{0,128},{128,0},{1,129},{129,1},{2,130},{130,2},{3,131},{131,3},{4... | collective-permute-start | bytes 786440 | tf_op jit(solution)/shard_map/ppermute | solution.py:355
  4.3 0.6 collective-permute-start.5
  4.9 1.0 copy-done.3
  5.9 0.9 shard_map.115
  6.8 0.6 pad_add_fusion.1.s_ref
  7.5 5.2 %shard_map.111.own_ref = f32[16,8,128]{2,1,0:T(8,128)} custom-call(s32[2]{0:T(128)} %bitcast.41, bf16[64,2048]{1,0:T(8,128)(2,1)} %bitcast.53, bf16[512,2048]{1,0:T(8,128)(2,1)} %bitcast.32, bf16[64,2048]{1,0:T(8,128)(2,1)} %bitcast.57, bf16[64,2048]{1,0:T(8,128)(2,1)} %bitcast.60), custom_call_target="tpu_custom_call" | custom-call | flops 3300000000 | bytes 1000 | tf_op jit(solution)/shard_map/pallas_call | solution.py:102
  12.7 0.4 collective-permute-done.1.q_ref.qp_ref
  13.1 0.8 copy-done.6
  13.9 2.8 %shard_map.112.mine_ref = f32[16,8,128]{2,1,0:T(8,128)S(1)} custom-call(s32[2]{0:T(128)S(1)} %bitcast.43, bf16[64,2048]{1,0:T(8,128)(2,1)S(1)} %collective-permute-done.1.q_ref.qp_ref, bf16[512,2048]{1,0:T(8,128)(2,1)S(1)} %bitcast.35, f32[16,8,128]{2,1,0:T(8,128)S(1)} %copy-done.6), custom_call_target="tpu_custom_call" | custom-call | flops 3300000000 | bytes 1000 | tf_op jit(solution)/shard_map/pallas_call | solution.py:102
  16.8 1.1 collective-permute-start.4
  17.9 7.3 %collective-permute-start.2 = (bf16[1,64,1024]{2,1,0:T(8,128)(2,1)S(1)}, bf16[1,64,1024]{2,1,0:T(8,128)(2,1)S(1)}, u32[]{:S(2)}, u32[]{:S(2)}) collective-permute-start(bf16[1,64,1024]{2,1,0:T(8,128)(2,1)S(1)} %bitcast.49), channel_id=1, source_target_pairs={{0,64},{1,65},{2,66},{3,67},{4,68},{5,69},{6,70},{7,71},{8,72},{9,... | collective-permute-start | bytes 393224 | tf_op jit(solution)/shard_map/ppermute | solution.py:371
  25.2 4.5 %all-to-all-start = ((bf16[4,64,1024]{2,1,0:T(8,128)(2,1)}), bf16[4,64,1024]{2,1,0:T(8,128)(2,1)S(1)}, u32[]{:S(2)}, u32[]{:S(2)}) async-start(bf16[4,64,1024]{2,1,0:T(8,128)(2,1)} %shard_map.115), calls=%async_computation | async-start | bytes 1048576 | tf_op jit(solution)/shard_map/all_to_all | solution.py:374
  29.7 0.7 copy-done.7
  30.4 7.2 %shard_map.113 = (bf16[2,64,1024]{2,1,0:T(8,128)(2,1)}, bf16[512,2048]{1,0:T(8,128)(2,1)}, bf16[512,2048]{1,0:T(8,128)(2,1)}) custom-call(s32[3]{0:T(128)} %pad_add_fusion.1.s_ref, f32[16,8,128]{2,1,0:T(8,128)} %copy-done.2, f32[16,8,128]{2,1,0:T(8,128)} %copy-done.8, bf16[64,2048]{1,0:T(8,128)(2,1)} %bitcast.54, bf16[64,2048]{1,0:T(8,128)(2,1)} %copy-done.1, ...), custom_call_target="tpu_custom_call" | custom-call | flops 6600000000 | bytes 1000 | tf_op jit(solution)/shard_map/pallas_call | solution.py:178
  37.6 1.1 collective-permute-start.6
  38.7 0.6 pad_add_fusion.2.s_ref
  39.3 7.3 %shard_map.114 = (f32[2,64,1024]{2,1,0:T(8,128)}, bf16[512,2048]{1,0:T(8,128)(2,1)}, bf16[512,2048]{1,0:T(8,128)(2,1)}) custom-call(s32[3]{0:T(128)} %pad_add_fusion.2.s_ref, f32[16,8,128]{2,1,0:T(8,128)} %copy-done.2, f32[16,8,128]{2,1,0:T(8,128)} %copy-done.8, bf16[64,2048]{1,0:T(8,128)(2,1)} %bitcast.55, ...), custom_call_target="tpu_custom_call", output_to_operand_aliasing={{1}: (9, {}), {2}: (10, {})} | custom-call | flops 220000000 | bytes 1000 | tf_op jit(solution)/shard_map/pallas_call | solution.py:178
  46.6 1.1 collective-permute-start.7
  47.8 1.5 %collective-permute-start.3 = (bf16[2,64,1024]{2,1,0:T(8,128)(2,1)S(1)}, bf16[2,64,1024]{2,1,0:T(8,128)(2,1)S(1)}, u32[]{:S(2)}, u32[]{:S(2)}) collective-permute-start(bf16[2,64,1024]{2,1,0:T(8,128)(2,1)S(1)} %pad_maximum_fusion.1), channel_id=1, source_target_pairs={{0,32},{1,33},{2,34},{3,35},{4,36},{5,37},{6,38},{7,39},{8,40},{9,... | collective-permute-start | bytes 786440 | tf_op jit(solution)/shard_map/ppermute | solution.py:371
  49.2 1.1 add_convert_fusion.2
  50.3 2.1 %collective-permute-start.10 = (bf16[128,1024]{1,0:T(8,128)(2,1)S(1)}, bf16[128,1024]{1,0:T(8,128)(2,1)S(1)}, u32[]{:S(2)}, u32[]{:S(2)}) collective-permute-start(bf16[128,1024]{1,0:T(8,128)(2,1)S(1)} %bitcast.36), channel_id=1, source_target_pairs={{0,4},{1,5},{2,6},{3,7},{4,8},{5,9},{6,10},{7,11},{8,12},{9,13},{1... | collective-permute-start | bytes 786440 | tf_op jit(solution)/shard_map/ppermute | solution.py:368
  52.4 2.7 %collective-permute-start.9 = (bf16[128,1024]{1,0:T(8,128)(2,1)S(1)}, bf16[128,1024]{1,0:T(8,128)(2,1)S(1)}, u32[]{:S(2)}, u32[]{:S(2)}) collective-permute-start(bf16[128,1024]{1,0:T(8,128)(2,1)S(1)} %bitcast.37), channel_id=1, source_target_pairs={{0,8},{1,9},{2,10},{3,11},{4,12},{5,13},{6,14},{7,15},{8,0},{9,1},... | collective-permute-start | bytes 786440 | tf_op jit(solution)/shard_map/ppermute | solution.py:368
  55.1 1.5 %collective-permute-start.8 = (bf16[128,1024]{1,0:T(8,128)(2,1)S(1)}, bf16[128,1024]{1,0:T(8,128)(2,1)S(1)}, u32[]{:S(2)}, u32[]{:S(2)}) collective-permute-start(bf16[128,1024]{1,0:T(8,128)(2,1)S(1)} %bitcast.38), channel_id=1, source_target_pairs={{0,12},{1,13},{2,14},{3,15},{4,0},{5,1},{6,2},{7,3},{8,4},{9,5},{1... | collective-permute-start | bytes 786440 | tf_op jit(solution)/shard_map/ppermute | solution.py:368
  56.7 3.4 %collective-permute-done.3 = bf16[2,64,1024]{2,1,0:T(8,128)(2,1)S(1)} collective-permute-done((bf16[2,64,1024]{2,1,0:T(8,128)(2,1)S(1)}, bf16[2,64,1024]{2,1,0:T(8,128)(2,1)S(1)}, u32[]{:S(2)}, u32[]{:S(2)}) %collective-permute-start.3) | collective-permute-done | bytes 262176 | tf_op jit(solution)/shard_map/ppermute | solution.py:371
  60.2 0.7 collective-permute-done.10.rest_3_
  60.8 3.2 %collective-permute-done.9.rest_2_ = bf16[128,1024]{1,0:T(8,128)(2,1)S(1)} collective-permute-done((bf16[128,1024]{1,0:T(8,128)(2,1)S(1)}, bf16[128,1024]{1,0:T(8,128)(2,1)S(1)}, u32[]{:S(2)}, u32[]{:S(2)}) %collective-permute-start.9) | collective-permute-done | bytes 262176 | tf_op jit(solution)/shard_map/ppermute | solution.py:368
  64.0 3.3 %shard_map.116 = (f32[2,8,32,1024]{3,2,1,0:T(8,128)S(1)}, bf16[2,8,32,1024]{3,2,1,0:T(8,128)(2,1)S(1)}, bf16[512,1024]{1,0:T(8,128)(2,1)S(1)}) custom-call(s32[4]{0:T(128)S(1)} %pad_add_fusion.s_ref, bf16[4,64,1024]{2,1,0:T(8,128)(2,1)S(1)} %all-to-all-done.own_ref, bf16[4,64,1024]{2,1,0:T(8,128)(2,1)S(1)} %collective-permute-done.7.peer_ref, ...), custom_call_target="tpu_custom_call" | custom-call | flops 2200000000 | bytes 1000 | tf_op jit(solution)/shard_map/pallas_call | solution.py:235
  67.4 2.6 %collective-permute-done.11 = bf16[2,8,32,1024]{3,2,1,0:T(8,128)(2,1)S(1)} collective-permute-done((bf16[2,8,32,1024]{3,2,1,0:T(8,128)(2,1)S(1)}, bf16[2,8,32,1024]{3,2,1,0:T(8,128)(2,1)S(1)}, u32[]{:S(2)}, u32[]{:S(2)}) %collective-permute-start.11) | collective-permute-done | bytes 1048608 | tf_op jit(solution)/shard_map/ppermute | solution.py:358
  70.2 1.3 %collective-permute-start.12 = (bf16[4,64,1024]{2,1,0:T(8,128)(2,1)S(1)}, bf16[4,64,1024]{2,1,0:T(8,128)(2,1)S(1)}, u32[]{:S(2)}, u32[]{:S(2)}) collective-permute-start(bf16[4,64,1024]{2,1,0:T(8,128)(2,1)S(1)} %pad_maximum_fusion), channel_id=1, source_target_pairs={{0,16},{1,17},{2,18},{3,19},{4,20},{5,21},{6,22},{7,23},{8,24},{9,... | collective-permute-start | bytes 1572872 | tf_op jit(solution)/shard_map/ppermute | solution.py:371
  71.5 0.3 collective-permute-start.13
  71.8 12.6 %collective-permute-done.12 = bf16[4,64,1024]{2,1,0:T(8,128)(2,1)S(1)} collective-permute-done((bf16[4,64,1024]{2,1,0:T(8,128)(2,1)S(1)}, bf16[4,64,1024]{2,1,0:T(8,128)(2,1)S(1)}, u32[]{:S(2)}, u32[]{:S(2)}) %collective-permute-start.12) | collective-permute-done | bytes 524320 | tf_op jit(solution)/shard_map/ppermute | solution.py:371
  84.4 2.2 %collective-permute-done.13 = bf16[8,32,1024]{2,1,0:T(8,128)(2,1)S(1)} collective-permute-done((bf16[8,32,1024]{2,1,0:T(8,128)(2,1)S(1)}, bf16[8,32,1024]{2,1,0:T(8,128)(2,1)S(1)}, u32[]{:S(2)}, u32[]{:S(2)}) %collective-permute-start.13) | collective-permute-done | bytes 524320 | tf_op jit(solution)/shard_map/ppermute | solution.py:361
  86.7 2.7 %collective-permute-done.14.other_ref = bf16[8,64,1024]{2,1,0:T(8,128)(2,1)S(1)} collective-permute-done((bf16[8,64,1024]{2,1,0:T(8,128)(2,1)S(1)}, bf16[8,64,1024]{2,1,0:T(8,128)(2,1)S(1)}, u32[]{:S(2)}, u32[]{:S(2)}) %collective-permute-start.14) | collective-permute-done | bytes 1048608 | tf_op jit(solution)/shard_map/ppermute | solution.py:358
  89.3 2.6 %shard_map.117 = (f32[4,64,1024]{2,1,0:T(8,128)S(1)}, bf16[4,64,1024]{2,1,0:T(8,128)(2,1)S(1)}) custom-call(s32[4]{0:T(128)S(1)} %pad_add_fusion.s_ref, bf16[8,64,1024]{2,1,0:T(8,128)(2,1)S(1)} %constant_dynamic-update-slice_fusion.mine_ref, bf16[8,64,1024]{2,1,0:T(8,128)(2,1)S(1)} %collective-permute-done.14.other_ref, ...), custom_call_target="tpu_custom_call" | custom-call | flops 2200000000 | bytes 1000 | tf_op jit(solution)/shard_map/pallas_call | solution.py:277
  91.9 0.6 collective-permute-start.15
  92.5 1.0 fusion
  93.6 3.5 %all-to-all-start.1 = ((bf16[8,32,1024]{2,1,0:T(8,128)(2,1)}), bf16[8,32,1024]{2,1,0:T(8,128)(2,1)S(1)}, u32[]{:S(2)}, u32[]{:S(2)}) async-start(bf16[8,32,1024]{2,1,0:T(8,128)(2,1)} %fusion), calls=%async_computation.1 | async-start | bytes 1048576 | tf_op jit(solution)/shard_map/all_to_all | solution.py:379
  97.1 8.9 %collective-permute-done.15 = bf16[4,64,1024]{2,1,0:T(8,128)(2,1)S(1)} collective-permute-done((bf16[4,64,1024]{2,1,0:T(8,128)(2,1)S(1)}, bf16[4,64,1024]{2,1,0:T(8,128)(2,1)S(1)}, u32[]{:S(2)}, u32[]{:S(2)}) %collective-permute-start.15) | collective-permute-done | bytes 524320 | tf_op jit(solution)/shard_map/ppermute | solution.py:355
  105.9 0.2 add_convert_fusion
  106.1 2.2 %collective-permute-start.18 = (bf16[64,1024]{1,0:T(8,128)(2,1)S(1)}, bf16[64,1024]{1,0:T(8,128)(2,1)S(1)}, u32[]{:S(2)}, u32[]{:S(2)}) collective-permute-start(bf16[64,1024]{1,0:T(8,128)(2,1)S(1)} %get-tuple-element.44), channel_id=1, source_target_pairs={{0,12},{1,13},{2,14},{3,15},{4,0},{5,1},{6,2},{7,3},{8,4},{9,5},{1... | collective-permute-start | bytes 393224 | tf_op jit(solution)/shard_map/ppermute | solution.py:368
  108.3 1.1 collective-permute-start.17
  109.5 0.8 collective-permute-start.16
  110.3 4.4 %all-to-all-done.1 = bf16[8,32,1024]{2,1,0:T(8,128)(2,1)S(1)} async-done(((bf16[8,32,1024]{2,1,0:T(8,128)(2,1)}), bf16[8,32,1024]{2,1,0:T(8,128)(2,1)S(1)}, u32[]{:S(2)}, u32[]{:S(2)}) %all-to-all-start.1) | async-done | bytes 524320 | tf_op jit(solution)/shard_map/all_to_all | solution.py:379
  114.8 0.7 convert_reduce_fusion
  115.5 0.2 collective-permute-done.17.rest_2_
  115.7 1.3 %collective-permute-done.16.rest_1_ = bf16[64,1024]{1,0:T(8,128)(2,1)S(1)} collective-permute-done((bf16[64,1024]{1,0:T(8,128)(2,1)S(1)}, bf16[64,1024]{1,0:T(8,128)(2,1)S(1)}, u32[]{:S(2)}, u32[]{:S(2)}) %collective-permute-start.16) | collective-permute-done | bytes 131104 | tf_op jit(solution)/shard_map/ppermute | solution.py:368
  117.1 1.5 %shard_map.118 = bf16[64,4096]{1,0:T(8,128)(2,1)} custom-call(s32[4]{0:T(128)S(1)} %pad_add_fusion.s_ref, bf16[64,1024]{1,0:T(8,128)(2,1)S(1)} %get-tuple-element.47.rest_0_, bf16[64,1024]{1,0:T(8,128)(2,1)S(1)} %collective-permute-done.16.rest_1_, bf16[64,1024]{1,0:T(8,128)(2,1)S(1)} %collective-permute-done.17.rest_2_, ...), custom_call_target="tpu_custom_call" | custom-call | flops 1100000000 | bytes 1000 | tf_op jit(solution)/shard_map/pallas_call | solution.py:325
  (36 shorter events, 0.6 us)
Async XLA Ops:
  0.6 6.2 %copy-start.4 = (s32[1,2]{1,0:T(1,128)S(1)}, s32[1,2]{1,0:T(1,128)}, u32[]{:S(2)}) copy-start(s32[1,2]{1,0:T(1,128)} %param.14) | copy-start | bytes 28
  0.6 17.3 %collective-permute-start = (bf16[32,1024]{1,0:T(8,128)(2,1)}, bf16[32,1024]{1,0:T(8,128)(2,1)S(1)}, u32[]{:S(2)}, u32[]{:S(2)}) collective-permute-start(bf16[32,1024]{1,0:T(8,128)(2,1)} %param.15), channel_id=1, source_target_pairs={{0,2},{1,3},{2,0},{3,1},{4,6},{5,7},{6,4},{7,5},{8,10},{9,11},{10,... | collective-permute-start | bytes 196616 | tf_op jit(solution)/shard_map/ppermute | solution.py:361
  2.9 10.2 %collective-permute-start.1 = (bf16[64,2048]{1,0:T(8,128)(2,1)}, bf16[64,2048]{1,0:T(8,128)(2,1)S(1)}, u32[]{:S(2)}, u32[]{:S(2)}) collective-permute-start(bf16[64,2048]{1,0:T(8,128)(2,1)} %bitcast.52), channel_id=1, source_target_pairs={{0,128},{128,0},{1,129},{129,1},{2,130},{130,2},{3,131},{131,3},{4... | collective-permute-start | bytes 786440 | tf_op jit(solution)/shard_map/ppermute | solution.py:355
  4.3 25.4 %collective-permute-start.5 = (bf16[64,2048]{1,0:T(8,128)(2,1)}, bf16[64,2048]{1,0:T(8,128)(2,1)S(1)}, u32[]{:S(2)}, u32[]{:S(2)}) collective-permute-start(bf16[64,2048]{1,0:T(8,128)(2,1)} %bitcast.56), channel_id=1, source_target_pairs={{0,128},{128,0},{1,129},{129,1},{2,130},{130,2},{3,131},{131,3},{4... | collective-permute-start | bytes 786440 | tf_op jit(solution)/shard_map/ppermute | solution.py:355
  4.9 1.0 copy-start.3
  7.5 5.6 %copy-start = (bf16[1,2,256,2048]{3,2,1,0:T(8,128)(2,1)S(1)}, bf16[1,2,256,2048]{3,2,1,0:T(8,128)(2,1)}, u32[]{:S(2)}) copy-start(bf16[1,2,256,2048]{3,2,1,0:T(8,128)(2,1)} %param.12) | copy-start | bytes 6291460
  7.5 5.6 %copy-start.5 = (s32[1,2]{1,0:T(1,128)S(1)}, s32[1,2]{1,0:T(1,128)}, u32[]{:S(2)}) copy-start(s32[1,2]{1,0:T(1,128)} %param.14) | copy-start | bytes 28
  13.1 0.8 copy-start.6
  13.9 2.8 %copy-start.1 = (bf16[64,2048]{1,0:T(8,128)(2,1)}, bf16[64,2048]{1,0:T(8,128)(2,1)S(1)}, u32[]{:S(2)}) copy-start(bf16[64,2048]{1,0:T(8,128)(2,1)S(1)} %collective-permute-done.1.q_ref.qp_ref) | copy-start | bytes 786436
  13.9 4.0 %copy-start.9 = (bf16[32,1024]{1,0:T(8,128)(2,1)S(1)}, bf16[32,1024]{1,0:T(8,128)(2,1)}, u32[]{:S(2)}) copy-start(bf16[32,1024]{1,0:T(8,128)(2,1)} %param.15) | copy-start | bytes 196612
  16.7 13.0 %copy-start.2 = (f32[16,8,128]{2,1,0:T(8,128)}, f32[16,8,128]{2,1,0:T(8,128)S(1)}, u32[]{:S(2)}) copy-start(f32[16,8,128]{2,1,0:T(8,128)S(1)} %shard_map.112.mine_ref) | copy-start | bytes 196612
  16.8 12.9 %collective-permute-start.4 = (f32[16,8,128]{2,1,0:T(8,128)S(1)}, f32[16,8,128]{2,1,0:T(8,128)S(1)}, u32[]{:S(2)}, u32[]{:S(2)}) collective-permute-start(f32[16,8,128]{2,1,0:T(8,128)S(1)} %shard_map.112.mine_ref), channel_id=1, source_target_pairs={{0,128},{128,0},{1,129},{129,1},{2,130},{130,2},{3,131},{131,3},{4... | collective-permute-start | bytes 196616 | tf_op jit(solution)/shard_map/ppermute | solution.py:355
  17.9 20.8 %collective-permute-start.2 = (bf16[1,64,1024]{2,1,0:T(8,128)(2,1)S(1)}, bf16[1,64,1024]{2,1,0:T(8,128)(2,1)S(1)}, u32[]{:S(2)}, u32[]{:S(2)}) collective-permute-start(bf16[1,64,1024]{2,1,0:T(8,128)(2,1)S(1)} %bitcast.49), channel_id=1, source_target_pairs={{0,64},{1,65},{2,66},{3,67},{4,68},{5,69},{6,70},{7,71},{8,72},{9,... | collective-permute-start | bytes 393224 | tf_op jit(solution)/shard_map/ppermute | solution.py:371
  25.2 21.4 %all-to-all-start = ((bf16[4,64,1024]{2,1,0:T(8,128)(2,1)}), bf16[4,64,1024]{2,1,0:T(8,128)(2,1)S(1)}, u32[]{:S(2)}, u32[]{:S(2)}) async-start(bf16[4,64,1024]{2,1,0:T(8,128)(2,1)} %shard_map.115), calls=%async_computation | async-start | bytes 1048576 | tf_op jit(solution)/shard_map/all_to_all | solution.py:374
  29.7 0.7 copy-start.7
  29.7 0.7 copy-start.8
  37.6 9.0 %collective-permute-start.6 = (bf16[2,64,1024]{2,1,0:T(8,128)(2,1)}, bf16[2,64,1024]{2,1,0:T(8,128)(2,1)S(1)}, u32[]{:S(2)}, u32[]{:S(2)}) collective-permute-start(bf16[2,64,1024]{2,1,0:T(8,128)(2,1)} %get-tuple-element.26), channel_id=1, source_target_pairs={{0,128},{128,0},{1,129},{129,1},{2,130},{130,2},{3,131},{131,3},{4... | collective-permute-start | bytes 786440 | tf_op jit(solution)/shard_map/ppermute | solution.py:355
  46.6 17.4 %collective-permute-start.7 = (bf16[4,64,1024]{2,1,0:T(8,128)(2,1)S(1)}, bf16[4,64,1024]{2,1,0:T(8,128)(2,1)S(1)}, u32[]{:S(2)}, u32[]{:S(2)}) collective-permute-start(bf16[4,64,1024]{2,1,0:T(8,128)(2,1)S(1)} %all-to-all-done.own_ref), channel_id=1, source_target_pairs={{0,128},{128,0},{1,129},{129,1},{2,130},{130,2},{3,131},{131,3},{4... | collective-permute-start | bytes 1572872 | tf_op jit(solution)/shard_map/ppermute | solution.py:355
  47.8 12.3 %collective-permute-start.3 = (bf16[2,64,1024]{2,1,0:T(8,128)(2,1)S(1)}, bf16[2,64,1024]{2,1,0:T(8,128)(2,1)S(1)}, u32[]{:S(2)}, u32[]{:S(2)}) collective-permute-start(bf16[2,64,1024]{2,1,0:T(8,128)(2,1)S(1)} %pad_maximum_fusion.1), channel_id=1, source_target_pairs={{0,32},{1,33},{2,34},{3,35},{4,36},{5,37},{6,38},{7,39},{8,40},{9,... | collective-permute-start | bytes 786440 | tf_op jit(solution)/shard_map/ppermute | solution.py:371
  50.3 10.5 %collective-permute-start.10 = (bf16[128,1024]{1,0:T(8,128)(2,1)S(1)}, bf16[128,1024]{1,0:T(8,128)(2,1)S(1)}, u32[]{:S(2)}, u32[]{:S(2)}) collective-permute-start(bf16[128,1024]{1,0:T(8,128)(2,1)S(1)} %bitcast.36), channel_id=1, source_target_pairs={{0,4},{1,5},{2,6},{3,7},{4,8},{5,9},{6,10},{7,11},{8,12},{9,13},{1... | collective-permute-start | bytes 786440 | tf_op jit(solution)/shard_map/ppermute | solution.py:368
  52.4 11.6 %collective-permute-start.9 = (bf16[128,1024]{1,0:T(8,128)(2,1)S(1)}, bf16[128,1024]{1,0:T(8,128)(2,1)S(1)}, u32[]{:S(2)}, u32[]{:S(2)}) collective-permute-start(bf16[128,1024]{1,0:T(8,128)(2,1)S(1)} %bitcast.37), channel_id=1, source_target_pairs={{0,8},{1,9},{2,10},{3,11},{4,12},{5,13},{6,14},{7,15},{8,0},{9,1},... | collective-permute-start | bytes 786440 | tf_op jit(solution)/shard_map/ppermute | solution.py:368
  55.1 8.9 %collective-permute-start.8 = (bf16[128,1024]{1,0:T(8,128)(2,1)S(1)}, bf16[128,1024]{1,0:T(8,128)(2,1)S(1)}, u32[]{:S(2)}, u32[]{:S(2)}) collective-permute-start(bf16[128,1024]{1,0:T(8,128)(2,1)S(1)} %bitcast.38), channel_id=1, source_target_pairs={{0,12},{1,13},{2,14},{3,15},{4,0},{5,1},{6,2},{7,3},{8,4},{9,5},{1... | collective-permute-start | bytes 786440 | tf_op jit(solution)/shard_map/ppermute | solution.py:368
  67.3 2.7 %collective-permute-start.11 = (bf16[2,8,32,1024]{3,2,1,0:T(8,128)(2,1)S(1)}, bf16[2,8,32,1024]{3,2,1,0:T(8,128)(2,1)S(1)}, u32[]{:S(2)}, u32[]{:S(2)}) collective-permute-start(bf16[2,8,32,1024]{3,2,1,0:T(8,128)(2,1)S(1)} %get-tuple-element.36), channel_id=1, source_target_pairs={{0,1},{1,0},{2,3},{3,2},{4,5},{5,4},{6,7},{7,6},{8,9},{9,8},{10,11... | collective-permute-start | bytes 3145736 | tf_op jit(solution)/shard_map/ppermute | solution.py:358
  70.2 14.2 %collective-permute-start.12 = (bf16[4,64,1024]{2,1,0:T(8,128)(2,1)S(1)}, bf16[4,64,1024]{2,1,0:T(8,128)(2,1)S(1)}, u32[]{:S(2)}, u32[]{:S(2)}) collective-permute-start(bf16[4,64,1024]{2,1,0:T(8,128)(2,1)S(1)} %pad_maximum_fusion), channel_id=1, source_target_pairs={{0,16},{1,17},{2,18},{3,19},{4,20},{5,21},{6,22},{7,23},{8,24},{9,... | collective-permute-start | bytes 1572872 | tf_op jit(solution)/shard_map/ppermute | solution.py:371
  71.5 15.2 %collective-permute-start.13 = (bf16[8,32,1024]{2,1,0:T(8,128)(2,1)S(1)}, bf16[8,32,1024]{2,1,0:T(8,128)(2,1)S(1)}, u32[]{:S(2)}, u32[]{:S(2)}) collective-permute-start(bf16[8,32,1024]{2,1,0:T(8,128)(2,1)S(1)} %fusion.1), channel_id=1, source_target_pairs={{0,2},{1,3},{2,0},{3,1},{4,6},{5,7},{6,4},{7,5},{8,10},{9,11},{10,... | collective-permute-start | bytes 1572872 | tf_op jit(solution)/shard_map/ppermute | solution.py:361
  86.7 2.7 %collective-permute-start.14 = (bf16[8,64,1024]{2,1,0:T(8,128)(2,1)S(1)}, bf16[8,64,1024]{2,1,0:T(8,128)(2,1)S(1)}, u32[]{:S(2)}, u32[]{:S(2)}) collective-permute-start(bf16[8,64,1024]{2,1,0:T(8,128)(2,1)S(1)} %constant_dynamic-update-slice_fusion.mine_ref), channel_id=1, source_target_pairs={{0,1},{1,0},{2,3},{3,2},{4,5},{5,4},{6,7},{7,6},{8,9},{9,8},{10,11... | collective-permute-start | bytes 3145736 | tf_op jit(solution)/shard_map/ppermute | solution.py:358
  91.9 14.1 %collective-permute-start.15 = (bf16[4,64,1024]{2,1,0:T(8,128)(2,1)S(1)}, bf16[4,64,1024]{2,1,0:T(8,128)(2,1)S(1)}, u32[]{:S(2)}, u32[]{:S(2)}) collective-permute-start(bf16[4,64,1024]{2,1,0:T(8,128)(2,1)S(1)} %get-tuple-element.41), channel_id=1, source_target_pairs={{0,128},{128,0},{1,129},{129,1},{2,130},{130,2},{3,131},{131,3},{4... | collective-permute-start | bytes 1572872 | tf_op jit(solution)/shard_map/ppermute | solution.py:355
  93.6 21.2 %all-to-all-start.1 = ((bf16[8,32,1024]{2,1,0:T(8,128)(2,1)}), bf16[8,32,1024]{2,1,0:T(8,128)(2,1)S(1)}, u32[]{:S(2)}, u32[]{:S(2)}) async-start(bf16[8,32,1024]{2,1,0:T(8,128)(2,1)} %fusion), calls=%async_computation.1 | async-start | bytes 1048576 | tf_op jit(solution)/shard_map/all_to_all | solution.py:379
  106.1 9.4 %collective-permute-start.18 = (bf16[64,1024]{1,0:T(8,128)(2,1)S(1)}, bf16[64,1024]{1,0:T(8,128)(2,1)S(1)}, u32[]{:S(2)}, u32[]{:S(2)}) collective-permute-start(bf16[64,1024]{1,0:T(8,128)(2,1)S(1)} %get-tuple-element.44), channel_id=1, source_target_pairs={{0,12},{1,13},{2,14},{3,15},{4,0},{5,1},{6,2},{7,3},{8,4},{9,5},{1... | collective-permute-start | bytes 393224 | tf_op jit(solution)/shard_map/ppermute | solution.py:368
  108.3 7.4 %collective-permute-start.17 = (bf16[64,1024]{1,0:T(8,128)(2,1)S(1)}, bf16[64,1024]{1,0:T(8,128)(2,1)S(1)}, u32[]{:S(2)}, u32[]{:S(2)}) collective-permute-start(bf16[64,1024]{1,0:T(8,128)(2,1)S(1)} %get-tuple-element.45), channel_id=1, source_target_pairs={{0,8},{1,9},{2,10},{3,11},{4,12},{5,13},{6,14},{7,15},{8,0},{9,1},... | collective-permute-start | bytes 393224 | tf_op jit(solution)/shard_map/ppermute | solution.py:368
  109.5 7.6 %collective-permute-start.16 = (bf16[64,1024]{1,0:T(8,128)(2,1)S(1)}, bf16[64,1024]{1,0:T(8,128)(2,1)S(1)}, u32[]{:S(2)}, u32[]{:S(2)}) collective-permute-start(bf16[64,1024]{1,0:T(8,128)(2,1)S(1)} %get-tuple-element.46), channel_id=1, source_target_pairs={{0,4},{1,5},{2,6},{3,7},{4,8},{5,9},{6,10},{7,11},{8,12},{9,13},{1... | collective-permute-start | bytes 393224 | tf_op jit(solution)/shard_map/ppermute | solution.py:368

commit v4 on v3

--- a/solution.py
+++ b/solution.py
@@ -436,7 +436,10 @@
     lens = after(lens, w_mine)
     dq_here, key_grad, value_grad = half_grad(blk, (key_part, value_part), jnp.float32)
     dq_there = other_blk(dq_send)
-    dq_there, dq_here, hidden_own = lax.optimization_barrier((dq_there, dq_here, hidden_own))
+    w_mine, z_order = along_z(w_mine, flip // 2, z_order)
+    dq_there, dq_here, hidden_own, w_mine = lax.optimization_barrier(
+        (dq_there, dq_here, hidden_own, w_mine)
+    )
     qg = (dq_here + dq_there.astype(jnp.float32)).astype(jnp.bfloat16)
     qg = qg.reshape(2 * rows, hd // 2)
     hidden_peer = other_blk(hidden_own)
@@ -444,7 +447,7 @@
     arrived = {s: from_y(qg, s) for s in offsets}
     blocks = [qg] + [arrived[s] for s in range(1, ny)]
 
-    w_mine, z_order = along_z(w_mine, flip // 2, z_order)
+    w_mine, z_order = along_z(after(w_mine, qg), flip // 4, z_order)
 
     w_kept, w_given, qg_all = weight_call(
         after(place, w_mine), hidden_own, hidden_peer, blocks, nz, part, max(nz // 4, 1)
@@ -454,8 +457,7 @@
     w_across = other_x(w_send)
     w_sum = (w_kept[0] + w_other[0].astype(jnp.float32)) + w_across.astype(jnp.float32)
 
-    w_mine, z_order = along_z(after(w_mine, w_send), flip // 4, z_order)
-    w_sibling = other_core(after(w_mine, w_across))
+    w_sibling = other_core(after(w_mine, w_send))
     state_kept, state_given = state_call(
         place, w_mine, w_sibling, qg_all, rows, max(nz // 4, 1)
     )

time: 119 us -> 113 us (0.950)
  waiting for transfers between devices: 42.7 us -> 36.4 us
    ppermute x3, waiting for transfers between devices: 16 us -> 2.3 us  [other_z(): lax.ppermute(x, 'pb', [(i, i ^ flip * plane) for i in range(devices)])]
    ppermute x2, waiting for transfers between devices: 2.2 us -> 10.4 us  [other_x(): return lax.ppermute(x, 'pb', [(i, i ^ nc) for i in range(devices)])]
    all_to_all x1, waiting for transfers between devices: 4.44 us -> 7.91 us  [swap_z(): lax.all_to_all(x, 'pb', split_axis=0, concat_axis=0, tiled=True, axis_ind...]
    ppermute x6, waiting for transfers between devices: 9.28 us -> 7.03 us  [other_blk(): return lax.ppermute(x, 'blk', [(0, 1), (1, 0)])]
    ppermute x6, waiting for transfers between devices: 5.43 us -> 4.2 us  [from_y(): return lax.ppermute(x, 'pb', [(i, target(i)) for i in range(devices)])]
    unnamed x21 -> x19, local copies, waits for them, and re-layouts: 2.63 us -> 1.6 us
  transfers between devices with their start and end apart: 21 -> 21, of which waited for: 12 -> 9; matrix products, arithmetic and copies ran while one was open for 4% -> 3% of each run, Pallas kernels for 20% -> 23%
where the time goes in v4:
time: 113 us; the launch traced here: 112 us
  starting transfers between devices  37.5 us (33%)
  waiting for transfers between devices  36.4 us (32%)
  Pallas kernels  30.7 us (27%)
  other arithmetic  4.58 us (4%)
  local copies, waits for them, and re-layouts  1.67 us (1%)
    pallas_call x2, Pallas kernels, grad_call(): pl.pallas_call(functools.partial(grad_kernel, pairs, passage_len, passage...  14.5 us
    ppermute x6, starting transfers between devices, from_y(): return lax.ppermute(x, 'pb', [(i, target(i)) for i in range(devices)])  10.6 us
    ppermute x2, waiting for transfers between devices, other_x(): return lax.ppermute(x, 'pb', [(i, i ^ nc) for i in range(devices)])  10.4 us
    ppermute x3, starting transfers between devices, other_z(): lax.ppermute(x, 'pb', [(i, i ^ flip * plane) for i in range(devices)])  9.94 us
    pallas_call x2, Pallas kernels, stats_call(): pl.pallas_call(functools.partial(kernel, pairs, passage_len, lengths.shap...  8.01 us
    all_to_all x1, waiting for transfers between devices, swap_z(): lax.all_to_all(x, 'pb', split_axis=0, concat_axis=0, tiled=True, axis_ind...  7.91 us
    ppermute x6, waiting for transfers between devices, other_blk(): return lax.ppermute(x, 'blk', [(0, 1), (1, 0)])  7.03 us
    ppermute x6, starting transfers between devices, other_blk(): return lax.ppermute(x, 'blk', [(0, 1), (1, 0)])  5.53 us
  transfers between devices with their start and end apart: 21, of which 9 were waited for; matrix products, arithmetic and copies ran while one was open for 3% of the time, Pallas kernels for 23%

profile of v4, /device:TPU:2, one launch (start us, length us, event | category | flops | bytes accessed | tf_op | source)
XLA Modules:
  0.0 111.7 jit_solution(15637930870990332413)
XLA Ops:
  0.6 2.2 %collective-permute-start.4 = (bf16[32,1024]{1,0:T(8,128)(2,1)}, bf16[32,1024]{1,0:T(8,128)(2,1)S(1)}, u32[]{:S(2)}, u32[]{:S(2)}) collective-permute-start(bf16[32,1024]{1,0:T(8,128)(2,1)} %param.15), channel_id=1, source_target_pairs={{0,2},{1,3},{2,0},{3,1},{4,6},{5,7},{6,4},{7,5},{8,10},{9,11},{10,... | collective-permute-start | bytes 196616 | tf_op jit(solution)/shard_map/ppermute | solution.py:361
  2.8 1.4 %collective-permute-start = (bf16[64,2048]{1,0:T(8,128)(2,1)}, bf16[64,2048]{1,0:T(8,128)(2,1)S(1)}, u32[]{:S(2)}, u32[]{:S(2)}) collective-permute-start(bf16[64,2048]{1,0:T(8,128)(2,1)} %bitcast.52), channel_id=1, source_target_pairs={{0,128},{128,0},{1,129},{129,1},{2,130},{130,2},{3,131},{131,3},{4... | collective-permute-start | bytes 786440 | tf_op jit(solution)/shard_map/ppermute | solution.py:355
  4.3 0.6 collective-permute-start.2
  4.9 5.2 %shard_map.111.own_ref = f32[16,8,128]{2,1,0:T(8,128)} custom-call(s32[2]{0:T(128)} %bitcast.41, bf16[64,2048]{1,0:T(8,128)(2,1)} %bitcast.53, bf16[512,2048]{1,0:T(8,128)(2,1)} %bitcast.32, bf16[64,2048]{1,0:T(8,128)(2,1)} %bitcast.57, bf16[64,2048]{1,0:T(8,128)(2,1)} %bitcast.60), custom_call_target="tpu_custom_call" | custom-call | flops 3300000000 | bytes 1000 | tf_op jit(solution)/shard_map/pallas_call | solution.py:102
  10.2 2.9 %collective-permute-done.q_ref.qp_ref = bf16[64,2048]{1,0:T(8,128)(2,1)S(1)} collective-permute-done((bf16[64,2048]{1,0:T(8,128)(2,1)}, bf16[64,2048]{1,0:T(8,128)(2,1)S(1)}, u32[]{:S(2)}, u32[]{:S(2)}) %collective-permute-start) | collective-permute-done | bytes 262176 | tf_op jit(solution)/shard_map/ppermute | solution.py:355
  13.1 0.8 copy-done.5
  13.9 2.8 %shard_map.112.mine_ref = f32[16,8,128]{2,1,0:T(8,128)S(1)} custom-call(s32[2]{0:T(128)S(1)} %bitcast.42, bf16[64,2048]{1,0:T(8,128)(2,1)S(1)} %collective-permute-done.q_ref.qp_ref, bf16[512,2048]{1,0:T(8,128)(2,1)S(1)} %bitcast.35, f32[16,8,128]{2,1,0:T(8,128)S(1)} %copy-done.5), custom_call_target="tpu_custom_call" | custom-call | flops 3300000000 | bytes 1000 | tf_op jit(solution)/shard_map/pallas_call | solution.py:102
  16.7 7.3 %collective-permute-start.5 = (bf16[1,64,1024]{2,1,0:T(8,128)(2,1)S(1)}, bf16[1,64,1024]{2,1,0:T(8,128)(2,1)S(1)}, u32[]{:S(2)}, u32[]{:S(2)}) collective-permute-start(bf16[1,64,1024]{2,1,0:T(8,128)(2,1)S(1)} %bitcast.49), channel_id=1, source_target_pairs={{0,64},{1,65},{2,66},{3,67},{4,68},{5,69},{6,70},{7,71},{8,72},{9,... | collective-permute-start | bytes 393224 | tf_op jit(solution)/shard_map/ppermute | solution.py:371
  24.0 0.9 shard_map.115
  24.9 0.6 pad_add_fusion.1.s_ref
  25.5 0.7 collective-permute-start.1
  26.1 4.5 %all-to-all-start = ((bf16[4,64,1024]{2,1,0:T(8,128)(2,1)}), bf16[4,64,1024]{2,1,0:T(8,128)(2,1)S(1)}, u32[]{:S(2)}, u32[]{:S(2)}) async-start(bf16[4,64,1024]{2,1,0:T(8,128)(2,1)} %shard_map.115), calls=%async_computation | async-start | bytes 1048576 | tf_op jit(solution)/shard_map/all_to_all | solution.py:374
  30.6 1.6 %collective-permute-start.6 = (bf16[2,64,1024]{2,1,0:T(8,128)(2,1)S(1)}, bf16[2,64,1024]{2,1,0:T(8,128)(2,1)S(1)}, u32[]{:S(2)}, u32[]{:S(2)}) collective-permute-start(bf16[2,64,1024]{2,1,0:T(8,128)(2,1)S(1)} %pad_maximum_fusion.1), channel_id=1, source_target_pairs={{0,32},{1,33},{2,34},{3,35},{4,36},{5,37},{6,38},{7,39},{8,40},{9,... | collective-permute-start | bytes 786440 | tf_op jit(solution)/shard_map/ppermute | solution.py:371
  32.2 0.7 copy-done.6
  32.9 7.2 %shard_map.113 = (bf16[2,64,1024]{2,1,0:T(8,128)(2,1)}, bf16[512,2048]{1,0:T(8,128)(2,1)}, bf16[512,2048]{1,0:T(8,128)(2,1)}) custom-call(s32[3]{0:T(128)} %pad_add_fusion.1.s_ref, f32[16,8,128]{2,1,0:T(8,128)} %copy-done.2, f32[16,8,128]{2,1,0:T(8,128)} %copy-done.7, bf16[64,2048]{1,0:T(8,128)(2,1)} %bitcast.54, bf16[64,2048]{1,0:T(8,128)(2,1)} %copy-done.1, ...), custom_call_target="tpu_custom_call" | custom-call | flops 6600000000 | bytes 1000 | tf_op jit(solution)/shard_map/pallas_call | solution.py:178
  40.1 1.4 %collective-permute-start.3 = (bf16[2,64,1024]{2,1,0:T(8,128)(2,1)}, bf16[2,64,1024]{2,1,0:T(8,128)(2,1)S(1)}, u32[]{:S(2)}, u32[]{:S(2)}) collective-permute-start(bf16[2,64,1024]{2,1,0:T(8,128)(2,1)} %get-tuple-element.25), channel_id=1, source_target_pairs={{0,128},{128,0},{1,129},{129,1},{2,130},{130,2},{3,131},{131,3},{4... | collective-permute-start | bytes 786440 | tf_op jit(solution)/shard_map/ppermute | solution.py:355
  41.6 0.6 pad_add_fusion.2.s_ref
  42.2 7.3 %shard_map.114 = (f32[2,64,1024]{2,1,0:T(8,128)}, bf16[512,2048]{1,0:T(8,128)(2,1)}, bf16[512,2048]{1,0:T(8,128)(2,1)}) custom-call(s32[3]{0:T(128)} %pad_add_fusion.2.s_ref, f32[16,8,128]{2,1,0:T(8,128)} %copy-done.2, f32[16,8,128]{2,1,0:T(8,128)} %copy-done.7, bf16[64,2048]{1,0:T(8,128)(2,1)} %bitcast.55, ...), custom_call_target="tpu_custom_call", output_to_operand_aliasing={{1}: (9, {}), {2}: (10, {})} | custom-call | flops 220000000 | bytes 1000 | tf_op jit(solution)/shard_map/pallas_call | solution.py:178
  49.6 1.1 add_convert_fusion.2
  50.7 1.1 collective-permute-start.7
  51.8 0.7 collective-permute-start.8
  52.5 2.0 %collective-permute-start.11 = (bf16[128,1024]{1,0:T(8,128)(2,1)S(1)}, bf16[128,1024]{1,0:T(8,128)(2,1)S(1)}, u32[]{:S(2)}, u32[]{:S(2)}) collective-permute-start(bf16[128,1024]{1,0:T(8,128)(2,1)S(1)} %bitcast.36), channel_id=1, source_target_pairs={{0,4},{1,5},{2,6},{3,7},{4,8},{5,9},{6,10},{7,11},{8,12},{9,13},{1... | collective-permute-start | bytes 786440 | tf_op jit(solution)/shard_map/ppermute | solution.py:368
  54.5 2.7 %collective-permute-start.10 = (bf16[128,1024]{1,0:T(8,128)(2,1)S(1)}, bf16[128,1024]{1,0:T(8,128)(2,1)S(1)}, u32[]{:S(2)}, u32[]{:S(2)}) collective-permute-start(bf16[128,1024]{1,0:T(8,128)(2,1)S(1)} %bitcast.37), channel_id=1, source_target_pairs={{0,8},{1,9},{2,10},{3,11},{4,12},{5,13},{6,14},{7,15},{8,0},{9,1},... | collective-permute-start | bytes 786440 | tf_op jit(solution)/shard_map/ppermute | solution.py:368
  57.2 1.5 %collective-permute-start.9 = (bf16[128,1024]{1,0:T(8,128)(2,1)S(1)}, bf16[128,1024]{1,0:T(8,128)(2,1)S(1)}, u32[]{:S(2)}, u32[]{:S(2)}) collective-permute-start(bf16[128,1024]{1,0:T(8,128)(2,1)S(1)} %bitcast.38), channel_id=1, source_target_pairs={{0,12},{1,13},{2,14},{3,15},{4,0},{5,1},{6,2},{7,3},{8,4},{9,5},{1... | collective-permute-start | bytes 786440 | tf_op jit(solution)/shard_map/ppermute | solution.py:368
  58.6 0.1 pad_add_fusion.s_ref
  58.8 2.3 %collective-permute-done.7 = bf16[4,64,1024]{2,1,0:T(8,128)(2,1)S(1)} collective-permute-done((bf16[4,64,1024]{2,1,0:T(8,128)(2,1)S(1)}, bf16[4,64,1024]{2,1,0:T(8,128)(2,1)S(1)}, u32[]{:S(2)}, u32[]{:S(2)}) %collective-permute-start.7) | collective-permute-done | bytes 524320 | tf_op jit(solution)/shard_map/ppermute | solution.py:371
  61.1 1.4 %collective-permute-done.11.rest_3_ = bf16[128,1024]{1,0:T(8,128)(2,1)S(1)} collective-permute-done((bf16[128,1024]{1,0:T(8,128)(2,1)S(1)}, bf16[128,1024]{1,0:T(8,128)(2,1)S(1)}, u32[]{:S(2)}, u32[]{:S(2)}) %collective-permute-start.11) | collective-permute-done | bytes 262176 | tf_op jit(solution)/shard_map/ppermute | solution.py:368
  62.5 2.8 %collective-permute-done.10.rest_2_ = bf16[128,1024]{1,0:T(8,128)(2,1)S(1)} collective-permute-done((bf16[128,1024]{1,0:T(8,128)(2,1)S(1)}, bf16[128,1024]{1,0:T(8,128)(2,1)S(1)}, u32[]{:S(2)}, u32[]{:S(2)}) %collective-permute-start.10) | collective-permute-done | bytes 262176 | tf_op jit(solution)/shard_map/ppermute | solution.py:368
  65.3 3.3 %shard_map.116 = (f32[2,8,32,1024]{3,2,1,0:T(8,128)S(1)}, bf16[2,8,32,1024]{3,2,1,0:T(8,128)(2,1)S(1)}, bf16[512,1024]{1,0:T(8,128)(2,1)S(1)}) custom-call(s32[4]{0:T(128)S(1)} %pad_add_fusion.s_ref, bf16[4,64,1024]{2,1,0:T(8,128)(2,1)S(1)} %all-to-all-done.own_ref, bf16[4,64,1024]{2,1,0:T(8,128)(2,1)S(1)} %collective-permute-done.8.peer_ref, ...), custom_call_target="tpu_custom_call" | custom-call | flops 2200000000 | bytes 1000 | tf_op jit(solution)/shard_map/pallas_call | solution.py:235
  68.5 0.3 collective-permute-start.12
  68.8 2.6 %collective-permute-done.12 = bf16[2,8,32,1024]{3,2,1,0:T(8,128)(2,1)S(1)} collective-permute-done((bf16[2,8,32,1024]{3,2,1,0:T(8,128)(2,1)S(1)}, bf16[2,8,32,1024]{3,2,1,0:T(8,128)(2,1)S(1)}, u32[]{:S(2)}, u32[]{:S(2)}) %collective-permute-start.12) | collective-permute-done | bytes 1048608 | tf_op jit(solution)/shard_map/ppermute | solution.py:358
  71.5 0.1 fusion.1
  71.6 0.2 collective-permute-start.13
  71.9 0.6 collective-permute-start.18
  72.5 1.9 %collective-permute-done.13.other_ref = bf16[8,64,1024]{2,1,0:T(8,128)(2,1)S(1)} collective-permute-done((bf16[8,64,1024]{2,1,0:T(8,128)(2,1)S(1)}, bf16[8,64,1024]{2,1,0:T(8,128)(2,1)S(1)}, u32[]{:S(2)}, u32[]{:S(2)}) %collective-permute-start.13) | collective-permute-done | bytes 1048608 | tf_op jit(solution)/shard_map/ppermute | solution.py:358
  74.4 2.6 %shard_map.117 = (f32[4,64,1024]{2,1,0:T(8,128)S(1)}, bf16[4,64,1024]{2,1,0:T(8,128)(2,1)S(1)}) custom-call(s32[4]{0:T(128)S(1)} %pad_add_fusion.s_ref, bf16[8,64,1024]{2,1,0:T(8,128)(2,1)S(1)} %constant_dynamic-update-slice_fusion.mine_ref, bf16[8,64,1024]{2,1,0:T(8,128)(2,1)S(1)} %collective-permute-done.13.other_ref, ...), custom_call_target="tpu_custom_call" | custom-call | flops 2200000000 | bytes 1000 | tf_op jit(solution)/shard_map/pallas_call | solution.py:277
  77.0 0.7 collective-permute-start.14
  77.7 10.4 %collective-permute-done.18 = bf16[8,32,1024]{2,1,0:T(8,128)(2,1)S(1)} collective-permute-done((bf16[8,32,1024]{2,1,0:T(8,128)(2,1)S(1)}, bf16[8,32,1024]{2,1,0:T(8,128)(2,1)S(1)}, u32[]{:S(2)}, u32[]{:S(2)}) %collective-permute-start.18) | collective-permute-done | bytes 524320 | tf_op jit(solution)/shard_map/ppermute | solution.py:361
  88.1 1.0 fusion
  89.2 3.7 %all-to-all-start.1 = ((bf16[8,32,1024]{2,1,0:T(8,128)(2,1)}), bf16[8,32,1024]{2,1,0:T(8,128)(2,1)S(1)}, u32[]{:S(2)}, u32[]{:S(2)}) async-start(bf16[8,32,1024]{2,1,0:T(8,128)(2,1)} %fusion), calls=%async_computation.1 | async-start | bytes 1048576 | tf_op jit(solution)/shard_map/all_to_all | solution.py:379
  92.8 4.1 %collective-permute-done.14 = bf16[4,64,1024]{2,1,0:T(8,128)(2,1)S(1)} collective-permute-done((bf16[4,64,1024]{2,1,0:T(8,128)(2,1)S(1)}, bf16[4,64,1024]{2,1,0:T(8,128)(2,1)S(1)}, u32[]{:S(2)}, u32[]{:S(2)}) %collective-permute-start.14) | collective-permute-done | bytes 524320 | tf_op jit(solution)/shard_map/ppermute | solution.py:355
  96.9 0.2 add_convert_fusion
  97.1 2.1 %collective-permute-start.17 = (bf16[64,1024]{1,0:T(8,128)(2,1)S(1)}, bf16[64,1024]{1,0:T(8,128)(2,1)S(1)}, u32[]{:S(2)}, u32[]{:S(2)}) collective-permute-start(bf16[64,1024]{1,0:T(8,128)(2,1)S(1)} %get-tuple-element.46), channel_id=1, source_target_pairs={{0,12},{1,13},{2,14},{3,15},{4,0},{5,1},{6,2},{7,3},{8,4},{9,5},{1... | collective-permute-start | bytes 393224 | tf_op jit(solution)/shard_map/ppermute | solution.py:368
  99.3 1.4 %collective-permute-start.16 = (bf16[64,1024]{1,0:T(8,128)(2,1)S(1)}, bf16[64,1024]{1,0:T(8,128)(2,1)S(1)}, u32[]{:S(2)}, u32[]{:S(2)}) collective-permute-start(bf16[64,1024]{1,0:T(8,128)(2,1)S(1)} %get-tuple-element.47), channel_id=1, source_target_pairs={{0,8},{1,9},{2,10},{3,11},{4,12},{5,13},{6,14},{7,15},{8,0},{9,1},... | collective-permute-start | bytes 393224 | tf_op jit(solution)/shard_map/ppermute | solution.py:368
  100.7 0.9 collective-permute-start.15
  101.6 7.9 %all-to-all-done.1 = bf16[8,32,1024]{2,1,0:T(8,128)(2,1)S(1)} async-done(((bf16[8,32,1024]{2,1,0:T(8,128)(2,1)}), bf16[8,32,1024]{2,1,0:T(8,128)(2,1)S(1)}, u32[]{:S(2)}, u32[]{:S(2)}) %all-to-all-start.1) | async-done | bytes 524320 | tf_op jit(solution)/shard_map/all_to_all | solution.py:379
  109.5 0.7 convert_reduce_fusion
  110.3 1.5 %shard_map.118 = bf16[64,4096]{1,0:T(8,128)(2,1)} custom-call(s32[4]{0:T(128)S(1)} %pad_add_fusion.s_ref, bf16[64,1024]{1,0:T(8,128)(2,1)S(1)} %get-tuple-element.49.rest_0_, bf16[64,1024]{1,0:T(8,128)(2,1)S(1)} %collective-permute-done.15.rest_1_, bf16[64,1024]{1,0:T(8,128)(2,1)S(1)} %collective-permute-done.16.rest_2_, ...), custom_call_target="tpu_custom_call" | custom-call | flops 1100000000 | bytes 1000 | tf_op jit(solution)/shard_map/pallas_call | solution.py:325
  (34 shorter events, 0.3 us)
Async XLA Ops:
  0.6 9.5 %collective-permute-start.4 = (bf16[32,1024]{1,0:T(8,128)(2,1)}, bf16[32,1024]{1,0:T(8,128)(2,1)S(1)}, u32[]{:S(2)}, u32[]{:S(2)}) collective-permute-start(bf16[32,1024]{1,0:T(8,128)(2,1)} %param.15), channel_id=1, source_target_pairs={{0,2},{1,3},{2,0},{3,1},{4,6},{5,7},{6,4},{7,5},{8,10},{9,11},{10,... | collective-permute-start | bytes 196616 | tf_op jit(solution)/shard_map/ppermute | solution.py:361
  2.8 10.2 %collective-permute-start = (bf16[64,2048]{1,0:T(8,128)(2,1)}, bf16[64,2048]{1,0:T(8,128)(2,1)S(1)}, u32[]{:S(2)}, u32[]{:S(2)}) collective-permute-start(bf16[64,2048]{1,0:T(8,128)(2,1)} %bitcast.52), channel_id=1, source_target_pairs={{0,128},{128,0},{1,129},{129,1},{2,130},{130,2},{3,131},{131,3},{4... | collective-permute-start | bytes 786440 | tf_op jit(solution)/shard_map/ppermute | solution.py:355
  4.3 27.9 %collective-permute-start.2 = (bf16[64,2048]{1,0:T(8,128)(2,1)}, bf16[64,2048]{1,0:T(8,128)(2,1)S(1)}, u32[]{:S(2)}, u32[]{:S(2)}) collective-permute-start(bf16[64,2048]{1,0:T(8,128)(2,1)} %bitcast.56), channel_id=1, source_target_pairs={{0,128},{128,0},{1,129},{129,1},{2,130},{130,2},{3,131},{131,3},{4... | collective-permute-start | bytes 786440 | tf_op jit(solution)/shard_map/ppermute | solution.py:355
  4.9 5.2 %copy-start.8 = (bf16[32,1024]{1,0:T(8,128)(2,1)S(1)}, bf16[32,1024]{1,0:T(8,128)(2,1)}, u32[]{:S(2)}) copy-start(bf16[32,1024]{1,0:T(8,128)(2,1)} %param.15) | copy-start | bytes 196612
  4.9 8.2 %copy-start = (bf16[1,2,256,2048]{3,2,1,0:T(8,128)(2,1)S(1)}, bf16[1,2,256,2048]{3,2,1,0:T(8,128)(2,1)}, u32[]{:S(2)}) copy-start(bf16[1,2,256,2048]{3,2,1,0:T(8,128)(2,1)} %param.12) | copy-start | bytes 6291460
  4.9 8.2 %copy-start.4 = (s32[1,2]{1,0:T(1,128)S(1)}, s32[1,2]{1,0:T(1,128)}, u32[]{:S(2)}) copy-start(s32[1,2]{1,0:T(1,128)} %param.14) | copy-start | bytes 28
  10.1 13.9 %copy-start.3 = (bf16[1,64,4096]{2,1,0:T(8,128)(2,1)S(1)}, bf16[1,64,4096]{2,1,0:T(8,128)(2,1)}, u32[]{:S(2)}) copy-start(bf16[1,64,4096]{2,1,0:T(8,128)(2,1)} %param.8) | copy-start | bytes 1572868
  13.1 0.8 copy-start.5
  13.9 2.8 %copy-start.1 = (bf16[64,2048]{1,0:T(8,128)(2,1)}, bf16[64,2048]{1,0:T(8,128)(2,1)S(1)}, u32[]{:S(2)}) copy-start(bf16[64,2048]{1,0:T(8,128)(2,1)S(1)} %collective-permute-done.q_ref.qp_ref) | copy-start | bytes 786436
  16.7 9.4 %copy-start.2 = (f32[16,8,128]{2,1,0:T(8,128)}, f32[16,8,128]{2,1,0:T(8,128)S(1)}, u32[]{:S(2)}) copy-start(f32[16,8,128]{2,1,0:T(8,128)S(1)} %shard_map.112.mine_ref) | copy-start | bytes 196612
  16.7 13.9 %collective-permute-start.5 = (bf16[1,64,1024]{2,1,0:T(8,128)(2,1)S(1)}, bf16[1,64,1024]{2,1,0:T(8,128)(2,1)S(1)}, u32[]{:S(2)}, u32[]{:S(2)}) collective-permute-start(bf16[1,64,1024]{2,1,0:T(8,128)(2,1)S(1)} %bitcast.49), channel_id=1, source_target_pairs={{0,64},{1,65},{2,66},{3,67},{4,68},{5,69},{6,70},{7,71},{8,72},{9,... | collective-permute-start | bytes 393224 | tf_op jit(solution)/shard_map/ppermute | solution.py:371
  25.5 6.7 %collective-permute-start.1 = (f32[16,8,128]{2,1,0:T(8,128)S(1)}, f32[16,8,128]{2,1,0:T(8,128)S(1)}, u32[]{:S(2)}, u32[]{:S(2)}) collective-permute-start(f32[16,8,128]{2,1,0:T(8,128)S(1)} %shard_map.112.mine_ref), channel_id=1, source_target_pairs={{0,128},{128,0},{1,129},{129,1},{2,130},{130,2},{3,131},{131,3},{4... | collective-permute-start | bytes 196616 | tf_op jit(solution)/shard_map/ppermute | solution.py:355
  26.1 23.5 %all-to-all-start = ((bf16[4,64,1024]{2,1,0:T(8,128)(2,1)}), bf16[4,64,1024]{2,1,0:T(8,128)(2,1)S(1)}, u32[]{:S(2)}, u32[]{:S(2)}) async-start(bf16[4,64,1024]{2,1,0:T(8,128)(2,1)} %shard_map.115), calls=%async_computation | async-start | bytes 1048576 | tf_op jit(solution)/shard_map/all_to_all | solution.py:374
  30.6 18.9 %collective-permute-start.6 = (bf16[2,64,1024]{2,1,0:T(8,128)(2,1)S(1)}, bf16[2,64,1024]{2,1,0:T(8,128)(2,1)S(1)}, u32[]{:S(2)}, u32[]{:S(2)}) collective-permute-start(bf16[2,64,1024]{2,1,0:T(8,128)(2,1)S(1)} %pad_maximum_fusion.1), channel_id=1, source_target_pairs={{0,32},{1,33},{2,34},{3,35},{4,36},{5,37},{6,38},{7,39},{8,40},{9,... | collective-permute-start | bytes 786440 | tf_op jit(solution)/shard_map/ppermute | solution.py:371
  32.2 0.7 copy-start.6
  32.2 0.7 copy-start.7
  40.1 9.4 %collective-permute-start.3 = (bf16[2,64,1024]{2,1,0:T(8,128)(2,1)}, bf16[2,64,1024]{2,1,0:T(8,128)(2,1)S(1)}, u32[]{:S(2)}, u32[]{:S(2)}) collective-permute-start(bf16[2,64,1024]{2,1,0:T(8,128)(2,1)} %get-tuple-element.25), channel_id=1, source_target_pairs={{0,128},{128,0},{1,129},{129,1},{2,130},{130,2},{3,131},{131,3},{4... | collective-permute-start | bytes 786440 | tf_op jit(solution)/shard_map/ppermute | solution.py:355
  50.7 10.3 %collective-permute-start.7 = (bf16[4,64,1024]{2,1,0:T(8,128)(2,1)S(1)}, bf16[4,64,1024]{2,1,0:T(8,128)(2,1)S(1)}, u32[]{:S(2)}, u32[]{:S(2)}) collective-permute-start(bf16[4,64,1024]{2,1,0:T(8,128)(2,1)S(1)} %pad_maximum_fusion), channel_id=1, source_target_pairs={{0,16},{1,17},{2,18},{3,19},{4,20},{5,21},{6,22},{7,23},{8,24},{9,... | collective-permute-start | bytes 1572872 | tf_op jit(solution)/shard_map/ppermute | solution.py:371
  51.8 13.5 %collective-permute-start.8 = (bf16[4,64,1024]{2,1,0:T(8,128)(2,1)S(1)}, bf16[4,64,1024]{2,1,0:T(8,128)(2,1)S(1)}, u32[]{:S(2)}, u32[]{:S(2)}) collective-permute-start(bf16[4,64,1024]{2,1,0:T(8,128)(2,1)S(1)} %all-to-all-done.own_ref), channel_id=1, source_target_pairs={{0,128},{128,0},{1,129},{129,1},{2,130},{130,2},{3,131},{131,3},{4... | collective-permute-start | bytes 1572872 | tf_op jit(solution)/shard_map/ppermute | solution.py:355
  52.5 10.0 %collective-permute-start.11 = (bf16[128,1024]{1,0:T(8,128)(2,1)S(1)}, bf16[128,1024]{1,0:T(8,128)(2,1)S(1)}, u32[]{:S(2)}, u32[]{:S(2)}) collective-permute-start(bf16[128,1024]{1,0:T(8,128)(2,1)S(1)} %bitcast.36), channel_id=1, source_target_pairs={{0,4},{1,5},{2,6},{3,7},{4,8},{5,9},{6,10},{7,11},{8,12},{9,13},{1... | collective-permute-start | bytes 786440 | tf_op jit(solution)/shard_map/ppermute | solution.py:368
  54.5 10.8 %collective-permute-start.10 = (bf16[128,1024]{1,0:T(8,128)(2,1)S(1)}, bf16[128,1024]{1,0:T(8,128)(2,1)S(1)}, u32[]{:S(2)}, u32[]{:S(2)}) collective-permute-start(bf16[128,1024]{1,0:T(8,128)(2,1)S(1)} %bitcast.37), channel_id=1, source_target_pairs={{0,8},{1,9},{2,10},{3,11},{4,12},{5,13},{6,14},{7,15},{8,0},{9,1},... | collective-permute-start | bytes 786440 | tf_op jit(solution)/shard_map/ppermute | solution.py:368
  57.2 8.1 %collective-permute-start.9 = (bf16[128,1024]{1,0:T(8,128)(2,1)S(1)}, bf16[128,1024]{1,0:T(8,128)(2,1)S(1)}, u32[]{:S(2)}, u32[]{:S(2)}) collective-permute-start(bf16[128,1024]{1,0:T(8,128)(2,1)S(1)} %bitcast.38), channel_id=1, source_target_pairs={{0,12},{1,13},{2,14},{3,15},{4,0},{5,1},{6,2},{7,3},{8,4},{9,5},{1... | collective-permute-start | bytes 786440 | tf_op jit(solution)/shard_map/ppermute | solution.py:368
  68.5 2.9 %collective-permute-start.12 = (bf16[2,8,32,1024]{3,2,1,0:T(8,128)(2,1)S(1)}, bf16[2,8,32,1024]{3,2,1,0:T(8,128)(2,1)S(1)}, u32[]{:S(2)}, u32[]{:S(2)}) collective-permute-start(bf16[2,8,32,1024]{3,2,1,0:T(8,128)(2,1)S(1)} %get-tuple-element.39), channel_id=1, source_target_pairs={{0,1},{1,0},{2,3},{3,2},{4,5},{5,4},{6,7},{7,6},{8,9},{9,8},{10,11... | collective-permute-start | bytes 3145736 | tf_op jit(solution)/shard_map/ppermute | solution.py:358
  71.6 2.7 %collective-permute-start.13 = (bf16[8,64,1024]{2,1,0:T(8,128)(2,1)S(1)}, bf16[8,64,1024]{2,1,0:T(8,128)(2,1)S(1)}, u32[]{:S(2)}, u32[]{:S(2)}) collective-permute-start(bf16[8,64,1024]{2,1,0:T(8,128)(2,1)S(1)} %constant_dynamic-update-slice_fusion.mine_ref), channel_id=1, source_target_pairs={{0,1},{1,0},{2,3},{3,2},{4,5},{5,4},{6,7},{7,6},{8,9},{9,8},{10,11... | collective-permute-start | bytes 3145736 | tf_op jit(solution)/shard_map/ppermute | solution.py:358
  71.9 16.3 %collective-permute-start.18 = (bf16[8,32,1024]{2,1,0:T(8,128)(2,1)S(1)}, bf16[8,32,1024]{2,1,0:T(8,128)(2,1)S(1)}, u32[]{:S(2)}, u32[]{:S(2)}) collective-permute-start(bf16[8,32,1024]{2,1,0:T(8,128)(2,1)S(1)} %fusion.1), channel_id=1, source_target_pairs={{0,2},{1,3},{2,0},{3,1},{4,6},{5,7},{6,4},{7,5},{8,10},{9,11},{10,... | collective-permute-start | bytes 1572872 | tf_op jit(solution)/shard_map/ppermute | solution.py:361
  77.0 20.0 %collective-permute-start.14 = (bf16[4,64,1024]{2,1,0:T(8,128)(2,1)S(1)}, bf16[4,64,1024]{2,1,0:T(8,128)(2,1)S(1)}, u32[]{:S(2)}, u32[]{:S(2)}) collective-permute-start(bf16[4,64,1024]{2,1,0:T(8,128)(2,1)S(1)} %get-tuple-element.43), channel_id=1, source_target_pairs={{0,128},{128,0},{1,129},{129,1},{2,130},{130,2},{3,131},{131,3},{4... | collective-permute-start | bytes 1572872 | tf_op jit(solution)/shard_map/ppermute | solution.py:355
  89.2 20.4 %all-to-all-start.1 = ((bf16[8,32,1024]{2,1,0:T(8,128)(2,1)}), bf16[8,32,1024]{2,1,0:T(8,128)(2,1)S(1)}, u32[]{:S(2)}, u32[]{:S(2)}) async-start(bf16[8,32,1024]{2,1,0:T(8,128)(2,1)} %fusion), calls=%async_computation.1 | async-start | bytes 1048576 | tf_op jit(solution)/shard_map/all_to_all | solution.py:379
  97.1 13.1 %collective-permute-start.17 = (bf16[64,1024]{1,0:T(8,128)(2,1)S(1)}, bf16[64,1024]{1,0:T(8,128)(2,1)S(1)}, u32[]{:S(2)}, u32[]{:S(2)}) collective-permute-start(bf16[64,1024]{1,0:T(8,128)(2,1)S(1)} %get-tuple-element.46), channel_id=1, source_target_pairs={{0,12},{1,13},{2,14},{3,15},{4,0},{5,1},{6,2},{7,3},{8,4},{9,5},{1... | collective-permute-start | bytes 393224 | tf_op jit(solution)/shard_map/ppermute | solution.py:368
  99.3 11.0 %collective-permute-start.16 = (bf16[64,1024]{1,0:T(8,128)(2,1)S(1)}, bf16[64,1024]{1,0:T(8,128)(2,1)S(1)}, u32[]{:S(2)}, u32[]{:S(2)}) collective-permute-start(bf16[64,1024]{1,0:T(8,128)(2,1)S(1)} %get-tuple-element.47), channel_id=1, source_target_pairs={{0,8},{1,9},{2,10},{3,11},{4,12},{5,13},{6,14},{7,15},{8,0},{9,1},... | collective-permute-start | bytes 393224 | tf_op jit(solution)/shard_map/ppermute | solution.py:368
  100.7 9.6 %collective-permute-start.15 = (bf16[64,1024]{1,0:T(8,128)(2,1)S(1)}, bf16[64,1024]{1,0:T(8,128)(2,1)S(1)}, u32[]{:S(2)}, u32[]{:S(2)}) collective-permute-start(bf16[64,1024]{1,0:T(8,128)(2,1)S(1)} %get-tuple-element.48), channel_id=1, source_target_pairs={{0,4},{1,5},{2,6},{3,7},{4,8},{5,9},{6,10},{7,11},{8,12},{9,13},{1... | collective-permute-start | bytes 393224 | tf_op jit(solution)/shard_map/ppermute | solution.py:368
